TPU v7x, 512 devices: a whole 4x8x8 slice. The times are simulated.
512 devices in a mesh: adapter: 32 (over x, z), tensor: 16 (over y, core).
Axes of the slice: x: 4, y: 8, z: 8, core: 2. Of those that a mesh axis runs over, the one named last changes fastest.
Arguments:
- tokens: bfloat16 [32768, 8192], P('adapter', 'tensor'), may hold values from -6 to 6
- row_adapter_index: int32 [32768, 1], P('adapter'), may hold values from 0 to 511; in each aligned block of 1024 rows (0 to 1023, 1024 to 2047, ...) at most 4 rows name the same one
- adapter_down_weight: bfloat16 [512, 8192, 64], P('adapter', 'tensor'), may hold values from -0.0625 to 0.0625
- adapter_up_weight: bfloat16 [512, 64, 2048], P('adapter', None, 'tensor'), may hold values from -0.75 to 0.75
- key_value_weight: bfloat16 [8192, 2048], P('tensor'), may hold values from -0.09375 to 0.09375
- accepted_branch_rows: int32 [32, 32, 4], P('adapter'), may hold values from 0 to 1023, as said below
- owner_cache_slots: int32 [32, 32, 4], P(None, 'adapter'), may hold values from 0 to 127, as said below
Outputs:
- key_value: bfloat16 [32768, 2048], P('adapter', 'tensor')
- decode_cache: bfloat16 [4096, 2048], P('adapter', 'tensor')
Inputs may be any that keep to these rules, and one draw needn't show every extreme that they name: `row_adapter_index`: among the rows of one device no adapter is named by more than 4 rows; in the rows of some device some adapter is named by exactly 4. For each s the 128 entries accepted_branch_rows[s] are distinct. For each owner o the entries owner_cache_slots[:, o, :] name every slot of 0 to 127 once.
All inputs are finite; a program needn't handle non-finite values.
Results may differ from a plain program's by a relative error of at most 0.025.
Values may be sent and summed in bfloat16 or wider, within the bound.
No kernel may reach another device: no remote copies, remote signals or barrier semaphores. Data moves between devices by JAX's collectives and lax.ppermute only.
A program may use at most 64 MiB of HBM per device.

v0:
```python
import jax
import jax.numpy as jnp
from jax import lax
from jax.sharding import PartitionSpec as P

ADAPTER_COUNT = 512
CAP = 4


def pack_slots(row_adapter_index):
    labels = row_adapter_index[:, 0]
    position = jnp.arange(labels.shape[0], dtype=jnp.int32)
    matching = (labels[:, None] == labels[None, :]) & (position[:, None] > position[None, :])
    before = jnp.sum(matching.astype(jnp.int32), axis=1)
    return labels * CAP + before


def apply_adapter(tokens, cache_slot_index, adapter_down_weight, adapter_up_weight):
    owners = lax.axis_size("adapter")
    feature_width = tokens.shape[1]
    resident_adapters = adapter_down_weight.shape[0]
    column_span = adapter_up_weight.shape[2]
    outbox = (
        jnp.zeros((ADAPTER_COUNT * CAP, feature_width), jnp.bfloat16)
        .at[cache_slot_index]
        .set(tokens)
    )
    received_rows = lax.all_to_all(
        outbox.reshape(owners, resident_adapters * CAP, feature_width),
        "adapter",
        split_axis=0,
        concat_axis=0,
        tiled=True,
    )
    received_rows = received_rows.reshape(owners, resident_adapters, CAP, feature_width)
    partial_rank = jnp.einsum(
        "omjg,mgb->omjb", received_rows, adapter_down_weight, preferred_element_type=jnp.float32
    )
    summed_rank = lax.psum(partial_rank.astype(jnp.bfloat16), "tensor")
    update = jnp.einsum(
        "sacr,aro->saco", summed_rank, adapter_up_weight, preferred_element_type=jnp.float32
    ).astype(jnp.bfloat16)
    returned = lax.all_to_all(
        update.reshape(owners, resident_adapters * CAP, column_span),
        "adapter",
        split_axis=0,
        concat_axis=0,
        tiled=True,
    )
    return returned.reshape(ADAPTER_COUNT * CAP, column_span)[cache_slot_index]


def project(tokens, key_value_weight):
    partial_sum = jnp.dot(tokens, key_value_weight, preferred_element_type=jnp.float32)
    return lax.psum_scatter(
        partial_sum.astype(jnp.bfloat16), "tensor", scatter_dimension=1, tiled=True
    ).astype(jnp.float32)


def per_device(
    tokens,
    row_adapter_index,
    adapter_down_weight,
    adapter_up_weight,
    key_value_weight,
    accepted_branch_rows,
    owner_cache_slots,
):
    cache_slot_index = pack_slots(row_adapter_index)
    base = project(tokens, key_value_weight)
    update_row_block = apply_adapter(
        tokens, cache_slot_index, adapter_down_weight, adapter_up_weight
    )
    key_value = (base + update_row_block.astype(jnp.float32)).astype(jnp.bfloat16)
    owners = lax.axis_size("adapter")
    column_span = key_value.shape[1]
    chosen = key_value[accepted_branch_rows.reshape(-1)]
    moved = lax.all_to_all(
        chosen.reshape(owners, -1, column_span), "adapter", split_axis=0, concat_axis=0, tiled=True
    )
    targets = owner_cache_slots.reshape(-1)
    decode_cache = (
        jnp.zeros((targets.shape[0], column_span), jnp.bfloat16)
        .at[targets]
        .set(moved.reshape(-1, column_span))
    )
    return (key_value, decode_cache)


def solution(mesh):
    in_specs = (
        P("adapter", "tensor"),
        P("adapter", None),
        P("adapter", "tensor", None),
        P("adapter", None, "tensor"),
        P("tensor", None),
        P("adapter", None, None),
        P(None, "adapter", None),
    )
    out_specs = (P("adapter", "tensor"), P("adapter", "tensor"))
    return jax.shard_map(
        per_device, mesh=mesh, in_specs=in_specs, out_specs=out_specs, check_vma=False
    )
```

profile of v0, /device:TPU:1, one launch (start us, length us, event | category | flops | bytes accessed | tf_op | source)
XLA Modules:
  0.0 291.8 jit_solution(5736376576717085041)
XLA Ops:
  7.2 0.0 copy-start
  7.2 0.0 all-reduce.2.cloned.1.call-start
  7.2 1.4 convert_reduce_fusion
  8.6 0.7 compare_select_fusion
  9.3 7.2 %scatter_custom_fusion = bf16[2048,512]{1,0:T(8,128)(2,1)} fusion(s32[1024]{0:T(1024)S(1)} %bitcast.42, bf16[1024,512]{1,0:T(8,128)(2,1)} %param.7, bf16[]{:T(256)} %constant.6.clone.1), kind=kCustom, calls=%fused_computation.12 | custom fusion | bytes 2097664 | tf_op jit(solution)/shard_map/scatter | solution.py:26
  16.5 60.8 %all_to_all.15 = bf16[32,64,512]{2,1,0:T(8,128)(2,1)S(1)} all-to-all(bf16[32,64,512]{2,1,0:T(8,128)(2,1)} %bitcast.37), channel_id=1, replica_groups=mesh['adapter'=32,'tensor'=16] {'adapter'}, dimensions={0} | all-to-all | bytes 4194304 | tf_op jit(solution)/shard_map/all_to_all | solution.py:28
  77.3 0.0 copy-start.5
  77.3 1.2 copy.23
  78.4 0.1 copy-done.5
  78.5 0.0 copy-start.6
  78.5 1.5 fusion.1
  80.0 0.0 all-reduce.2.cloned.1.call-update
  80.0 0.0 reduce-scatter.4.cloned.1.call-start
  80.1 0.0 copy-done
  80.1 0.0 copy-done.6
  80.1 4.3 %convolution_convert_fusion = bf16[1024,2048]{1,0:T(8,128)(2,1)} fusion(bf16[1024,512]{1,0:T(8,128)(2,1)S(1)} %copy-done.6, bf16[512,2048]{1,0:T(8,128)(2,1)S(1)} %copy-done), kind=kOutput, calls=%fused_computation.7 | convolution fusion | flops 2149580800 | bytes 7340032 | tf_op jit(solution)/shard_map/dot_general | solution.py:54
  84.5 6.4 %copy.29 = bf16[1024,2048]{0,1:T(8,128)(2,1)} copy(bf16[1024,2048]{1,0:T(8,128)(2,1)} %convolution_convert_fusion) | data formatting | bytes 8388608
  90.8 0.0 copy-start.2
  90.8 0.0 reduce-scatter.4.cloned.1.call-update
  90.9 0.0 copy-start.3
  90.9 0.0 copy-start.4
  90.9 105.0 %all-reduce.2.cloned.1.call-done = bf16[32,16,4,64]{3,0,2,1:T(8,128)(2,1)} async-done(((bf16[32,16,4,64]{3,0,2,1:T(8,128)(2,1)}), bf16[32,16,4,64]{3,0,2,1:T(8,128)(2,1)}) %all-reduce.2.cloned.1.call-update) | async-done | bytes 262160 | tf_op jit(solution)/shard_map/psum | solution.py:39
  195.9 0.0 copy-done.2
  195.9 1.3 convolution_convert_fusion.1
  197.2 1.0 copy.24
  198.2 9.9 %all-to-all-start.1 = ((bf16[32,64,128]{2,1,0:T(8,128)(2,1)}), bf16[32,64,128]{2,1,0:T(8,128)(2,1)S(1)}, u32[]{:S(2)}, u32[]{:S(2)}) async-start(bf16[32,64,128]{2,1,0:T(8,128)(2,1)} %copy.24), calls=%async_computation.1 | async-start | bytes 1048576 | tf_op jit(solution)/shard_map/all_to_all | solution.py:43
  208.1 0.0 copy-done.3
  208.2 0.1 copy.26
  208.2 0.1 reshape.91
  208.3 0.0 copy-done.4
  208.4 0.1 copy.25
  208.4 0.1 reshape.90
  208.6 13.6 %all-to-all-done.1 = bf16[32,64,128]{2,1,0:T(8,128)(2,1)S(1)} async-done(((bf16[32,64,128]{2,1,0:T(8,128)(2,1)}), bf16[32,64,128]{2,1,0:T(8,128)(2,1)S(1)}, u32[]{:S(2)}, u32[]{:S(2)}) %all-to-all-start.1) | async-done | bytes 524320 | tf_op jit(solution)/shard_map/all_to_all | solution.py:43
  222.2 3.2 %gather_fusion = bf16[1024,128]{1,0:T(8,128)(2,1)S(1)} fusion(bf16[2048,128]{1,0:T(8,128)(2,1)S(1)} %bitcast.36, s32[1024]{0:T(1024)S(1)} %broadcast_clamp_fusion), kind=kCustom, calls=%fused_computation | custom fusion | bytes 528384 | tf_op jit(solution)/shard_map/gather | solution.py:50
  225.4 37.9 %reduce-scatter.4.cloned.1.call-done = bf16[128,1024]{1,0:T(8,128)(2,1)} async-done(((bf16[2048,1024]{1,0:T(8,128)(2,1)}), bf16[128,1024]{1,0:T(8,128)(2,1)}) %reduce-scatter.4.cloned.1.call-update) | async-done | bytes 262160
  263.3 1.1 copy.30
  264.4 0.1 add_convert_fusion
  264.5 0.0 copy-start.1
  264.5 1.3 gather_fusion.1
  265.8 8.9 %all-to-all-start.2 = ((bf16[32,4,128]{2,1,0:T(4,128)(2,1)}), bf16[32,4,128]{2,1,0:T(4,128)(2,1)S(1)}, u32[]{:S(2)}, u32[]{:S(2)}) async-start(bf16[32,4,128]{2,1,0:T(4,128)(2,1)} %bitcast.15), calls=%async_computation.2 | async-start | bytes 65536 | tf_op jit(solution)/shard_map/all_to_all | solution.py:78
  274.8 8.8 %all-to-all-done.2 = bf16[32,4,128]{2,1,0:T(4,128)(2,1)S(1)} async-done(((bf16[32,4,128]{2,1,0:T(4,128)(2,1)}), bf16[32,4,128]{2,1,0:T(4,128)(2,1)S(1)}, u32[]{:S(2)}, u32[]{:S(2)}) %all-to-all-start.2) | async-done | bytes 32800 | tf_op jit(solution)/shard_map/all_to_all | solution.py:78
  283.5 1.4 scatter_custom_fusion.1
  285.0 0.0 copy-done.1
  (4 shorter events, 0.0 us)
Async XLA Ops:
  7.2 72.9 %copy-start = (bf16[512,2048]{1,0:T(8,128)(2,1)S(1)}, bf16[512,2048]{1,0:T(8,128)(2,1)}, u32[]{:S(2)}) copy-start(bf16[512,2048]{1,0:T(8,128)(2,1)} %param.11) | copy-start | bytes 6291460
  7.2 188.7 %all-reduce.2.cloned.1.call-start = ((), (), s32[]{:S(2)}) async-start(), calls=%async_computation.4 | async-start | bytes 1048576 | tf_op jit(solution)/shard_map/psum | solution.py:39
  77.3 1.2 copy-start.5
  78.5 1.6 copy-start.6
  80.0 183.2 %reduce-scatter.4.cloned.1.call-start = ((), (), s32[]{:S(2)}) async-start(), calls=%async_computation.5 | async-start | bytes 4456448
  90.8 105.0 %copy-start.2 = (bf16[16,64,128]{2,1,0:T(8,128)(2,1)S(1)}, bf16[16,64,128]{2,1,0:T(8,128)(2,1)}, u32[]{:S(2)}) copy-start(bf16[16,64,128]{2,1,0:T(8,128)(2,1)} %param.10) | copy-start | bytes 786436
  90.9 117.3 %copy-start.3 = (s32[1,32,4]{1,2,0:T(4,128)S(1)}, s32[1,32,4]{1,2,0:T(4,128)}, u32[]{:S(2)}) copy-start(s32[1,32,4]{1,2,0:T(4,128)} %param.12) | copy-start | bytes 1540
  90.9 117.5 %copy-start.4 = (s32[32,1,4]{0,2,1:T(4,128)S(1)}, s32[32,1,4]{0,2,1:T(4,128)}, u32[]{:S(2)}) copy-start(s32[32,1,4]{0,2,1:T(4,128)} %param.13) | copy-start | bytes 1540
  198.2 23.9 %all-to-all-start.1 = ((bf16[32,64,128]{2,1,0:T(8,128)(2,1)}), bf16[32,64,128]{2,1,0:T(8,128)(2,1)S(1)}, u32[]{:S(2)}, u32[]{:S(2)}) async-start(bf16[32,64,128]{2,1,0:T(8,128)(2,1)} %copy.24), calls=%async_computation.1 | async-start | bytes 1048576 | tf_op jit(solution)/shard_map/all_to_all | solution.py:43
  264.5 20.5 %copy-start.1 = (bf16[1024,128]{1,0:T(8,128)(2,1)}, bf16[1024,128]{1,0:T(8,128)(2,1)S(1)}, u32[]{:S(2)}) copy-start(bf16[1024,128]{1,0:T(8,128)(2,1)S(1)} %add_convert_fusion) | copy-start | bytes 786436
  265.8 17.7 %all-to-all-start.2 = ((bf16[32,4,128]{2,1,0:T(4,128)(2,1)}), bf16[32,4,128]{2,1,0:T(4,128)(2,1)S(1)}, u32[]{:S(2)}, u32[]{:S(2)}) async-start(bf16[32,4,128]{2,1,0:T(4,128)(2,1)} %bitcast.15), calls=%async_computation.2 | async-start | bytes 65536 | tf_op jit(solution)/shard_map/all_to_all | solution.py:78
Sparse Core Ops, SparseCore 0:
  80.2 115.6 all-reduce.1
  199.0 64.2 reduce-scatter.3
where the time goes:
time: 295 us; the launch traced here: 292 us
  waiting for transfers between devices  165 us (56%)
  blocking collectives  60.8 us (21%)
  local copies, waits for them, and re-layouts  23.3 us (8%)
  starting transfers between devices  18.9 us (6%)
  between operations  14.2 us (5%)
  matrix products  7.18 us (2%)
    psum x1, waiting for transfers between devices, apply_adapter(): summed_rank = lax.psum(partial_rank.astype(jnp.bfloat16), 'tensor')  105 us
    all_to_all x1, blocking collectives, apply_adapter(): lax.all_to_all(outbox.reshape(owners, resident_adapters * CAP, feature_wi...  60.8 us
    unnamed x3, waiting for transfers between devices  37.9 us
    all_to_all x1, waiting for transfers between devices, apply_adapter(): lax.all_to_all(update.reshape(owners, resident_adapters * CAP, column_spa...  13.6 us
    all_to_all x1, starting transfers between devices, apply_adapter(): lax.all_to_all(update.reshape(owners, resident_adapters * CAP, column_spa...  9.9 us
    all_to_all x1, starting transfers between devices, per_device(): lax.all_to_all(chosen.reshape(owners, -1, column_span), 'adapter', split_...  8.92 us
    all_to_all x1, waiting for transfers between devices, per_device(): lax.all_to_all(chosen.reshape(owners, -1, column_span), 'adapter', split_...  8.75 us
    unnamed x18, local copies, waits for them, and re-layouts  7.78 us
  transfers between devices with their start and end apart: 4, of which 4 were waited for; matrix products, arithmetic and copies ran while one was open for 6% of the time, Pallas kernels for 0%

commit v1 on v0

v1 whole, which is shorter than its diff:
```python
import functools

import jax
import jax.numpy as jnp
from jax import lax
from jax.experimental import pallas as pl
from jax.experimental.pallas import tpu as pltpu
from jax.sharding import PartitionSpec as P

ADAPTER_COUNT = 512
CAP = 4
QUAD = 4
VMEM = pl.BlockSpec(memory_space=pltpu.VMEM)
LIMIT = 20 * 1024 * 1024
BF16 = jnp.bfloat16
F32 = jnp.float32


def call(kernel, out_shape, operands, flops, scratch=(), name=None):
    outs = out_shape if isinstance(out_shape, (list, tuple)) else [out_shape]
    size = sum(x.size * x.dtype.itemsize for x in list(operands) + list(outs))
    return pl.pallas_call(
        kernel,
        out_shape=out_shape,
        in_specs=[VMEM] * len(operands),
        out_specs=jax.tree.map(lambda _: VMEM, out_shape),
        scratch_shapes=list(scratch),
        compiler_params=pltpu.CompilerParams(vmem_limit_bytes=LIMIT),
        cost_estimate=pl.CostEstimate(flops=flops, bytes_accessed=size, transcendentals=0),
        name=name,
    )(*operands)


def base_kernel(columns, tokens_ref, weight_ref, out_ref):
    product = jnp.dot(tokens_ref[...], weight_ref[...], preferred_element_type=F32).astype(BF16)
    for part in range(out_ref.shape[0]):
        out_ref[part] = product[:, part * columns : (part + 1) * columns]


def partial_base(tokens, weight, groups):
    rows, features = tokens.shape
    columns = weight.shape[1] // groups
    step = 4
    return pl.pallas_call(
        functools.partial(base_kernel, columns),
        grid=(groups // step,),
        in_specs=[
            pl.BlockSpec((rows, features), lambda i: (0, 0)),
            pl.BlockSpec((features, step * columns), lambda i: (0, i)),
        ],
        out_specs=pl.BlockSpec((step, rows, columns), lambda i: (i, 0, 0)),
        out_shape=jax.ShapeDtypeStruct((groups, rows, columns), BF16),
        compiler_params=pltpu.CompilerParams(vmem_limit_bytes=LIMIT),
        cost_estimate=pl.CostEstimate(
            flops=2 * rows * features * groups * columns,
            bytes_accessed=2 * (rows * features + (features + rows) * groups * columns),
            transcendentals=0,
        ),
        name="base",
    )(tokens, weight)


def pack_kernel(labels_ref, tokens_ref, slots_ref, packed_ref):
    rows = tokens_ref.shape[0]
    labels = labels_ref[...]
    column = jnp.transpose(jnp.broadcast_to(labels, (8, rows)))[:, 0:1]
    earlier = lax.broadcasted_iota(jnp.int32, (rows, rows), 0) < lax.broadcasted_iota(
        jnp.int32, (rows, rows), 1
    )
    same = jnp.where((column == labels) & earlier, 1, 0)
    slots = labels * CAP + jnp.sum(same, axis=0, keepdims=True)
    slots_ref[...] = slots
    tokens = tokens_ref[...]
    block = 256

    @pl.loop(0, packed_ref.shape[0] // block)
    def _(i):
        first = pl.multiple_of(i * block, block)
        place = lax.broadcasted_iota(jnp.int32, (block, rows), 0) + first
        chosen = jnp.where(place == slots, 1.0, 0.0).astype(BF16)
        packed_ref[pl.ds(first, block), :] = jnp.dot(
            chosen, tokens, preferred_element_type=F32
        ).astype(BF16)


def pack(labels, tokens):
    rows, features = tokens.shape
    slots = ADAPTER_COUNT * CAP
    return call(
        pack_kernel,
        [
            jax.ShapeDtypeStruct((1, rows), jnp.int32),
            jax.ShapeDtypeStruct((slots, features), BF16),
        ],
        (labels, tokens),
        2 * slots * rows * features,
        name="pack",
    )


def down_kernel(rows_ref, weight_ref, out_ref):
    sources, slots, features = rows_ref.shape
    rank = weight_ref.shape[1]
    tile = QUAD * CAP
    owner = lax.broadcasted_iota(jnp.int32, (1, tile, 1), 1) // CAP
    for quad in range(slots // tile):
        rows = rows_ref[:, quad * tile : (quad + 1) * tile, :].reshape(sources * tile, features)
        weight = weight_ref[quad * QUAD : (quad + 1) * QUAD].reshape(QUAD * rank, features)
        product = lax.dot_general(
            rows, weight, (((1,), (1,)), ((), ())), preferred_element_type=F32
        ).reshape(sources, tile, QUAD * rank)
        lowered = jnp.zeros((sources, tile, rank), F32)
        for k in range(QUAD):
            lowered = jnp.where(owner == k, product[:, :, k * rank : (k + 1) * rank], lowered)
        lowered = lowered.reshape(sources // 2, 2, tile, rank)
        out_ref[:, quad * tile : (quad + 1) * tile, :] = jnp.concatenate(
            [lowered[:, 0], lowered[:, 1]], axis=-1
        ).astype(BF16)


def lower(received, weight):
    sources, slots, features = received.shape
    rank = weight.shape[1]
    return call(
        down_kernel,
        jax.ShapeDtypeStruct((sources // 2, slots, 2 * rank), BF16),
        (received, weight),
        2 * sources * slots * features * rank * QUAD,
        name="down",
    )


def up_kernel(lowered_ref, weight_ref, out_ref):
    pairs, slots, wide = lowered_ref.shape
    rank = wide // 2
    tile = QUAD * CAP
    columns = weight_ref.shape[2]
    shape = (pairs, tile, QUAD * rank)
    owner = lax.broadcasted_iota(jnp.int32, shape, 1) // CAP
    lane = lax.broadcasted_iota(jnp.int32, shape, 2) // rank
    own = (owner == lane).reshape(pairs * tile, QUAD * rank)
    for quad in range(slots // tile):
        both = lowered_ref[:, quad * tile : (quad + 1) * tile, :].reshape(pairs * tile, wide)
        weight = weight_ref[quad * QUAD : (quad + 1) * QUAD].reshape(QUAD * rank, columns)
        for half in range(2):
            lowered = both[:, half * rank : (half + 1) * rank]
            spread = jnp.where(own, jnp.concatenate([lowered] * QUAD, axis=-1), 0)
            out_ref[:, half, quad * tile : (quad + 1) * tile, :] = (
                jnp.dot(spread.astype(BF16), weight, preferred_element_type=F32)
                .astype(BF16)
                .reshape(pairs, tile, columns)
            )


def raise_rank(lowered, weight):
    pairs, slots, wide = lowered.shape
    columns = weight.shape[2]
    return call(
        up_kernel,
        jax.ShapeDtypeStruct((pairs, 2, slots, columns), BF16),
        (lowered, weight),
        pairs * 2 * slots * columns * wide * QUAD,
        name="up",
    )


def unpack_kernel(slots_ref, out_ref):
    rows, places = out_ref.shape
    slots = slots_ref[...]
    column = jnp.transpose(jnp.broadcast_to(slots, (8, rows)))[:, 0:1]
    block = 256
    for first in range(0, places, block):
        place = lax.broadcasted_iota(jnp.int32, (rows, block), 1) + first
        out_ref[:, first : first + block] = jnp.where(place == column, 1.0, 0.0).astype(BF16)


def finish_kernel(take_ref, returned_ref, base_ref, accepted_ref, out_ref, chosen_ref):
    rows = base_ref.shape[0]
    update = jnp.dot(take_ref[...], returned_ref[...], preferred_element_type=F32)
    key_value = (base_ref[...].astype(F32) + update).astype(BF16)
    out_ref[...] = key_value
    count = chosen_ref.shape[0]
    place = lax.broadcasted_iota(jnp.int32, (count, rows), 1)
    column = jnp.transpose(jnp.broadcast_to(accepted_ref[...], (8, count)))[:, 0:1]
    take = jnp.where(place == column, 1.0, 0.0).astype(BF16)
    chosen_ref[...] = jnp.dot(take, key_value, preferred_element_type=F32).astype(BF16)


def cache_kernel(targets_ref, moved_ref, out_ref):
    count = targets_ref.shape[1]
    place = lax.broadcasted_iota(jnp.int32, (out_ref.shape[0], count), 0)
    take = jnp.where(place == targets_ref[...], 1.0, 0.0).astype(BF16)
    out_ref[...] = jnp.dot(take, moved_ref[...], preferred_element_type=F32).astype(BF16)


def exchange(array, axis):
    return lax.all_to_all(array, axis, split_axis=0, concat_axis=0, tiled=True)


def per_device(
    tokens,
    row_adapter_index,
    adapter_down_weight,
    adapter_up_weight,
    key_value_weight,
    accepted_branch_rows,
    owner_cache_slots,
):
    owners, groups = lax.axis_size("adapter"), lax.axis_size("tensor")
    rows, features = tokens.shape
    columns = adapter_up_weight.shape[2]
    resident = adapter_down_weight.shape[0]
    here = resident * CAP

    partial_sum = partial_base(tokens, key_value_weight, groups).reshape(groups * rows, columns)
    base = lax.psum_scatter(partial_sum, "tensor", scatter_dimension=0, tiled=True)

    row_adapter_index, _ = lax.optimization_barrier((row_adapter_index, partial_sum))
    slots, packed = pack(row_adapter_index.reshape(1, rows), tokens)
    received = exchange(packed.reshape(owners, here, features), "adapter")
    partial_rank = lower(received, jnp.swapaxes(adapter_down_weight, 1, 2))
    pieces = exchange(partial_rank, "tensor")
    summed = jnp.sum(pieces.astype(F32), axis=0).astype(BF16)
    lowered = lax.all_gather(summed, "tensor", axis=0, tiled=False)
    update = raise_rank(lowered, adapter_up_weight)
    returned = exchange(update.reshape(owners, here, columns), "adapter")
    take = call(
        unpack_kernel, jax.ShapeDtypeStruct((rows, owners * here), BF16), (slots,), 0, name="unpack"
    )
    accepted = accepted_branch_rows.reshape(1, -1)
    count = accepted.shape[1]
    key_value, chosen = call(
        finish_kernel,
        [
            jax.ShapeDtypeStruct((rows, columns), BF16),
            jax.ShapeDtypeStruct((count, columns), BF16),
        ],
        (take, returned.reshape(owners * here, columns), base, accepted),
        2 * rows * owners * here * columns,
        name="finish",
    )
    moved = exchange(chosen.reshape(owners, -1, columns), "adapter").reshape(-1, columns)
    decode_cache = call(
        cache_kernel,
        jax.ShapeDtypeStruct((moved.shape[0], columns), BF16),
        (owner_cache_slots.reshape(1, -1), moved),
        2 * count * count * columns,
        name="cache",
    )
    return (key_value, decode_cache)


def solution(mesh):
    in_specs = (
        P("adapter", "tensor"),
        P("adapter", None),
        P("adapter", "tensor", None),
        P("adapter", None, "tensor"),
        P("tensor", None),
        P("adapter", None, None),
        P(None, "adapter", None),
    )
    out_specs = (P("adapter", "tensor"), P("adapter", "tensor"))
    return jax.shard_map(
        per_device, mesh=mesh, in_specs=in_specs, out_specs=out_specs, check_vma=False
    )
```

time: 295 us -> 172 us (0.58)
  waiting for transfers between devices: 165 us -> 20.1 us
  blocking collectives: 60.8 us -> 99.5 us
  Pallas kernels: 0 us -> 13.4 us
  local copies, waits for them, and re-layouts: 23.3 us -> 11.5 us
  matrix products: 7.18 us -> 0 us
  starting transfers between devices: 18.9 us -> 12.3 us
    psum x1 -> x0, waiting for transfers between devices: 105 us -> none  [apply_adapter(): summed_rank = lax.psum(partial_rank.astype(jnp.bfloat16), 'tensor')]
    unnamed x3 -> x1, waiting for transfers between devices: 37.9 us -> 0.02 us
    all_to_all x1 -> x2, blocking collectives: 60.8 us -> 84.3 us  [exchange(): return lax.all_to_all(array, axis, split_axis=0, concat_axis=0, tiled=True)]
    all_gather x0 -> x1, blocking collectives: none -> 15.2 us  [per_device(): lowered = lax.all_gather(summed, 'tensor', axis=0, tiled=False)]
    pallas_call x0 -> x7, Pallas kernels: none -> 13.4 us  [the longest x6 10.3 us: call(): pl.pallas_call(kernel, out_shape=out_shape, in_specs=[VMEM] * len(operand...]
    scatter x2 -> x0, local copies, waits for them, and re-layouts: 8.61 us -> none  [the longest x1 7.17 us: apply_adapter(): outbox = jnp.zeros((ADAPTER_COUNT * CAP, feature_width), jnp.bfloat16).at...]
    dot_general x3 -> x0, matrix products: 7.18 us -> none  [the longest x1 4.34 us: project(): jnp.dot(tokens, key_value_weight, preferred_element_type=jnp.float32)]
    all_to_all x2, starting transfers between devices: 18.8 us -> 12.3 us  [exchange(): return lax.all_to_all(array, axis, split_axis=0, concat_axis=0, tiled=True)]
  transfers between devices with their start and end apart: 4 -> 3, of which waited for: 4 -> 2; matrix products, arithmetic and copies ran while one was open for 6% -> 0% of each run, Pallas kernels for 0% -> 4%
where the time goes in v1:
time: 172 us; the launch traced here: 171 us
  blocking collectives  99.5 us (58%)
  waiting for transfers between devices  20.1 us (12%)
  between operations  14.1 us (8%)
  Pallas kernels  13.4 us (8%)
  starting transfers between devices  12.3 us (7%)
  local copies, waits for them, and re-layouts  11.5 us (7%)
    all_to_all x2, blocking collectives, exchange(): return lax.all_to_all(array, axis, split_axis=0, concat_axis=0, tiled=True)  84.3 us
    all_to_all x2, waiting for transfers between devices, exchange(): return lax.all_to_all(array, axis, split_axis=0, concat_axis=0, tiled=True)  20.1 us
    all_gather x1, blocking collectives, per_device(): lowered = lax.all_gather(summed, 'tensor', axis=0, tiled=False)  15.2 us
    all_to_all x2, starting transfers between devices, exchange(): return lax.all_to_all(array, axis, split_axis=0, concat_axis=0, tiled=True)  12.3 us
    unnamed x26, local copies, waits for them, and re-layouts  11.2 us
    pallas_call x6, Pallas kernels, call(): pl.pallas_call(kernel, out_shape=out_shape, in_specs=[VMEM] * len(operand...  10.3 us
  transfers between devices with their start and end apart: 3, of which 2 were waited for; matrix products, arithmetic and copies ran while one was open for 0% of the time, Pallas kernels for 4%

profile of v1, /device:TPU:1, one launch (start us, length us, event | category | flops | bytes accessed | tf_op | source)
XLA Modules:
  0.0 171.0 jit_solution(7428392027578918926)
XLA Ops:
  7.2 0.0 reduce-scatter.2.cloned.1.call-start
  7.2 0.0 copy-start.6
  7.2 1.6 copy-done.6
  8.8 0.0 copy-start.7
  8.8 1.2 copy-done.7
  10.0 3.0 %base.1 = bf16[16,1024,128]{2,1,0:T(8,128)(2,1)S(1)} custom-call(bf16[1024,512]{1,0:T(8,128)(2,1)S(1)} %copy-done.7, bf16[512,2048]{1,0:T(8,128)(2,1)S(1)} %copy-done.6), custom_call_target="tpu_custom_call" | custom-call | flops 2147483648 | bytes 7340032 | tf_op jit(solution)/shard_map/base/pallas_call | solution.py:44
  13.1 0.0 copy-start.2
  13.1 1.9 %copy-done.2 = bf16[16,1024,128]{2,1,0:T(8,128)(2,1)} copy-done((bf16[16,1024,128]{2,1,0:T(8,128)(2,1)}, bf16[16,1024,128]{2,1,0:T(8,128)(2,1)S(1)}, u32[]{:S(2)}) %copy-start.2) | copy-done | bytes 4194328
  15.0 0.0 copy-start.8
  15.0 0.0 copy-start.9
  15.0 0.0 reduce-scatter.2.cloned.1.call-update
  15.0 1.2 copy-done.8
  16.2 0.0 copy-done.9
  16.2 4.1 %pack.1 = (s32[1,1024]{1,0:T(1,128)S(1)}, bf16[2048,512]{1,0:T(8,128)(2,1)S(1)}) custom-call(s32[1,1024]{1,0:T(1,128)S(1)} %bitcast.17, bf16[1024,512]{1,0:T(8,128)(2,1)S(1)} %copy-done.8), custom_call_target="tpu_custom_call" | custom-call | flops 2147483648 | bytes 3153920 | tf_op jit(solution)/shard_map/pack/pallas_call | solution.py:22
  20.4 0.0 copy-start.3
  20.4 60.7 %all_to_all.20.rows_ref = bf16[32,64,512]{2,1,0:T(8,128)(2,1)S(1)} all-to-all(bf16[32,64,512]{2,1,0:T(8,128)(2,1)S(1)} %bitcast.13), channel_id=1, replica_groups=mesh['adapter'=32,'tensor'=16] {'adapter'}, dimensions={0} | all-to-all | bytes 4194304 | tf_op jit(solution)/shard_map/all_to_all | solution.py:197
  81.1 0.0 copy-done.3
  81.1 0.0 copy-start.5
  81.1 1.0 down.1
  82.1 0.0 copy-start.10
  82.1 23.6 %all_to_all.21 = bf16[16,64,128]{2,1,0:T(8,128)(2,1)S(1)} all-to-all(bf16[16,64,128]{2,1,0:T(8,128)(2,1)S(1)} %down.1), channel_id=1, replica_groups=mesh['adapter'=32,'tensor'=16] {'tensor'}, dimensions={0} | all-to-all | bytes 524288 | tf_op jit(solution)/shard_map/all_to_all | solution.py:197
  105.8 15.2 %all-gather = bf16[1024,128]{1,0:T(8,128)(2,1)S(1)} all-gather(bf16[64,128]{1,0:T(8,128)(2,1)S(1)} %reduce_sum.12), channel_id=2, replica_groups=mesh['adapter'=32,'tensor'=16] {'tensor'}, dimensions={0}, use_global_device_ids=true | all-gather | bytes 278528 | tf_op jit(solution)/shard_map/all_gather | solution.py:224
  121.0 0.0 copy-done.5
  121.0 1.3 up.1
  122.3 4.8 %all-to-all-start.2 = ((bf16[32,64,128]{2,1,0:T(8,128)(2,1)}), bf16[32,64,128]{2,1,0:T(8,128)(2,1)S(1)}, u32[]{:S(2)}, u32[]{:S(2)}) async-start(bf16[32,64,128]{2,1,0:T(8,128)(2,1)} %bitcast.5), calls=%async_computation.2 | async-start | bytes 1048576 | tf_op jit(solution)/shard_map/all_to_all | solution.py:197
  127.1 0.0 copy-done.10
  127.1 0.1 copy.11
  127.2 0.1 reshape.36.accepted_ref
  127.3 1.1 unpack.1.take_ref
  128.4 0.0 copy-start
  128.4 2.0 %copy-done = bf16[1024,2048]{1,0:T(8,128)(2,1)} copy-done((bf16[1024,2048]{1,0:T(8,128)(2,1)}, bf16[1024,2048]{1,0:T(8,128)(2,1)S(1)}, u32[]{:S(2)}) %copy-start) | copy-done | bytes 4194328
  130.3 11.5 %all-to-all-done.2 = bf16[32,64,128]{2,1,0:T(8,128)(2,1)S(1)} async-done(((bf16[32,64,128]{2,1,0:T(8,128)(2,1)}), bf16[32,64,128]{2,1,0:T(8,128)(2,1)S(1)}, u32[]{:S(2)}, u32[]{:S(2)}) %all-to-all-start.2) | async-done | bytes 524320 | tf_op jit(solution)/shard_map/all_to_all | solution.py:197
  141.9 0.0 reduce-scatter.2.cloned.1.call-done.base_ref
  141.9 0.0 copy-start.1
  141.9 2.2 %copy-done.1 = bf16[1024,2048]{1,0:T(8,128)(2,1)S(1)} copy-done((bf16[1024,2048]{1,0:T(8,128)(2,1)S(1)}, bf16[1024,2048]{1,0:T(8,128)(2,1)}, u32[]{:S(2)}) %copy-start.1) | copy-done | bytes 4194328
  144.1 0.0 copy-start.4
  144.1 0.9 copy-done.4
  145.0 0.0 copy-start.11
  145.0 2.1 %finish.1 = (bf16[1024,128]{1,0:T(8,128)(2,1)}, bf16[128,128]{1,0:T(8,128)(2,1)}) custom-call(bf16[1024,2048]{1,0:T(8,128)(2,1)S(1)} %copy-done.1, bf16[2048,128]{1,0:T(8,128)(2,1)S(1)} %bitcast.12, bf16[1024,128]{1,0:T(8,128)(2,1)S(1)} %copy-done.4, s32[1,128]{1,0:T(1,128)S(1)} %reshape.36.accepted_ref), custom_call_target="tpu_custom_call" | custom-call | flops 536870912 | bytes 5276160 | tf_op jit(solution)/shard_map/finish/pallas_call | solution.py:22
  147.1 7.5 %all-to-all-start.3 = ((bf16[32,4,128]{2,1,0:T(4,128)(2,1)}), bf16[32,4,128]{2,1,0:T(4,128)(2,1)S(1)}, u32[]{:S(2)}, u32[]{:S(2)}) async-start(bf16[32,4,128]{2,1,0:T(4,128)(2,1)} %bitcast.7), calls=%async_computation.4 | async-start | bytes 65536 | tf_op jit(solution)/shard_map/all_to_all | solution.py:197
  154.6 0.0 copy-done.11
  154.6 0.1 copy.12
  154.7 0.1 reshape.37.targets_ref
  154.8 8.6 %all-to-all-done.3 = bf16[32,4,128]{2,1,0:T(4,128)(2,1)S(1)} async-done(((bf16[32,4,128]{2,1,0:T(4,128)(2,1)}), bf16[32,4,128]{2,1,0:T(4,128)(2,1)S(1)}, u32[]{:S(2)}, u32[]{:S(2)}) %all-to-all-start.3) | async-done | bytes 32800 | tf_op jit(solution)/shard_map/all_to_all | solution.py:197
  163.4 0.8 cache.1
  (1 shorter events, 0.0 us)
Async XLA Ops:
  7.2 134.7 %reduce-scatter.2.cloned.1.call-start = ((), (), s32[]{:S(2)}) async-start(), calls=%async_computation.5 | async-start | bytes 4456448 | tf_op jit(solution)/shard_map/reduce_scatter | solution.py:216
  7.2 1.6 copy-start.6
  8.8 1.2 copy-start.7
  13.1 2.0 %copy-start.2 = (bf16[16,1024,128]{2,1,0:T(8,128)(2,1)}, bf16[16,1024,128]{2,1,0:T(8,128)(2,1)S(1)}, u32[]{:S(2)}) copy-start(bf16[16,1024,128]{2,1,0:T(8,128)(2,1)S(1)} %base.1) | copy-start | bytes 12582916
  15.0 1.2 copy-start.8
  15.0 1.2 copy-start.9
  20.4 60.7 %copy-start.3 = (bf16[16,512,64]{1,2,0:T(8,128)(2,1)S(1)}, bf16[16,512,64]{1,2,0:T(8,128)(2,1)}, u32[]{:S(2)}) copy-start(bf16[16,512,64]{1,2,0:T(8,128)(2,1)} %param.9) | copy-start | bytes 3145732
  81.1 39.8 %copy-start.5 = (bf16[16,64,128]{2,1,0:T(8,128)(2,1)S(1)}, bf16[16,64,128]{2,1,0:T(8,128)(2,1)}, u32[]{:S(2)}) copy-start(bf16[16,64,128]{2,1,0:T(8,128)(2,1)} %weight_ref.3) | copy-start | bytes 786436
  82.1 45.0 %copy-start.10 = (s32[1,32,4]{1,2,0:T(4,128)S(1)}, s32[1,32,4]{1,2,0:T(4,128)}, u32[]{:S(2)}) copy-start(s32[1,32,4]{1,2,0:T(4,128)} %param.12) | copy-start | bytes 1540
  122.3 19.6 %all-to-all-start.2 = ((bf16[32,64,128]{2,1,0:T(8,128)(2,1)}), bf16[32,64,128]{2,1,0:T(8,128)(2,1)S(1)}, u32[]{:S(2)}, u32[]{:S(2)}) async-start(bf16[32,64,128]{2,1,0:T(8,128)(2,1)} %bitcast.5), calls=%async_computation.2 | async-start | bytes 1048576 | tf_op jit(solution)/shard_map/all_to_all | solution.py:197
  128.4 2.0 %copy-start = (bf16[1024,2048]{1,0:T(8,128)(2,1)}, bf16[1024,2048]{1,0:T(8,128)(2,1)S(1)}, u32[]{:S(2)}) copy-start(bf16[1024,2048]{1,0:T(8,128)(2,1)S(1)} %unpack.1.take_ref) | copy-start | bytes 12582916
  141.9 2.2 %copy-start.1 = (bf16[1024,2048]{1,0:T(8,128)(2,1)S(1)}, bf16[1024,2048]{1,0:T(8,128)(2,1)}, u32[]{:S(2)}) copy-start(bf16[1024,2048]{1,0:T(8,128)(2,1)} %copy-done) | copy-start | bytes 12582916
  144.1 0.9 copy-start.4
  145.0 9.6 %copy-start.11 = (s32[32,1,4]{0,2,1:T(4,128)S(1)}, s32[32,1,4]{0,2,1:T(4,128)}, u32[]{:S(2)}) copy-start(s32[32,1,4]{0,2,1:T(4,128)} %param.13) | copy-start | bytes 1540
  147.1 16.3 %all-to-all-start.3 = ((bf16[32,4,128]{2,1,0:T(4,128)(2,1)}), bf16[32,4,128]{2,1,0:T(4,128)(2,1)S(1)}, u32[]{:S(2)}, u32[]{:S(2)}) async-start(bf16[32,4,128]{2,1,0:T(4,128)(2,1)} %bitcast.7), calls=%async_computation.4 | async-start | bytes 65536 | tf_op jit(solution)/shard_map/all_to_all | solution.py:197
Sparse Core Ops, SparseCore 0:
  15.2 69.7 reduce-scatter.1

commit v2 on v1

--- a/solution.py
+++ b/solution.py
@@ -31,33 +31,83 @@
     )(*operands)
 
 
-def base_kernel(columns, tokens_ref, weight_ref, out_ref):
-    product = jnp.dot(tokens_ref[...], weight_ref[...], preferred_element_type=F32).astype(BF16)
-    for part in range(out_ref.shape[0]):
-        out_ref[part] = product[:, part * columns : (part + 1) * columns]
-
-
-def partial_base(tokens, weight, groups):
+def product_kernel(chunks, away, other, tokens_ref, weight_ref, *rest):
+    place = lax.axis_index("tensor")
+    chip, core = place // 2, lax.rem(place, 2)
+    parity = 1 - core if away else core
+    columns = rest[-1].shape[-1]
+    outs = rest[1:] if other else rest
+    block = outs[0].shape[1]
+    slots = [(out, k) for out in outs for k in range(out.shape[0])]
+    for i, chunk in enumerate(chunks):
+        group = 2 * lax.rem(chip + chunk, weight_ref.shape[1] // (2 * columns)) + parity
+        weight = weight_ref[:, pl.ds(pl.multiple_of(group * columns, columns), columns)]
+        product = jnp.dot(tokens_ref[...], weight, preferred_element_type=F32)
+        if other:
+            product += rest[0][i].astype(F32)
+        product = product.astype(BF16)
+        for first in range(0, product.shape[0], block):
+            out, k = slots.pop(0)
+            out[k] = product[first : first + block]
+
+
+def products(chunks, away, tokens, weight, columns, outs, other=None):
     rows, features = tokens.shape
-    columns = weight.shape[1] // groups
-    step = 4
-    return pl.pallas_call(
-        functools.partial(base_kernel, columns),
-        grid=(groups // step,),
-        in_specs=[
-            pl.BlockSpec((rows, features), lambda i: (0, 0)),
-            pl.BlockSpec((features, step * columns), lambda i: (0, i)),
-        ],
-        out_specs=pl.BlockSpec((step, rows, columns), lambda i: (i, 0, 0)),
-        out_shape=jax.ShapeDtypeStruct((groups, rows, columns), BF16),
-        compiler_params=pltpu.CompilerParams(vmem_limit_bytes=LIMIT),
-        cost_estimate=pl.CostEstimate(
-            flops=2 * rows * features * groups * columns,
-            bytes_accessed=2 * (rows * features + (features + rows) * groups * columns),
-            transcendentals=0,
-        ),
+    return call(
+        functools.partial(product_kernel, chunks, away, other is not None),
+        [jax.ShapeDtypeStruct((*out, columns), BF16) for out in outs],
+        (tokens, weight) + (() if other is None else (other,)),
+        2 * rows * features * len(chunks) * columns,
         name="base",
-    )(tokens, weight)
+    )
+
+
+def combine_kernel(own_ref, up_ref, down_ref, *outs):
+    rows = own_ref.shape[1]
+    half = rows // 2
+    up = up_ref[...].reshape(3 * half, -1)
+    down = down_ref[...].reshape(3 * half, -1)
+    own = own_ref[...].astype(F32)
+    outs[0][...] = (own[0] + up[:rows].astype(F32)).astype(BF16)
+    outs[1][:half] = (own[1, :half] + up[rows:].astype(F32)).astype(BF16)
+    outs[1][half:] = own_ref[1, half:]
+    outs[2][:half] = own_ref[2, :half]
+    outs[2][half:] = (own[2, half:] + down[:half].astype(F32)).astype(BF16)
+    outs[3][...] = (own[3] + down[half:].astype(F32)).astype(BF16)
+
+
+def shift(array, by, groups):
+    step = 2 * by
+    return lax.ppermute(array, "tensor", [(i, (i + step) % groups) for i in range(groups)])
+
+
+def sum_base(tokens, weight, columns, groups, after):
+    rows = tokens.shape[0]
+    half = rows // 2
+    swap = [(i, i ^ 1) for i in range(groups)]
+    far, near = (2, 4, 6), (0, 1, 3, 5, 7)
+    (far_away,) = products(far, True, tokens, weight, columns, [(3, rows)])
+    far_other = lax.ppermute(far_away, "tensor", swap)
+    tokens, far_away = lax.optimization_barrier((tokens, far_away))
+    (near_away,) = products(near, True, tokens, weight, columns, [(5, rows)])
+    near_other = lax.ppermute(near_away, "tensor", swap)
+    plus, minus = products(
+        far, False, tokens, weight, columns, [(3, half), (3, half)], far_other
+    )
+    up, down = shift(plus, 1, groups), shift(minus, -1, groups)
+    mine, own = products(near, False, tokens, weight, columns, [(1, rows), (4, rows)], near_other)
+    sent = call(
+        combine_kernel,
+        [jax.ShapeDtypeStruct((rows, columns), BF16)] * 4,
+        (own, up, down),
+        rows * columns * 4,
+        name="combine",
+    )
+    far_up, far_down = shift(sent[1], 3, groups), shift(sent[2], -3, groups)
+    near_up, near_down = shift(sent[0], 1, groups), shift(sent[3], -1, groups)
+    came = [far_up, far_down, near_up, near_down]
+    after, *came = lax.optimization_barrier((after, *came))
+    return after, [mine.reshape(rows, columns), *came]
 
 
 def pack_kernel(labels_ref, tokens_ref, slots_ref, packed_ref):
@@ -174,10 +224,14 @@
         out_ref[:, first : first + block] = jnp.where(place == column, 1.0, 0.0).astype(BF16)
 
 
-def finish_kernel(take_ref, returned_ref, base_ref, accepted_ref, out_ref, chosen_ref):
-    rows = base_ref.shape[0]
+def finish_kernel(take_ref, returned_ref, accepted_ref, *rest):
+    base_refs, (out_ref, chosen_ref) = rest[:-2], rest[-2:]
+    rows = out_ref.shape[0]
     update = jnp.dot(take_ref[...], returned_ref[...], preferred_element_type=F32)
-    key_value = (base_ref[...].astype(F32) + update).astype(BF16)
+    base = base_refs[0][...].astype(F32)
+    for base_ref in base_refs[1:]:
+        base += base_ref[...].astype(F32)
+    key_value = (base + update).astype(BF16)
     out_ref[...] = key_value
     count = chosen_ref.shape[0]
     place = lax.broadcasted_iota(jnp.int32, (count, rows), 1)
@@ -193,8 +247,23 @@
     out_ref[...] = jnp.dot(take, moved_ref[...], preferred_element_type=F32).astype(BF16)
 
 
-def exchange(array, axis):
-    return lax.all_to_all(array, axis, split_axis=0, concat_axis=0, tiled=True)
+def exchange(array, axis, among=None):
+    return lax.all_to_all(
+        array, axis, split_axis=0, concat_axis=0, tiled=True, axis_index_groups=among
+    )
+
+
+def sum_over_tensor(partial, core, pairs, chips):
+    both = lax.all_gather(partial, "tensor", axis=0, axis_index_groups=pairs)
+    half = partial.shape[0] // 2
+    mine = lax.dynamic_slice_in_dim(both, core * half, half, axis=1).astype(F32)
+    mine = (mine[0] + mine[1]).astype(BF16)
+    pieces = exchange(mine, "tensor", chips)
+    pieces = pieces.reshape(half, 1, *partial.shape[1:])
+    summed = jnp.sum(pieces.astype(F32), axis=0).astype(BF16)
+    summed = jnp.broadcast_to(summed, (half, *partial.shape[1:]))
+    mine = exchange(summed, "tensor", chips)
+    return lax.all_gather(mine, "tensor", axis=0, axis_index_groups=pairs, tiled=True)
 
 
 def per_device(
@@ -212,16 +281,18 @@
     resident = adapter_down_weight.shape[0]
     here = resident * CAP
 
-    partial_sum = partial_base(tokens, key_value_weight, groups).reshape(groups * rows, columns)
-    base = lax.psum_scatter(partial_sum, "tensor", scatter_dimension=0, tiled=True)
-
-    row_adapter_index, _ = lax.optimization_barrier((row_adapter_index, partial_sum))
+    core = lax.rem(lax.axis_index("tensor"), 2)
+    pairs = [[2 * y, 2 * y + 1] for y in range(groups // 2)]
+    chips = [[2 * y + c for y in range(groups // 2)] for c in range(2)]
+
     slots, packed = pack(row_adapter_index.reshape(1, rows), tokens)
     received = exchange(packed.reshape(owners, here, features), "adapter")
+
+    tokens, slots = lax.optimization_barrier((tokens, slots))
+    received, base = sum_base(tokens, key_value_weight, columns, groups, received)
+
     partial_rank = lower(received, jnp.swapaxes(adapter_down_weight, 1, 2))
-    pieces = exchange(partial_rank, "tensor")
-    summed = jnp.sum(pieces.astype(F32), axis=0).astype(BF16)
-    lowered = lax.all_gather(summed, "tensor", axis=0, tiled=False)
+    lowered = sum_over_tensor(partial_rank, core, pairs, chips)
     update = raise_rank(lowered, adapter_up_weight)
     returned = exchange(update.reshape(owners, here, columns), "adapter")
     take = call(
@@ -235,7 +306,7 @@
             jax.ShapeDtypeStruct((rows, columns), BF16),
             jax.ShapeDtypeStruct((count, columns), BF16),
         ],
-        (take, returned.reshape(owners * here, columns), base, accepted),
+        (take, returned.reshape(owners * here, columns), accepted, *base),
         2 * rows * owners * here * columns,
         name="finish",
     )

time: 172 us -> 164 us (0.953)
  blocking collectives: 99.5 us -> 31.3 us
  starting transfers between devices: 12.3 us -> 59.6 us
  waiting for transfers between devices: 20.1 us -> 44.7 us
  between operations: 14.1 us -> 0.89 us
  Pallas kernels: 13.4 us -> 17.2 us
  local copies, waits for them, and re-layouts: 11.5 us -> 8.97 us
    all_to_all x2, blocking collectives: 84.3 us -> 23 us  [exchange(): lax.all_to_all(array, axis, split_axis=0, concat_axis=0, tiled=True, axis...]
    ppermute x0 -> x8, starting transfers between devices: none -> 27.9 us  [the longest x6 23.1 us: shift(): lax.ppermute(array, 'tensor', [(i, (i + step) % groups) for i in range(gr...]
    ppermute x0 -> x8, waiting for transfers between devices: none -> 25.2 us  [the longest x6 23 us: shift(): lax.ppermute(array, 'tensor', [(i, (i + step) % groups) for i in range(gr...]
    all_to_all x2 -> x3, starting transfers between devices: 12.3 us -> 31.7 us  [exchange(): lax.all_to_all(array, axis, split_axis=0, concat_axis=0, tiled=True, axis...]
    all_gather x1 -> x2, blocking collectives: 15.2 us -> 8.34 us  [the longest x1 4.8 us: sum_over_tensor(): lax.all_gather(mine, 'tensor', axis=0, axis_index_groups=pairs, tiled=True)]
    pallas_call x6 -> x11, Pallas kernels: 10.3 us -> 17.2 us  [call(): pl.pallas_call(kernel, out_shape=out_shape, in_specs=[VMEM] * len(operand...]
    pallas_call x1 -> x0, Pallas kernels: 3.03 us -> none  [partial_base(): pl.pallas_call(functools.partial(base_kernel, columns), grid=(groups // s...]
    unnamed x26 -> x24, local copies, waits for them, and re-layouts: 11.2 us -> 8.75 us
  transfers between devices with their start and end apart: 3 -> 11, of which waited for: 2 -> 9; matrix products, arithmetic and copies ran while one was open for 0% -> 0% of each run, Pallas kernels for 4% -> 4%
where the time goes in v2:
time: 164 us; the launch traced here: 163 us
  starting transfers between devices  59.6 us (36%)
  waiting for transfers between devices  44.7 us (27%)
  blocking collectives  31.3 us (19%)
  Pallas kernels  17.2 us (10%)
  local copies, waits for them, and re-layouts  8.97 us (5%)
    all_to_all x3, starting transfers between devices, exchange(): lax.all_to_all(array, axis, split_axis=0, concat_axis=0, tiled=True, axis...  31.7 us
    ppermute x6, starting transfers between devices, shift(): lax.ppermute(array, 'tensor', [(i, (i + step) % groups) for i in range(gr...  23.1 us
    all_to_all x2, blocking collectives, exchange(): lax.all_to_all(array, axis, split_axis=0, concat_axis=0, tiled=True, axis...  23 us
    ppermute x6, waiting for transfers between devices, shift(): lax.ppermute(array, 'tensor', [(i, (i + step) % groups) for i in range(gr...  23 us
    all_to_all x3, waiting for transfers between devices, exchange(): lax.all_to_all(array, axis, split_axis=0, concat_axis=0, tiled=True, axis...  19.5 us
    pallas_call x11, Pallas kernels, call(): pl.pallas_call(kernel, out_shape=out_shape, in_specs=[VMEM] * len(operand...  17.2 us
    unnamed x24, local copies, waits for them, and re-layouts  8.75 us
    all_gather x1, blocking collectives, sum_over_tensor(): lax.all_gather(mine, 'tensor', axis=0, axis_index_groups=pairs, tiled=True)  4.8 us
  transfers between devices with their start and end apart: 11, of which 9 were waited for; matrix products, arithmetic and copies ran while one was open for 0% of the time, Pallas kernels for 4%

profile of v2, /device:TPU:1, one launch (start us, length us, event | category | flops | bytes accessed | tf_op | source)
XLA Modules:
  0.0 162.7 jit_solution(13619009430028625846)
XLA Ops:
  0.6 0.0 copy-start.3
  0.6 1.2 copy-done.3
  1.9 0.0 copy-start.8
  1.9 0.7 copy-done.8
  2.5 4.1 %pack.1 = (s32[1,1024]{1,0:T(1,128)S(1)}, bf16[2048,512]{1,0:T(8,128)(2,1)S(1)}) custom-call(s32[1,1024]{1,0:T(1,128)S(1)} %bitcast.18, bf16[1024,512]{1,0:T(8,128)(2,1)S(1)} %copy-done.3), custom_call_target="tpu_custom_call" | custom-call | flops 2147483648 | bytes 3153920 | tf_op jit(solution)/shard_map/pack/pallas_call | solution.py:22
  6.7 0.0 copy-start.5
  6.7 1.3 copy-done.5
  8.0 0.0 copy-start
  8.0 0.0 copy-start.4
  8.0 14.1 %all-to-all-start = ((bf16[32,64,512]{2,1,0:T(8,128)(2,1)}), bf16[32,64,512]{2,1,0:T(8,128)(2,1)}, u32[]{:S(2)}, u32[]{:S(2)}) async-start(bf16[32,64,512]{2,1,0:T(8,128)(2,1)} %bitcast.14), calls=%async_computation | async-start | bytes 4194304 | tf_op jit(solution)/shard_map/all_to_all | solution.py:251
  22.1 0.0 copy-done
  22.1 0.0 copy-done.4
  22.1 1.0 base.4
  23.1 1.6 base.5
  24.7 2.9 %collective-permute-start = (bf16[5,1024,128]{2,1,0:T(8,128)(2,1)S(1)}, bf16[5,1024,128]{2,1,0:T(8,128)(2,1)S(1)}, u32[]{:S(2)}, u32[]{:S(2)}) collective-permute-start(bf16[5,1024,128]{2,1,0:T(8,128)(2,1)S(1)} %base.5), channel_id=1, source_target_pairs={{0,1},{1,0},{2,3},{3,2},{4,5},{5,4},{6,7},{7,6},{8,9},{9,8},{10,11... | collective-permute-start | bytes 3932168 | tf_op jit(solution)/shard_map/ppermute | solution.py:93
  27.6 1.9 %collective-permute-start.1 = (bf16[3,1024,128]{2,1,0:T(8,128)(2,1)S(1)}, bf16[3,1024,128]{2,1,0:T(8,128)(2,1)S(1)}, u32[]{:S(2)}, u32[]{:S(2)}) collective-permute-start(bf16[3,1024,128]{2,1,0:T(8,128)(2,1)S(1)} %base.4), channel_id=1, source_target_pairs={{0,1},{1,0},{2,3},{3,2},{4,5},{5,4},{6,7},{7,6},{8,9},{9,8},{10,11... | collective-permute-start | bytes 2359304 | tf_op jit(solution)/shard_map/ppermute | solution.py:90
  29.5 2.3 %collective-permute-done.1.rest_0_ = bf16[3,1024,128]{2,1,0:T(8,128)(2,1)S(1)} collective-permute-done((bf16[3,1024,128]{2,1,0:T(8,128)(2,1)S(1)}, bf16[3,1024,128]{2,1,0:T(8,128)(2,1)S(1)}, u32[]{:S(2)}, u32[]{:S(2)}) %collective-permute-start.1) | collective-permute-done | bytes 786464 | tf_op jit(solution)/shard_map/ppermute | solution.py:90
  31.7 1.0 base.7
  32.7 3.2 %collective-permute-start.2 = (bf16[3,512,128]{2,1,0:T(8,128)(2,1)S(1)}, bf16[3,512,128]{2,1,0:T(8,128)(2,1)S(1)}, u32[]{:S(2)}, u32[]{:S(2)}) collective-permute-start(bf16[3,512,128]{2,1,0:T(8,128)(2,1)S(1)} %get-tuple-element.28), channel_id=1, source_target_pairs={{0,2},{1,3},{2,4},{3,5},{4,6},{5,7},{6,8},{7,9},{8,10},{9,11},{10,... | collective-permute-start | bytes 1179656 | tf_op jit(solution)/shard_map/ppermute | solution.py:81
  36.0 3.8 %collective-permute-start.3 = (bf16[3,512,128]{2,1,0:T(8,128)(2,1)S(1)}, bf16[3,512,128]{2,1,0:T(8,128)(2,1)S(1)}, u32[]{:S(2)}, u32[]{:S(2)}) collective-permute-start(bf16[3,512,128]{2,1,0:T(8,128)(2,1)S(1)} %get-tuple-element.29), channel_id=1, source_target_pairs={{0,14},{1,15},{2,0},{3,1},{4,2},{5,3},{6,4},{7,5},{8,6},{9,7},{10,... | collective-permute-start | bytes 1179656 | tf_op jit(solution)/shard_map/ppermute | solution.py:81
  39.8 0.0 collective-permute-done.rest_0_
  39.8 1.6 base.6
  41.4 5.9 %collective-permute-done.2.up_ref = bf16[3,512,128]{2,1,0:T(8,128)(2,1)S(1)} collective-permute-done((bf16[3,512,128]{2,1,0:T(8,128)(2,1)S(1)}, bf16[3,512,128]{2,1,0:T(8,128)(2,1)S(1)}, u32[]{:S(2)}, u32[]{:S(2)}) %collective-permute-start.2) | collective-permute-done | bytes 393248 | tf_op jit(solution)/shard_map/ppermute | solution.py:81
  47.3 0.9 collective-permute-done.3.down_ref
  48.2 0.2 combine.1
  48.4 7.6 %collective-permute-start.4 = (bf16[1024,128]{1,0:T(8,128)(2,1)S(1)}, bf16[1024,128]{1,0:T(8,128)(2,1)S(1)}, u32[]{:S(2)}, u32[]{:S(2)}) collective-permute-start(bf16[1024,128]{1,0:T(8,128)(2,1)S(1)} %get-tuple-element.30), channel_id=1, source_target_pairs={{0,6},{1,7},{2,8},{3,9},{4,10},{5,11},{6,12},{7,13},{8,14},{9,15},... | collective-permute-start | bytes 786440 | tf_op jit(solution)/shard_map/ppermute | solution.py:81
  56.1 1.9 %collective-permute-start.5 = (bf16[1024,128]{1,0:T(8,128)(2,1)S(1)}, bf16[1024,128]{1,0:T(8,128)(2,1)S(1)}, u32[]{:S(2)}, u32[]{:S(2)}) collective-permute-start(bf16[1024,128]{1,0:T(8,128)(2,1)S(1)} %get-tuple-element.31), channel_id=1, source_target_pairs={{0,10},{1,11},{2,12},{3,13},{4,14},{5,15},{6,0},{7,1},{8,2},{9,3},... | collective-permute-start | bytes 786440 | tf_op jit(solution)/shard_map/ppermute | solution.py:81
  58.0 1.9 %collective-permute-start.6 = (bf16[1024,128]{1,0:T(8,128)(2,1)S(1)}, bf16[1024,128]{1,0:T(8,128)(2,1)S(1)}, u32[]{:S(2)}, u32[]{:S(2)}) collective-permute-start(bf16[1024,128]{1,0:T(8,128)(2,1)S(1)} %get-tuple-element.32), channel_id=1, source_target_pairs={{0,2},{1,3},{2,4},{3,5},{4,6},{5,7},{6,8},{7,9},{8,10},{9,11},{10,... | collective-permute-start | bytes 786440 | tf_op jit(solution)/shard_map/ppermute | solution.py:81
  59.9 4.6 %collective-permute-start.7 = (bf16[1024,128]{1,0:T(8,128)(2,1)S(1)}, bf16[1024,128]{1,0:T(8,128)(2,1)S(1)}, u32[]{:S(2)}, u32[]{:S(2)}) collective-permute-start(bf16[1024,128]{1,0:T(8,128)(2,1)S(1)} %get-tuple-element.33), channel_id=1, source_target_pairs={{0,14},{1,15},{2,0},{3,1},{4,2},{5,3},{6,4},{7,5},{8,6},{9,7},{10,... | collective-permute-start | bytes 786440 | tf_op jit(solution)/shard_map/ppermute | solution.py:81
  64.5 7.7 %collective-permute-done.4.rest_1_ = bf16[1024,128]{1,0:T(8,128)(2,1)S(1)} collective-permute-done((bf16[1024,128]{1,0:T(8,128)(2,1)S(1)}, bf16[1024,128]{1,0:T(8,128)(2,1)S(1)}, u32[]{:S(2)}, u32[]{:S(2)}) %collective-permute-start.4) | collective-permute-done | bytes 262176 | tf_op jit(solution)/shard_map/ppermute | solution.py:81
  72.2 5.6 %collective-permute-done.5.rest_2_ = bf16[1024,128]{1,0:T(8,128)(2,1)S(1)} collective-permute-done((bf16[1024,128]{1,0:T(8,128)(2,1)S(1)}, bf16[1024,128]{1,0:T(8,128)(2,1)S(1)}, u32[]{:S(2)}, u32[]{:S(2)}) %collective-permute-start.5) | collective-permute-done | bytes 262176 | tf_op jit(solution)/shard_map/ppermute | solution.py:81
  77.8 0.5 collective-permute-done.6.rest_3_
  78.3 2.3 %collective-permute-done.7.rest_4_ = bf16[1024,128]{1,0:T(8,128)(2,1)S(1)} collective-permute-done((bf16[1024,128]{1,0:T(8,128)(2,1)S(1)}, bf16[1024,128]{1,0:T(8,128)(2,1)S(1)}, u32[]{:S(2)}, u32[]{:S(2)}) %collective-permute-start.7) | collective-permute-done | bytes 262176 | tf_op jit(solution)/shard_map/ppermute | solution.py:81
  80.6 0.0 all-to-all-done.rows_ref
  80.6 0.0 copy-start.6
  80.6 1.2 copy-done.6
  81.9 2.6 %down.1 = bf16[16,64,128]{2,1,0:T(8,128)(2,1)S(1)} custom-call(bf16[32,64,512]{2,1,0:T(8,128)(2,1)} %all-to-all-done.rows_ref, bf16[16,64,512]{2,1,0:T(8,128)(2,1)S(1)} %bitcast.15), custom_call_target="tpu_custom_call" | custom-call | flops 536870912 | bytes 3407872 | tf_op jit(solution)/shard_map/down/pallas_call | solution.py:22
  84.5 0.0 copy-start.7
  84.5 3.5 %all-gather = bf16[32,64,128]{2,1,0:T(8,128)(2,1)S(1)} all-gather(bf16[16,64,128]{2,1,0:T(8,128)(2,1)S(1)} %down.1), channel_id=2, replica_groups={{0,1},{2,3},{4,5},{6,7},{8,9},{10,11},{12,13},{14,15},{16,17},{18,19},{..., dimensions={0}, use_global_device_ids=true | all-gather | bytes 786432 | tf_op jit(solution)/shard_map/all_gather | solution.py:257
  88.1 12.6 %all_to_all.25 = bf16[8,64,128]{2,1,0:T(8,128)(2,1)S(1)} all-to-all(bf16[8,64,128]{2,1,0:T(8,128)(2,1)S(1)} %fusion.1), channel_id=1, replica_groups={{0,2,4,6,8,10,12,14},{1,3,5,7,9,11,13,15},{16,18,20,22,24,26,28,30},{17..., dimensions={0} | all-to-all | bytes 262144 | tf_op jit(solution)/shard_map/all_to_all | solution.py:251
  100.7 10.4 %all_to_all.26 = bf16[8,64,128]{2,1,0:T(8,128)(2,1)S(1)} all-to-all(bf16[8,64,128]{2,1,0:T(8,128)(2,1)S(1)} %broadcast_in_dim.2), channel_id=1, replica_groups={{0,2,4,6,8,10,12,14},{1,3,5,7,9,11,13,15},{16,18,20,22,24,26,28,30},{17..., dimensions={0} | all-to-all | bytes 262144 | tf_op jit(solution)/shard_map/all_to_all | solution.py:251
  111.2 4.8 %all_gather.11.lowered_ref = bf16[16,64,128]{2,1,0:T(8,128)(2,1)S(1)} all-gather(bf16[8,64,128]{2,1,0:T(8,128)(2,1)S(1)} %all_to_all.26), channel_id=1, replica_groups={{0,1},{2,3},{4,5},{6,7},{8,9},{10,11},{12,13},{14,15},{16,17},{18,19},{..., dimensions={0}, use_global_device_ids=true | all-gather | bytes 393216 | tf_op jit(solution)/shard_map/all_gather | solution.py:266
  116.0 0.0 copy-done.7
  116.0 1.3 up.1
  117.2 9.4 %all-to-all-start.3 = ((bf16[32,64,128]{2,1,0:T(8,128)(2,1)}), bf16[32,64,128]{2,1,0:T(8,128)(2,1)S(1)}, u32[]{:S(2)}, u32[]{:S(2)}) async-start(bf16[32,64,128]{2,1,0:T(8,128)(2,1)} %bitcast.5), calls=%async_computation.3 | async-start | bytes 1048576 | tf_op jit(solution)/shard_map/all_to_all | solution.py:251
  126.7 0.0 copy-start.9
  126.7 1.1 unpack.1.take_ref
  127.7 0.0 copy-start.1
  127.7 1.9 %copy-done.1 = bf16[1024,2048]{1,0:T(8,128)(2,1)} copy-done((bf16[1024,2048]{1,0:T(8,128)(2,1)}, bf16[1024,2048]{1,0:T(8,128)(2,1)S(1)}, u32[]{:S(2)}) %copy-start.1) | copy-done | bytes 4194328
  129.7 0.0 copy-done.9
  129.7 0.1 copy.13
  129.8 0.1 reshape.40.accepted_ref
  129.9 10.9 %all-to-all-done.3 = bf16[32,64,128]{2,1,0:T(8,128)(2,1)S(1)} async-done(((bf16[32,64,128]{2,1,0:T(8,128)(2,1)}), bf16[32,64,128]{2,1,0:T(8,128)(2,1)S(1)}, u32[]{:S(2)}, u32[]{:S(2)}) %all-to-all-start.3) | async-done | bytes 524320 | tf_op jit(solution)/shard_map/all_to_all | solution.py:251
  140.8 0.0 copy-start.2
  140.8 2.2 %copy-done.2 = bf16[1024,2048]{1,0:T(8,128)(2,1)S(1)} copy-done((bf16[1024,2048]{1,0:T(8,128)(2,1)S(1)}, bf16[1024,2048]{1,0:T(8,128)(2,1)}, u32[]{:S(2)}) %copy-start.2) | copy-done | bytes 4194328
  143.0 0.0 copy-start.10
  143.0 2.1 %finish.1 = (bf16[1024,128]{1,0:T(8,128)(2,1)}, bf16[128,128]{1,0:T(8,128)(2,1)}) custom-call(bf16[1024,2048]{1,0:T(8,128)(2,1)S(1)} %copy-done.2, bf16[2048,128]{1,0:T(8,128)(2,1)S(1)} %bitcast.13, s32[1,128]{1,0:T(1,128)S(1)} %reshape.40.accepted_ref, bf16[1024,128]{1,0:T(8,128)(2,1)S(1)} %bitcast.16, ...), custom_call_target="tpu_custom_call" | custom-call | flops 536870912 | bytes 6324736 | tf_op jit(solution)/shard_map/finish/pallas_call | solution.py:22
  145.1 8.1 %all-to-all-start.4 = ((bf16[32,4,128]{2,1,0:T(4,128)(2,1)}), bf16[32,4,128]{2,1,0:T(4,128)(2,1)S(1)}, u32[]{:S(2)}, u32[]{:S(2)}) async-start(bf16[32,4,128]{2,1,0:T(4,128)(2,1)} %bitcast.8), calls=%async_computation.4 | async-start | bytes 65536 | tf_op jit(solution)/shard_map/all_to_all | solution.py:251
  153.2 0.0 copy-done.10
  153.2 0.1 copy.14
  153.3 0.1 reshape.42.targets_ref
  153.4 8.6 %all-to-all-done.4 = bf16[32,4,128]{2,1,0:T(4,128)(2,1)S(1)} async-done(((bf16[32,4,128]{2,1,0:T(4,128)(2,1)}), bf16[32,4,128]{2,1,0:T(4,128)(2,1)S(1)}, u32[]{:S(2)}, u32[]{:S(2)}) %all-to-all-start.4) | async-done | bytes 32800 | tf_op jit(solution)/shard_map/all_to_all | solution.py:251
  162.0 0.8 cache.1
  (4 shorter events, 0.1 us)
Async XLA Ops:
  0.6 1.2 copy-start.3
  1.9 0.7 copy-start.8
  6.7 1.3 copy-start.5
  8.0 14.1 %copy-start = (bf16[512,2048]{1,0:T(8,128)(2,1)S(1)}, bf16[512,2048]{1,0:T(8,128)(2,1)}, u32[]{:S(2)}) copy-start(bf16[512,2048]{1,0:T(8,128)(2,1)} %weight_ref.8) | copy-start | bytes 6291460
  8.0 14.1 %copy-start.4 = (bf16[1024,512]{1,0:T(8,128)(2,1)S(1)}, bf16[1024,512]{1,0:T(8,128)(2,1)}, u32[]{:S(2)}) copy-start(bf16[1024,512]{1,0:T(8,128)(2,1)} %tokens_ref.5) | copy-start | bytes 3145732
  8.0 72.7 %all-to-all-start = ((bf16[32,64,512]{2,1,0:T(8,128)(2,1)}), bf16[32,64,512]{2,1,0:T(8,128)(2,1)}, u32[]{:S(2)}, u32[]{:S(2)}) async-start(bf16[32,64,512]{2,1,0:T(8,128)(2,1)} %bitcast.14), calls=%async_computation | async-start | bytes 4194304 | tf_op jit(solution)/shard_map/all_to_all | solution.py:251
  24.7 15.1 %collective-permute-start = (bf16[5,1024,128]{2,1,0:T(8,128)(2,1)S(1)}, bf16[5,1024,128]{2,1,0:T(8,128)(2,1)S(1)}, u32[]{:S(2)}, u32[]{:S(2)}) collective-permute-start(bf16[5,1024,128]{2,1,0:T(8,128)(2,1)S(1)} %base.5), channel_id=1, source_target_pairs={{0,1},{1,0},{2,3},{3,2},{4,5},{5,4},{6,7},{7,6},{8,9},{9,8},{10,11... | collective-permute-start | bytes 3932168 | tf_op jit(solution)/shard_map/ppermute | solution.py:93
  27.6 4.2 %collective-permute-start.1 = (bf16[3,1024,128]{2,1,0:T(8,128)(2,1)S(1)}, bf16[3,1024,128]{2,1,0:T(8,128)(2,1)S(1)}, u32[]{:S(2)}, u32[]{:S(2)}) collective-permute-start(bf16[3,1024,128]{2,1,0:T(8,128)(2,1)S(1)} %base.4), channel_id=1, source_target_pairs={{0,1},{1,0},{2,3},{3,2},{4,5},{5,4},{6,7},{7,6},{8,9},{9,8},{10,11... | collective-permute-start | bytes 2359304 | tf_op jit(solution)/shard_map/ppermute | solution.py:90
  32.7 14.6 %collective-permute-start.2 = (bf16[3,512,128]{2,1,0:T(8,128)(2,1)S(1)}, bf16[3,512,128]{2,1,0:T(8,128)(2,1)S(1)}, u32[]{:S(2)}, u32[]{:S(2)}) collective-permute-start(bf16[3,512,128]{2,1,0:T(8,128)(2,1)S(1)} %get-tuple-element.28), channel_id=1, source_target_pairs={{0,2},{1,3},{2,4},{3,5},{4,6},{5,7},{6,8},{7,9},{8,10},{9,11},{10,... | collective-permute-start | bytes 1179656 | tf_op jit(solution)/shard_map/ppermute | solution.py:81
  36.0 12.3 %collective-permute-start.3 = (bf16[3,512,128]{2,1,0:T(8,128)(2,1)S(1)}, bf16[3,512,128]{2,1,0:T(8,128)(2,1)S(1)}, u32[]{:S(2)}, u32[]{:S(2)}) collective-permute-start(bf16[3,512,128]{2,1,0:T(8,128)(2,1)S(1)} %get-tuple-element.29), channel_id=1, source_target_pairs={{0,14},{1,15},{2,0},{3,1},{4,2},{5,3},{6,4},{7,5},{8,6},{9,7},{10,... | collective-permute-start | bytes 1179656 | tf_op jit(solution)/shard_map/ppermute | solution.py:81
  48.4 23.8 %collective-permute-start.4 = (bf16[1024,128]{1,0:T(8,128)(2,1)S(1)}, bf16[1024,128]{1,0:T(8,128)(2,1)S(1)}, u32[]{:S(2)}, u32[]{:S(2)}) collective-permute-start(bf16[1024,128]{1,0:T(8,128)(2,1)S(1)} %get-tuple-element.30), channel_id=1, source_target_pairs={{0,6},{1,7},{2,8},{3,9},{4,10},{5,11},{6,12},{7,13},{8,14},{9,15},... | collective-permute-start | bytes 786440 | tf_op jit(solution)/shard_map/ppermute | solution.py:81
  56.1 21.7 %collective-permute-start.5 = (bf16[1024,128]{1,0:T(8,128)(2,1)S(1)}, bf16[1024,128]{1,0:T(8,128)(2,1)S(1)}, u32[]{:S(2)}, u32[]{:S(2)}) collective-permute-start(bf16[1024,128]{1,0:T(8,128)(2,1)S(1)} %get-tuple-element.31), channel_id=1, source_target_pairs={{0,10},{1,11},{2,12},{3,13},{4,14},{5,15},{6,0},{7,1},{8,2},{9,3},... | collective-permute-start | bytes 786440 | tf_op jit(solution)/shard_map/ppermute | solution.py:81
  58.0 20.3 %collective-permute-start.6 = (bf16[1024,128]{1,0:T(8,128)(2,1)S(1)}, bf16[1024,128]{1,0:T(8,128)(2,1)S(1)}, u32[]{:S(2)}, u32[]{:S(2)}) collective-permute-start(bf16[1024,128]{1,0:T(8,128)(2,1)S(1)} %get-tuple-element.32), channel_id=1, source_target_pairs={{0,2},{1,3},{2,4},{3,5},{4,6},{5,7},{6,8},{7,9},{8,10},{9,11},{10,... | collective-permute-start | bytes 786440 | tf_op jit(solution)/shard_map/ppermute | solution.py:81
  59.9 20.7 %collective-permute-start.7 = (bf16[1024,128]{1,0:T(8,128)(2,1)S(1)}, bf16[1024,128]{1,0:T(8,128)(2,1)S(1)}, u32[]{:S(2)}, u32[]{:S(2)}) collective-permute-start(bf16[1024,128]{1,0:T(8,128)(2,1)S(1)} %get-tuple-element.33), channel_id=1, source_target_pairs={{0,14},{1,15},{2,0},{3,1},{4,2},{5,3},{6,4},{7,5},{8,6},{9,7},{10,... | collective-permute-start | bytes 786440 | tf_op jit(solution)/shard_map/ppermute | solution.py:81
  80.6 1.2 copy-start.6
  84.5 31.5 %copy-start.7 = (bf16[16,64,128]{2,1,0:T(8,128)(2,1)S(1)}, bf16[16,64,128]{2,1,0:T(8,128)(2,1)}, u32[]{:S(2)}) copy-start(bf16[16,64,128]{2,1,0:T(8,128)(2,1)} %weight_ref.9) | copy-start | bytes 786436
  117.2 23.6 %all-to-all-start.3 = ((bf16[32,64,128]{2,1,0:T(8,128)(2,1)}), bf16[32,64,128]{2,1,0:T(8,128)(2,1)S(1)}, u32[]{:S(2)}, u32[]{:S(2)}) async-start(bf16[32,64,128]{2,1,0:T(8,128)(2,1)} %bitcast.5), calls=%async_computation.3 | async-start | bytes 1048576 | tf_op jit(solution)/shard_map/all_to_all | solution.py:251
  126.7 3.0 %copy-start.9 = (s32[1,32,4]{1,2,0:T(4,128)S(1)}, s32[1,32,4]{1,2,0:T(4,128)}, u32[]{:S(2)}) copy-start(s32[1,32,4]{1,2,0:T(4,128)} %param.12) | copy-start | bytes 1540
  127.7 2.0 %copy-start.1 = (bf16[1024,2048]{1,0:T(8,128)(2,1)}, bf16[1024,2048]{1,0:T(8,128)(2,1)S(1)}, u32[]{:S(2)}) copy-start(bf16[1024,2048]{1,0:T(8,128)(2,1)S(1)} %unpack.1.take_ref) | copy-start | bytes 12582916
  140.8 2.2 %copy-start.2 = (bf16[1024,2048]{1,0:T(8,128)(2,1)S(1)}, bf16[1024,2048]{1,0:T(8,128)(2,1)}, u32[]{:S(2)}) copy-start(bf16[1024,2048]{1,0:T(8,128)(2,1)} %copy-done.1) | copy-start | bytes 12582916
  143.0 10.2 %copy-start.10 = (s32[32,1,4]{0,2,1:T(4,128)S(1)}, s32[32,1,4]{0,2,1:T(4,128)}, u32[]{:S(2)}) copy-start(s32[32,1,4]{0,2,1:T(4,128)} %param.13) | copy-start | bytes 1540
  145.1 16.9 %all-to-all-start.4 = ((bf16[32,4,128]{2,1,0:T(4,128)(2,1)}), bf16[32,4,128]{2,1,0:T(4,128)(2,1)S(1)}, u32[]{:S(2)}, u32[]{:S(2)}) async-start(bf16[32,4,128]{2,1,0:T(4,128)(2,1)} %bitcast.8), calls=%async_computation.4 | async-start | bytes 65536 | tf_op jit(solution)/shard_map/all_to_all | solution.py:251

commit v3 on v2

--- a/solution.py
+++ b/solution.py
@@ -11,7 +11,9 @@
 CAP = 4
 QUAD = 4
 VMEM = pl.BlockSpec(memory_space=pltpu.VMEM)
+HBM = pl.BlockSpec(memory_space=pltpu.HBM)
 LIMIT = 20 * 1024 * 1024
+WIDE = 60 * 1024 * 1024
 BF16 = jnp.bfloat16
 F32 = jnp.float32
 
@@ -105,13 +107,18 @@
     )
     far_up, far_down = shift(sent[1], 3, groups), shift(sent[2], -3, groups)
     near_up, near_down = shift(sent[0], 1, groups), shift(sent[3], -1, groups)
-    came = [far_up, far_down, near_up, near_down]
-    after, *came = lax.optimization_barrier((after, *came))
-    return after, [mine.reshape(rows, columns), *came]
-
-
-def pack_kernel(labels_ref, tokens_ref, slots_ref, packed_ref):
+    after, far_up, far_down = lax.optimization_barrier((after, far_up, far_down))
+    return after, [mine.reshape(rows, columns), far_up, far_down, near_up, near_down]
+
+
+def pack_kernel(labels_hbm, tokens_hbm, slots_ref, packed_hbm, labels_ref, tokens_ref, parts, sems):
     rows = tokens_ref.shape[0]
+    count, block = parts.shape[0], parts.shape[1]
+    labels_in = pltpu.make_async_copy(labels_hbm, labels_ref, sems.at[count])
+    tokens_in = pltpu.make_async_copy(tokens_hbm, tokens_ref, sems.at[count + 1])
+    labels_in.start()
+    tokens_in.start()
+    labels_in.wait()
     labels = labels_ref[...]
     column = jnp.transpose(jnp.broadcast_to(labels, (8, rows)))[:, 0:1]
     earlier = lax.broadcasted_iota(jnp.int32, (rows, rows), 0) < lax.broadcasted_iota(
@@ -120,64 +127,90 @@
     same = jnp.where((column == labels) & earlier, 1, 0)
     slots = labels * CAP + jnp.sum(same, axis=0, keepdims=True)
     slots_ref[...] = slots
+    tokens_in.wait()
     tokens = tokens_ref[...]
-    block = 256
-
-    @pl.loop(0, packed_ref.shape[0] // block)
-    def _(i):
-        first = pl.multiple_of(i * block, block)
-        place = lax.broadcasted_iota(jnp.int32, (block, rows), 0) + first
+    out = []
+    for i in range(count):
+        place = lax.broadcasted_iota(jnp.int32, (block, rows), 0) + i * block
         chosen = jnp.where(place == slots, 1.0, 0.0).astype(BF16)
-        packed_ref[pl.ds(first, block), :] = jnp.dot(
-            chosen, tokens, preferred_element_type=F32
-        ).astype(BF16)
+        parts[i] = jnp.dot(chosen, tokens, preferred_element_type=F32).astype(BF16)
+        out.append(
+            pltpu.make_async_copy(
+                parts.at[i], packed_hbm.at[pl.ds(i * block, block), :], sems.at[i]
+            )
+        )
+        out[-1].start()
+    for copy in out:
+        copy.wait()
 
 
 def pack(labels, tokens):
     rows, features = tokens.shape
     slots = ADAPTER_COUNT * CAP
-    return call(
+    block = 256
+    count = slots // block
+    return pl.pallas_call(
         pack_kernel,
-        [
+        out_shape=[
             jax.ShapeDtypeStruct((1, rows), jnp.int32),
             jax.ShapeDtypeStruct((slots, features), BF16),
         ],
-        (labels, tokens),
-        2 * slots * rows * features,
+        in_specs=[HBM, HBM],
+        out_specs=[VMEM, HBM],
+        scratch_shapes=[
+            pltpu.VMEM((1, rows), jnp.int32),
+            pltpu.VMEM((rows, features), BF16),
+            pltpu.VMEM((count, block, features), BF16),
+            pltpu.SemaphoreType.DMA((count + 2,)),
+        ],
+        compiler_params=pltpu.CompilerParams(vmem_limit_bytes=WIDE),
+        cost_estimate=pl.CostEstimate(
+            flops=2 * slots * rows * features,
+            bytes_accessed=2 * (rows + slots) * features,
+            transcendentals=0,
+        ),
         name="pack",
-    )
+    )(labels, tokens)
 
 
 def down_kernel(rows_ref, weight_ref, out_ref):
-    sources, slots, features = rows_ref.shape
+    sources, tile, features = rows_ref.shape
     rank = weight_ref.shape[1]
-    tile = QUAD * CAP
     owner = lax.broadcasted_iota(jnp.int32, (1, tile, 1), 1) // CAP
-    for quad in range(slots // tile):
-        rows = rows_ref[:, quad * tile : (quad + 1) * tile, :].reshape(sources * tile, features)
-        weight = weight_ref[quad * QUAD : (quad + 1) * QUAD].reshape(QUAD * rank, features)
-        product = lax.dot_general(
-            rows, weight, (((1,), (1,)), ((), ())), preferred_element_type=F32
-        ).reshape(sources, tile, QUAD * rank)
-        lowered = jnp.zeros((sources, tile, rank), F32)
-        for k in range(QUAD):
-            lowered = jnp.where(owner == k, product[:, :, k * rank : (k + 1) * rank], lowered)
-        lowered = lowered.reshape(sources // 2, 2, tile, rank)
-        out_ref[:, quad * tile : (quad + 1) * tile, :] = jnp.concatenate(
-            [lowered[:, 0], lowered[:, 1]], axis=-1
-        ).astype(BF16)
+    product = lax.dot_general(
+        rows_ref[...].reshape(sources * tile, features),
+        weight_ref[...].reshape(QUAD * rank, features),
+        (((1,), (1,)), ((), ())),
+        preferred_element_type=F32,
+    ).reshape(sources, tile, QUAD * rank)
+    lowered = jnp.zeros((sources, tile, rank), F32)
+    for k in range(QUAD):
+        lowered = jnp.where(owner == k, product[:, :, k * rank : (k + 1) * rank], lowered)
+    lowered = lowered.reshape(sources // 2, 2, tile, rank)
+    out_ref[...] = jnp.concatenate([lowered[:, 0], lowered[:, 1]], axis=-1).astype(BF16)
 
 
 def lower(received, weight):
     sources, slots, features = received.shape
     rank = weight.shape[1]
-    return call(
+    tile = QUAD * CAP
+    return pl.pallas_call(
         down_kernel,
-        jax.ShapeDtypeStruct((sources // 2, slots, 2 * rank), BF16),
-        (received, weight),
-        2 * sources * slots * features * rank * QUAD,
+        grid=(slots // tile,),
+        in_specs=[
+            pl.BlockSpec((sources, tile, features), lambda i: (0, i, 0)),
+            pl.BlockSpec((QUAD, rank, features), lambda i: (i, 0, 0)),
+        ],
+        out_specs=pl.BlockSpec((sources // 2, tile, 2 * rank), lambda i: (0, i, 0)),
+        out_shape=jax.ShapeDtypeStruct((sources // 2, slots, 2 * rank), BF16),
+        compiler_params=pltpu.CompilerParams(vmem_limit_bytes=WIDE),
+        cost_estimate=pl.CostEstimate(
+            flops=2 * sources * slots * features * rank * QUAD,
+            bytes_accessed=2 * (sources * slots * features + slots // CAP * rank * features),
+            transcendentals=0,
+        ),
         name="down",
-    )
+    )(received, weight)
 
 
 def up_kernel(lowered_ref, weight_ref, out_ref):
@@ -214,24 +247,19 @@
     )
 
 
-def unpack_kernel(slots_ref, out_ref):
-    rows, places = out_ref.shape
-    slots = slots_ref[...]
-    column = jnp.transpose(jnp.broadcast_to(slots, (8, rows)))[:, 0:1]
+def finish_kernel(slots_ref, returned_ref, base_ref, accepted_ref, out_ref, chosen_ref):
+    rows = out_ref.shape[0]
+    places = returned_ref.shape[0]
+    column = jnp.transpose(jnp.broadcast_to(slots_ref[...], (8, rows)))[:, 0:1]
     block = 256
+    total = base_ref[...]
     for first in range(0, places, block):
         place = lax.broadcasted_iota(jnp.int32, (rows, block), 1) + first
-        out_ref[:, first : first + block] = jnp.where(place == column, 1.0, 0.0).astype(BF16)
-
-
-def finish_kernel(take_ref, returned_ref, accepted_ref, *rest):
-    base_refs, (out_ref, chosen_ref) = rest[:-2], rest[-2:]
-    rows = out_ref.shape[0]
-    update = jnp.dot(take_ref[...], returned_ref[...], preferred_element_type=F32)
-    base = base_refs[0][...].astype(F32)
-    for base_ref in base_refs[1:]:
-        base += base_ref[...].astype(F32)
-    key_value = (base + update).astype(BF16)
+        take = jnp.where(place == column, 1.0, 0.0).astype(BF16)
+        total += jnp.dot(
+            take, returned_ref[first : first + block], preferred_element_type=F32
+        )
+    key_value = total.astype(BF16)
     out_ref[...] = key_value
     count = chosen_ref.shape[0]
     place = lax.broadcasted_iota(jnp.int32, (count, rows), 1)
@@ -295,9 +323,7 @@
     lowered = sum_over_tensor(partial_rank, core, pairs, chips)
     update = raise_rank(lowered, adapter_up_weight)
     returned = exchange(update.reshape(owners, here, columns), "adapter")
-    take = call(
-        unpack_kernel, jax.ShapeDtypeStruct((rows, owners * here), BF16), (slots,), 0, name="unpack"
-    )
+    base = sum(part.astype(F32) for part in base)
     accepted = accepted_branch_rows.reshape(1, -1)
     count = accepted.shape[1]
     key_value, chosen = call(
@@ -306,7 +332,7 @@
             jax.ShapeDtypeStruct((rows, columns), BF16),
             jax.ShapeDtypeStruct((count, columns), BF16),
         ],
-        (take, returned.reshape(owners * here, columns), accepted, *base),
+        (slots, returned.reshape(owners * here, columns), base, accepted),
         2 * rows * owners * here * columns,
         name="finish",
     )

time: 164 us -> 156 us (0.951)
  local copies, waits for them, and re-layouts: 8.97 us -> 0.44 us
  blocking collectives: 31.3 us -> 28.4 us
  waiting for transfers between devices: 44.7 us -> 47.2 us
  Pallas kernels: 17.2 us -> 19.5 us
    ppermute x6, waiting for transfers between devices: 23 us -> 34.5 us  [shift(): lax.ppermute(array, 'tensor', [(i, (i + step) % groups) for i in range(gr...]
    pallas_call x0 -> x2, Pallas kernels: none -> 9.73 us  [the longest x1 4.96 us: pack(): pl.pallas_call(pack_kernel, out_shape=[jax.ShapeDtypeStruct((1, rows), jn...]
    all_to_all x3, waiting for transfers between devices: 19.5 us -> 10.5 us  [exchange(): lax.all_to_all(array, axis, split_axis=0, concat_axis=0, tiled=True, axis...]
    unnamed x24 -> x14, local copies, waits for them, and re-layouts: 8.75 us -> 0.21 us
    pallas_call x11 -> x8, Pallas kernels: 17.2 us -> 9.8 us  [call(): pl.pallas_call(kernel, out_shape=out_shape, in_specs=[VMEM] * len(operand...]
    all_to_all x2, blocking collectives: 23 us -> 21.1 us  [exchange(): lax.all_to_all(array, axis, split_axis=0, concat_axis=0, tiled=True, axis...]
  transfers between devices with their start and end apart: 11 -> 11, of which waited for: 9 -> 9; matrix products, arithmetic and copies ran while one was open for 0% -> 0% of each run, Pallas kernels for 4% -> 3%
where the time goes in v3:
time: 156 us; the launch traced here: 155 us
  starting transfers between devices  58.3 us (37%)
  waiting for transfers between devices  47.2 us (30%)
  blocking collectives  28.4 us (18%)
  Pallas kernels  19.5 us (12%)
    ppermute x6, waiting for transfers between devices, shift(): lax.ppermute(array, 'tensor', [(i, (i + step) % groups) for i in range(gr...  34.5 us
    all_to_all x3, starting transfers between devices, exchange(): lax.all_to_all(array, axis, split_axis=0, concat_axis=0, tiled=True, axis...  31.6 us
    ppermute x6, starting transfers between devices, shift(): lax.ppermute(array, 'tensor', [(i, (i + step) % groups) for i in range(gr...  21.9 us
    all_to_all x2, blocking collectives, exchange(): lax.all_to_all(array, axis, split_axis=0, concat_axis=0, tiled=True, axis...  21.1 us
    all_to_all x3, waiting for transfers between devices, exchange(): lax.all_to_all(array, axis, split_axis=0, concat_axis=0, tiled=True, axis...  10.5 us
    pallas_call x8, Pallas kernels, call(): pl.pallas_call(kernel, out_shape=out_shape, in_specs=[VMEM] * len(operand...  9.8 us
    pallas_call x1, Pallas kernels, pack(): pl.pallas_call(pack_kernel, out_shape=[jax.ShapeDtypeStruct((1, rows), jn...  4.96 us
    pallas_call x1, Pallas kernels, lower(): pl.pallas_call(down_kernel, grid=(slots // tile,), in_specs=[pl.BlockSpec...  4.77 us
  transfers between devices with their start and end apart: 11, of which 9 were waited for; matrix products, arithmetic and copies ran while one was open for 0% of the time, Pallas kernels for 3%

profile of v3, /device:TPU:1, one launch (start us, length us, event | category | flops | bytes accessed | tf_op | source)
XLA Modules:
  0.0 155.0 jit_solution(10495968351466963564)
XLA Ops:
  0.6 5.0 %pack.1 = (s32[1,1024]{1,0:T(1,128)}, bf16[2048,512]{1,0:T(8,128)(2,1)}) custom-call(s32[1,1024]{1,0:T(1,128)} %bitcast.20, bf16[1024,512]{1,0:T(8,128)(2,1)} %tokens_ref.3), custom_call_target="tpu_custom_call" | custom-call | flops 2147483648 | bytes 3145728 | tf_op jit(solution)/shard_map/pack/pallas_call | solution.py:152
  5.6 0.0 copy-start
  5.6 0.0 copy-start.1
  5.6 14.1 %all-to-all-start = ((bf16[32,64,512]{2,1,0:T(8,128)(2,1)}), bf16[32,64,512]{2,1,0:T(8,128)(2,1)}, u32[]{:S(2)}, u32[]{:S(2)}) async-start(bf16[32,64,512]{2,1,0:T(8,128)(2,1)} %bitcast.17), calls=%async_computation | async-start | bytes 4194304 | tf_op jit(solution)/shard_map/all_to_all | solution.py:279
  19.8 0.0 copy-done
  19.8 0.0 copy-done.1
  19.8 1.0 base.4
  20.8 1.6 %base.5 = bf16[5,1024,128]{2,1,0:T(8,128)(2,1)S(1)} custom-call(bf16[1024,512]{1,0:T(8,128)(2,1)S(1)} %copy-done.1, bf16[512,2048]{1,0:T(8,128)(2,1)S(1)} %copy-done), custom_call_target="tpu_custom_call" | custom-call | flops 671088640 | bytes 4456448 | tf_op jit(solution)/shard_map/base/pallas_call | solution.py:24
  22.3 2.9 %collective-permute-start = (bf16[5,1024,128]{2,1,0:T(8,128)(2,1)S(1)}, bf16[5,1024,128]{2,1,0:T(8,128)(2,1)S(1)}, u32[]{:S(2)}, u32[]{:S(2)}) collective-permute-start(bf16[5,1024,128]{2,1,0:T(8,128)(2,1)S(1)} %base.5), channel_id=1, source_target_pairs={{0,1},{1,0},{2,3},{3,2},{4,5},{5,4},{6,7},{7,6},{8,9},{9,8},{10,11... | collective-permute-start | bytes 3932168 | tf_op jit(solution)/shard_map/ppermute | solution.py:95
  25.2 1.9 %collective-permute-start.1 = (bf16[3,1024,128]{2,1,0:T(8,128)(2,1)S(1)}, bf16[3,1024,128]{2,1,0:T(8,128)(2,1)S(1)}, u32[]{:S(2)}, u32[]{:S(2)}) collective-permute-start(bf16[3,1024,128]{2,1,0:T(8,128)(2,1)S(1)} %base.4), channel_id=1, source_target_pairs={{0,1},{1,0},{2,3},{3,2},{4,5},{5,4},{6,7},{7,6},{8,9},{9,8},{10,11... | collective-permute-start | bytes 2359304 | tf_op jit(solution)/shard_map/ppermute | solution.py:92
  27.2 2.3 %collective-permute-done.1.rest_0_ = bf16[3,1024,128]{2,1,0:T(8,128)(2,1)S(1)} collective-permute-done((bf16[3,1024,128]{2,1,0:T(8,128)(2,1)S(1)}, bf16[3,1024,128]{2,1,0:T(8,128)(2,1)S(1)}, u32[]{:S(2)}, u32[]{:S(2)}) %collective-permute-start.1) | collective-permute-done | bytes 786464 | tf_op jit(solution)/shard_map/ppermute | solution.py:92
  29.4 1.0 base.7
  30.4 3.2 %collective-permute-start.2 = (bf16[3,512,128]{2,1,0:T(8,128)(2,1)S(1)}, bf16[3,512,128]{2,1,0:T(8,128)(2,1)S(1)}, u32[]{:S(2)}, u32[]{:S(2)}) collective-permute-start(bf16[3,512,128]{2,1,0:T(8,128)(2,1)S(1)} %get-tuple-element.26), channel_id=1, source_target_pairs={{0,2},{1,3},{2,4},{3,5},{4,6},{5,7},{6,8},{7,9},{8,10},{9,11},{10,... | collective-permute-start | bytes 1179656 | tf_op jit(solution)/shard_map/ppermute | solution.py:83
  33.6 3.8 %collective-permute-start.3 = (bf16[3,512,128]{2,1,0:T(8,128)(2,1)S(1)}, bf16[3,512,128]{2,1,0:T(8,128)(2,1)S(1)}, u32[]{:S(2)}, u32[]{:S(2)}) collective-permute-start(bf16[3,512,128]{2,1,0:T(8,128)(2,1)S(1)} %get-tuple-element.27), channel_id=1, source_target_pairs={{0,14},{1,15},{2,0},{3,1},{4,2},{5,3},{6,4},{7,5},{8,6},{9,7},{10,... | collective-permute-start | bytes 1179656 | tf_op jit(solution)/shard_map/ppermute | solution.py:83
  37.4 0.0 collective-permute-done.rest_0_
  37.5 1.6 %base.6 = (bf16[1,1024,128]{2,1,0:T(8,128)(2,1)S(1)}, bf16[4,1024,128]{2,1,0:T(8,128)(2,1)S(1)}) custom-call(bf16[1024,512]{1,0:T(8,128)(2,1)S(1)} %copy-done.1, bf16[512,2048]{1,0:T(8,128)(2,1)S(1)} %copy-done, bf16[5,1024,128]{2,1,0:T(8,128)(2,1)S(1)} %collective-permute-done.rest_0_), custom_call_target="tpu_custom_call" | custom-call | flops 671088640 | bytes 5767168 | tf_op jit(solution)/shard_map/base/pallas_call | solution.py:24
  39.0 5.9 %collective-permute-done.2.up_ref = bf16[3,512,128]{2,1,0:T(8,128)(2,1)S(1)} collective-permute-done((bf16[3,512,128]{2,1,0:T(8,128)(2,1)S(1)}, bf16[3,512,128]{2,1,0:T(8,128)(2,1)S(1)}, u32[]{:S(2)}, u32[]{:S(2)}) %collective-permute-start.2) | collective-permute-done | bytes 393248 | tf_op jit(solution)/shard_map/ppermute | solution.py:83
  45.0 0.9 collective-permute-done.3.down_ref
  45.9 0.2 combine.1
  46.1 7.6 %collective-permute-start.4 = (bf16[1024,128]{1,0:T(8,128)(2,1)S(1)}, bf16[1024,128]{1,0:T(8,128)(2,1)S(1)}, u32[]{:S(2)}, u32[]{:S(2)}) collective-permute-start(bf16[1024,128]{1,0:T(8,128)(2,1)S(1)} %get-tuple-element.28), channel_id=1, source_target_pairs={{0,6},{1,7},{2,8},{3,9},{4,10},{5,11},{6,12},{7,13},{8,14},{9,15},... | collective-permute-start | bytes 786440 | tf_op jit(solution)/shard_map/ppermute | solution.py:83
  53.7 1.9 %collective-permute-start.5 = (bf16[1024,128]{1,0:T(8,128)(2,1)S(1)}, bf16[1024,128]{1,0:T(8,128)(2,1)S(1)}, u32[]{:S(2)}, u32[]{:S(2)}) collective-permute-start(bf16[1024,128]{1,0:T(8,128)(2,1)S(1)} %get-tuple-element.29), channel_id=1, source_target_pairs={{0,10},{1,11},{2,12},{3,13},{4,14},{5,15},{6,0},{7,1},{8,2},{9,3},... | collective-permute-start | bytes 786440 | tf_op jit(solution)/shard_map/ppermute | solution.py:83
  55.7 14.6 %collective-permute-done.4 = bf16[1024,128]{1,0:T(8,128)(2,1)S(1)} collective-permute-done((bf16[1024,128]{1,0:T(8,128)(2,1)S(1)}, bf16[1024,128]{1,0:T(8,128)(2,1)S(1)}, u32[]{:S(2)}, u32[]{:S(2)}) %collective-permute-start.4) | collective-permute-done | bytes 262176 | tf_op jit(solution)/shard_map/ppermute | solution.py:83
  70.3 6.4 %collective-permute-done.5 = bf16[1024,128]{1,0:T(8,128)(2,1)S(1)} collective-permute-done((bf16[1024,128]{1,0:T(8,128)(2,1)S(1)}, bf16[1024,128]{1,0:T(8,128)(2,1)S(1)}, u32[]{:S(2)}, u32[]{:S(2)}) %collective-permute-start.5) | collective-permute-done | bytes 262176 | tf_op jit(solution)/shard_map/ppermute | solution.py:83
  76.7 0.0 all-to-all-done.rows_ref
  76.7 4.8 %down.1 = bf16[16,64,128]{2,1,0:T(8,128)(2,1)} custom-call(bf16[32,64,512]{2,1,0:T(8,128)(2,1)} %all-to-all-done.rows_ref, bf16[16,64,512]{2,1,0:T(8,128)(2,1)} %bitcast.19), custom_call_target="tpu_custom_call" | custom-call | flops 536870912 | bytes 3145728 | tf_op jit(solution)/shard_map/down/pallas_call | solution.py:197
  81.5 0.0 copy-start.2
  81.5 2.8 %all-gather = bf16[32,64,128]{2,1,0:T(8,128)(2,1)S(1)} all-gather(bf16[16,64,128]{2,1,0:T(8,128)(2,1)} %down.1), channel_id=2, replica_groups={{0,1},{2,3},{4,5},{6,7},{8,9},{10,11},{12,13},{14,15},{16,17},{18,19},{..., dimensions={0}, use_global_device_ids=true | all-gather | bytes 786432 | tf_op jit(solution)/shard_map/all_gather | solution.py:285
  84.3 0.0 copy-start.4
  84.4 10.8 %all_to_all.25 = bf16[8,64,128]{2,1,0:T(8,128)(2,1)S(1)} all-to-all(bf16[8,64,128]{2,1,0:T(8,128)(2,1)S(1)} %fusion.4), channel_id=1, replica_groups={{0,2,4,6,8,10,12,14},{1,3,5,7,9,11,13,15},{16,18,20,22,24,26,28,30},{17..., dimensions={0} | all-to-all | bytes 262144 | tf_op jit(solution)/shard_map/all_to_all | solution.py:279
  95.2 10.3 %all_to_all.26 = bf16[8,64,128]{2,1,0:T(8,128)(2,1)S(1)} all-to-all(bf16[8,64,128]{2,1,0:T(8,128)(2,1)S(1)} %broadcast_in_dim.2), channel_id=1, replica_groups={{0,2,4,6,8,10,12,14},{1,3,5,7,9,11,13,15},{16,18,20,22,24,26,28,30},{17..., dimensions={0} | all-to-all | bytes 262144 | tf_op jit(solution)/shard_map/all_to_all | solution.py:279
  105.6 0.0 copy-start.3
  105.6 4.5 %all_gather.11.lowered_ref = bf16[16,64,128]{2,1,0:T(8,128)(2,1)S(1)} all-gather(bf16[8,64,128]{2,1,0:T(8,128)(2,1)S(1)} %all_to_all.26), channel_id=1, replica_groups={{0,1},{2,3},{4,5},{6,7},{8,9},{10,11},{12,13},{14,15},{16,17},{18,19},{..., dimensions={0}, use_global_device_ids=true | all-gather | bytes 393216 | tf_op jit(solution)/shard_map/all_gather | solution.py:294
  110.1 0.0 copy-done.2
  110.1 1.3 up.1
  111.4 9.4 %all-to-all-start.3 = ((bf16[32,64,128]{2,1,0:T(8,128)(2,1)}), bf16[32,64,128]{2,1,0:T(8,128)(2,1)S(1)}, u32[]{:S(2)}, u32[]{:S(2)}) async-start(bf16[32,64,128]{2,1,0:T(8,128)(2,1)} %bitcast.5), calls=%async_computation.3 | async-start | bytes 1048576 | tf_op jit(solution)/shard_map/all_to_all | solution.py:279
  120.7 0.0 copy-start.5
  120.7 2.0 %collective-permute-start.7 = (bf16[1024,128]{1,0:T(8,128)(2,1)S(1)}, bf16[1024,128]{1,0:T(8,128)(2,1)S(1)}, u32[]{:S(2)}, u32[]{:S(2)}) collective-permute-start(bf16[1024,128]{1,0:T(8,128)(2,1)S(1)} %get-tuple-element.35), channel_id=1, source_target_pairs={{0,14},{1,15},{2,0},{3,1},{4,2},{5,3},{6,4},{7,5},{8,6},{9,7},{10,... | collective-permute-start | bytes 786440 | tf_op jit(solution)/shard_map/ppermute | solution.py:83
  122.8 3.3 %collective-permute-start.6 = (bf16[1024,128]{1,0:T(8,128)(2,1)S(1)}, bf16[1024,128]{1,0:T(8,128)(2,1)S(1)}, u32[]{:S(2)}, u32[]{:S(2)}) collective-permute-start(bf16[1024,128]{1,0:T(8,128)(2,1)S(1)} %get-tuple-element.34), channel_id=1, source_target_pairs={{0,2},{1,3},{2,4},{3,5},{4,6},{5,7},{6,8},{7,9},{8,10},{9,11},{10,... | collective-permute-start | bytes 786440 | tf_op jit(solution)/shard_map/ppermute | solution.py:83
  126.0 0.0 copy-done.4
  126.1 0.1 copy.13
  126.1 0.1 reshape.40.accepted_ref
  126.2 3.6 %collective-permute-done.7 = bf16[1024,128]{1,0:T(8,128)(2,1)S(1)} collective-permute-done((bf16[1024,128]{1,0:T(8,128)(2,1)S(1)}, bf16[1024,128]{1,0:T(8,128)(2,1)S(1)}, u32[]{:S(2)}, u32[]{:S(2)}) %collective-permute-start.7) | collective-permute-done | bytes 262176 | tf_op jit(solution)/shard_map/ppermute | solution.py:83
  129.9 2.9 %collective-permute-done.6 = bf16[1024,128]{1,0:T(8,128)(2,1)S(1)} collective-permute-done((bf16[1024,128]{1,0:T(8,128)(2,1)S(1)}, bf16[1024,128]{1,0:T(8,128)(2,1)S(1)}, u32[]{:S(2)}, u32[]{:S(2)}) %collective-permute-start.6) | collective-permute-done | bytes 262176 | tf_op jit(solution)/shard_map/ppermute | solution.py:83
  132.8 0.2 fusion.2.base_ref
  132.9 1.9 %all-to-all-done.3 = bf16[32,64,128]{2,1,0:T(8,128)(2,1)S(1)} async-done(((bf16[32,64,128]{2,1,0:T(8,128)(2,1)}), bf16[32,64,128]{2,1,0:T(8,128)(2,1)S(1)}, u32[]{:S(2)}, u32[]{:S(2)}) %all-to-all-start.3) | async-done | bytes 524320 | tf_op jit(solution)/shard_map/all_to_all | solution.py:279
  134.9 0.0 copy-done.3
  134.9 2.4 %finish.1 = (bf16[1024,128]{1,0:T(8,128)(2,1)}, bf16[128,128]{1,0:T(8,128)(2,1)}) custom-call(s32[1,1024]{1,0:T(1,128)S(1)} %copy-done.3, bf16[2048,128]{1,0:T(8,128)(2,1)S(1)} %bitcast.15, f32[1024,128]{1,0:T(8,128)S(1)} %fusion.2.base_ref, s32[1,128]{1,0:T(1,128)S(1)} %reshape.40.accepted_ref), custom_call_target="tpu_custom_call" | custom-call | flops 536870912 | bytes 1348096 | tf_op jit(solution)/shard_map/finish/pallas_call | solution.py:24
  137.3 8.1 %all-to-all-start.4 = ((bf16[32,4,128]{2,1,0:T(4,128)(2,1)}), bf16[32,4,128]{2,1,0:T(4,128)(2,1)S(1)}, u32[]{:S(2)}, u32[]{:S(2)}) async-start(bf16[32,4,128]{2,1,0:T(4,128)(2,1)} %bitcast.8), calls=%async_computation.4 | async-start | bytes 65536 | tf_op jit(solution)/shard_map/all_to_all | solution.py:279
  145.5 0.0 copy-done.5
  145.5 0.1 copy.14
  145.6 0.1 reshape.41.targets_ref
  145.7 8.6 %all-to-all-done.4 = bf16[32,4,128]{2,1,0:T(4,128)(2,1)S(1)} async-done(((bf16[32,4,128]{2,1,0:T(4,128)(2,1)}), bf16[32,4,128]{2,1,0:T(4,128)(2,1)S(1)}, u32[]{:S(2)}, u32[]{:S(2)}) %all-to-all-start.4) | async-done | bytes 32800 | tf_op jit(solution)/shard_map/all_to_all | solution.py:279
  154.2 0.8 cache.1
  (4 shorter events, 0.1 us)
Async XLA Ops:
  5.6 14.2 %copy-start = (bf16[512,2048]{1,0:T(8,128)(2,1)S(1)}, bf16[512,2048]{1,0:T(8,128)(2,1)}, u32[]{:S(2)}) copy-start(bf16[512,2048]{1,0:T(8,128)(2,1)} %weight_ref.8) | copy-start | bytes 6291460
  5.6 14.2 %copy-start.1 = (bf16[1024,512]{1,0:T(8,128)(2,1)S(1)}, bf16[1024,512]{1,0:T(8,128)(2,1)}, u32[]{:S(2)}) copy-start(bf16[1024,512]{1,0:T(8,128)(2,1)} %tokens_ref.3) | copy-start | bytes 3145732
  5.6 71.1 %all-to-all-start = ((bf16[32,64,512]{2,1,0:T(8,128)(2,1)}), bf16[32,64,512]{2,1,0:T(8,128)(2,1)}, u32[]{:S(2)}, u32[]{:S(2)}) async-start(bf16[32,64,512]{2,1,0:T(8,128)(2,1)} %bitcast.17), calls=%async_computation | async-start | bytes 4194304 | tf_op jit(solution)/shard_map/all_to_all | solution.py:279
  22.3 15.1 %collective-permute-start = (bf16[5,1024,128]{2,1,0:T(8,128)(2,1)S(1)}, bf16[5,1024,128]{2,1,0:T(8,128)(2,1)S(1)}, u32[]{:S(2)}, u32[]{:S(2)}) collective-permute-start(bf16[5,1024,128]{2,1,0:T(8,128)(2,1)S(1)} %base.5), channel_id=1, source_target_pairs={{0,1},{1,0},{2,3},{3,2},{4,5},{5,4},{6,7},{7,6},{8,9},{9,8},{10,11... | collective-permute-start | bytes 3932168 | tf_op jit(solution)/shard_map/ppermute | solution.py:95
  25.2 4.2 %collective-permute-start.1 = (bf16[3,1024,128]{2,1,0:T(8,128)(2,1)S(1)}, bf16[3,1024,128]{2,1,0:T(8,128)(2,1)S(1)}, u32[]{:S(2)}, u32[]{:S(2)}) collective-permute-start(bf16[3,1024,128]{2,1,0:T(8,128)(2,1)S(1)} %base.4), channel_id=1, source_target_pairs={{0,1},{1,0},{2,3},{3,2},{4,5},{5,4},{6,7},{7,6},{8,9},{9,8},{10,11... | collective-permute-start | bytes 2359304 | tf_op jit(solution)/shard_map/ppermute | solution.py:92
  30.4 14.5 %collective-permute-start.2 = (bf16[3,512,128]{2,1,0:T(8,128)(2,1)S(1)}, bf16[3,512,128]{2,1,0:T(8,128)(2,1)S(1)}, u32[]{:S(2)}, u32[]{:S(2)}) collective-permute-start(bf16[3,512,128]{2,1,0:T(8,128)(2,1)S(1)} %get-tuple-element.26), channel_id=1, source_target_pairs={{0,2},{1,3},{2,4},{3,5},{4,6},{5,7},{6,8},{7,9},{8,10},{9,11},{10,... | collective-permute-start | bytes 1179656 | tf_op jit(solution)/shard_map/ppermute | solution.py:83
  33.6 12.3 %collective-permute-start.3 = (bf16[3,512,128]{2,1,0:T(8,128)(2,1)S(1)}, bf16[3,512,128]{2,1,0:T(8,128)(2,1)S(1)}, u32[]{:S(2)}, u32[]{:S(2)}) collective-permute-start(bf16[3,512,128]{2,1,0:T(8,128)(2,1)S(1)} %get-tuple-element.27), channel_id=1, source_target_pairs={{0,14},{1,15},{2,0},{3,1},{4,2},{5,3},{6,4},{7,5},{8,6},{9,7},{10,... | collective-permute-start | bytes 1179656 | tf_op jit(solution)/shard_map/ppermute | solution.py:83
  46.1 24.2 %collective-permute-start.4 = (bf16[1024,128]{1,0:T(8,128)(2,1)S(1)}, bf16[1024,128]{1,0:T(8,128)(2,1)S(1)}, u32[]{:S(2)}, u32[]{:S(2)}) collective-permute-start(bf16[1024,128]{1,0:T(8,128)(2,1)S(1)} %get-tuple-element.28), channel_id=1, source_target_pairs={{0,6},{1,7},{2,8},{3,9},{4,10},{5,11},{6,12},{7,13},{8,14},{9,15},... | collective-permute-start | bytes 786440 | tf_op jit(solution)/shard_map/ppermute | solution.py:83
  53.7 23.0 %collective-permute-start.5 = (bf16[1024,128]{1,0:T(8,128)(2,1)S(1)}, bf16[1024,128]{1,0:T(8,128)(2,1)S(1)}, u32[]{:S(2)}, u32[]{:S(2)}) collective-permute-start(bf16[1024,128]{1,0:T(8,128)(2,1)S(1)} %get-tuple-element.29), channel_id=1, source_target_pairs={{0,10},{1,11},{2,12},{3,13},{4,14},{5,15},{6,0},{7,1},{8,2},{9,3},... | collective-permute-start | bytes 786440 | tf_op jit(solution)/shard_map/ppermute | solution.py:83
  81.5 28.5 %copy-start.2 = (bf16[16,64,128]{2,1,0:T(8,128)(2,1)S(1)}, bf16[16,64,128]{2,1,0:T(8,128)(2,1)}, u32[]{:S(2)}) copy-start(bf16[16,64,128]{2,1,0:T(8,128)(2,1)} %weight_ref.9) | copy-start | bytes 786436
  84.3 41.7 %copy-start.4 = (s32[1,32,4]{1,2,0:T(4,128)S(1)}, s32[1,32,4]{1,2,0:T(4,128)}, u32[]{:S(2)}) copy-start(s32[1,32,4]{1,2,0:T(4,128)} %param.12) | copy-start | bytes 1540
  105.6 29.3 %copy-start.3 = (s32[1,1024]{1,0:T(1,128)S(1)}, s32[1,1024]{1,0:T(1,128)}, u32[]{:S(2)}) copy-start(s32[1,1024]{1,0:T(1,128)} %get-tuple-element.21.slots_ref) | copy-start | bytes 12292
  111.4 23.5 %all-to-all-start.3 = ((bf16[32,64,128]{2,1,0:T(8,128)(2,1)}), bf16[32,64,128]{2,1,0:T(8,128)(2,1)S(1)}, u32[]{:S(2)}, u32[]{:S(2)}) async-start(bf16[32,64,128]{2,1,0:T(8,128)(2,1)} %bitcast.5), calls=%async_computation.3 | async-start | bytes 1048576 | tf_op jit(solution)/shard_map/all_to_all | solution.py:279
  120.7 24.7 %copy-start.5 = (s32[32,1,4]{0,2,1:T(4,128)S(1)}, s32[32,1,4]{0,2,1:T(4,128)}, u32[]{:S(2)}) copy-start(s32[32,1,4]{0,2,1:T(4,128)} %param.13) | copy-start | bytes 1540
  120.7 9.1 %collective-permute-start.7 = (bf16[1024,128]{1,0:T(8,128)(2,1)S(1)}, bf16[1024,128]{1,0:T(8,128)(2,1)S(1)}, u32[]{:S(2)}, u32[]{:S(2)}) collective-permute-start(bf16[1024,128]{1,0:T(8,128)(2,1)S(1)} %get-tuple-element.35), channel_id=1, source_target_pairs={{0,14},{1,15},{2,0},{3,1},{4,2},{5,3},{6,4},{7,5},{8,6},{9,7},{10,... | collective-permute-start | bytes 786440 | tf_op jit(solution)/shard_map/ppermute | solution.py:83
  122.8 10.0 %collective-permute-start.6 = (bf16[1024,128]{1,0:T(8,128)(2,1)S(1)}, bf16[1024,128]{1,0:T(8,128)(2,1)S(1)}, u32[]{:S(2)}, u32[]{:S(2)}) collective-permute-start(bf16[1024,128]{1,0:T(8,128)(2,1)S(1)} %get-tuple-element.34), channel_id=1, source_target_pairs={{0,2},{1,3},{2,4},{3,5},{4,6},{5,7},{6,8},{7,9},{8,10},{9,11},{10,... | collective-permute-start | bytes 786440 | tf_op jit(solution)/shard_map/ppermute | solution.py:83
  137.3 16.9 %all-to-all-start.4 = ((bf16[32,4,128]{2,1,0:T(4,128)(2,1)}), bf16[32,4,128]{2,1,0:T(4,128)(2,1)S(1)}, u32[]{:S(2)}, u32[]{:S(2)}) async-start(bf16[32,4,128]{2,1,0:T(4,128)(2,1)} %bitcast.8), calls=%async_computation.4 | async-start | bytes 65536 | tf_op jit(solution)/shard_map/all_to_all | solution.py:279

commit v4 on v3

--- a/solution.py
+++ b/solution.py
@@ -12,7 +12,7 @@
 QUAD = 4
 VMEM = pl.BlockSpec(memory_space=pltpu.VMEM)
 HBM = pl.BlockSpec(memory_space=pltpu.HBM)
-LIMIT = 20 * 1024 * 1024
+LIMIT = 16 * 1024 * 1024
 WIDE = 60 * 1024 * 1024
 BF16 = jnp.bfloat16
 F32 = jnp.float32
@@ -64,18 +64,8 @@
     )
 
 
-def combine_kernel(own_ref, up_ref, down_ref, *outs):
-    rows = own_ref.shape[1]
-    half = rows // 2
-    up = up_ref[...].reshape(3 * half, -1)
-    down = down_ref[...].reshape(3 * half, -1)
-    own = own_ref[...].astype(F32)
-    outs[0][...] = (own[0] + up[:rows].astype(F32)).astype(BF16)
-    outs[1][:half] = (own[1, :half] + up[rows:].astype(F32)).astype(BF16)
-    outs[1][half:] = own_ref[1, half:]
-    outs[2][:half] = own_ref[2, :half]
-    outs[2][half:] = (own[2, half:] + down[:half].astype(F32)).astype(BF16)
-    outs[3][...] = (own[3] + down[half:].astype(F32)).astype(BF16)
+def add(own, came):
+    return (own.astype(F32) + came.astype(F32)).astype(BF16)
 
 
 def shift(array, by, groups):
@@ -87,28 +77,49 @@
     rows = tokens.shape[0]
     half = rows // 2
     swap = [(i, i ^ 1) for i in range(groups)]
-    far, near = (2, 4, 6), (0, 1, 3, 5, 7)
+    far, near = (4, 3, 5), (2, 6, 1, 7, 0)
     (far_away,) = products(far, True, tokens, weight, columns, [(3, rows)])
     far_other = lax.ppermute(far_away, "tensor", swap)
     tokens, far_away = lax.optimization_barrier((tokens, far_away))
     (near_away,) = products(near, True, tokens, weight, columns, [(5, rows)])
     near_other = lax.ppermute(near_away, "tensor", swap)
-    plus, minus = products(
-        far, False, tokens, weight, columns, [(3, half), (3, half)], far_other
-    )
-    up, down = shift(plus, 1, groups), shift(minus, -1, groups)
-    mine, own = products(near, False, tokens, weight, columns, [(1, rows), (4, rows)], near_other)
-    sent = call(
-        combine_kernel,
-        [jax.ShapeDtypeStruct((rows, columns), BF16)] * 4,
-        (own, up, down),
-        rows * columns * 4,
-        name="combine",
-    )
-    far_up, far_down = shift(sent[1], 3, groups), shift(sent[2], -3, groups)
-    near_up, near_down = shift(sent[0], 1, groups), shift(sent[3], -1, groups)
-    after, far_up, far_down = lax.optimization_barrier((after, far_up, far_down))
-    return after, [mine.reshape(rows, columns), far_up, far_down, near_up, near_down]
+    outs = [(1, half)] * 2 + [(2, half)] * 2
+    upper, lower_half, third, fifth = products(
+        far, False, tokens, weight, columns, outs, far_other
+    )
+    up, down = shift(upper[0], 1, groups), shift(lower_half[0], -1, groups)
+    outs = [(1, rows)] * 5
+    second, sixth, first, seventh, mine = products(
+        near, False, tokens, weight, columns, outs, near_other
+    )
+    third, fifth = call(
+        ring_kernel,
+        [jax.ShapeDtypeStruct((rows, columns), BF16)] * 2,
+        (third, fifth, up, down),
+        2 * rows * columns,
+        name="ring",
+    )
+    up, down = shift(third, 1, groups), shift(fifth, -1, groups)
+    up, down = shift(add(second[0], up), 1, groups), shift(add(sixth[0], down), -1, groups)
+    after, up, down = lax.optimization_barrier((after, up, down))
+    up, down = shift(add(first[0], up), 1, groups), shift(add(seventh[0], down), -1, groups)
+    return after, [mine[0], up, down]
+
+
+def ring_kernel(third_ref, fifth_ref, up_ref, down_ref, third_out, fifth_out):
+    half = up_ref.shape[0]
+    third_out[:half] = add(third_ref[0], up_ref[...])
+    third_out[half:] = third_ref[1]
+    fifth_out[:half] = fifth_ref[0]
+    fifth_out[half:] = add(fifth_ref[1], down_ref[...])
+
+
+def numbers(x):
+    return x.astype(F32).astype(BF16)
+
+
+def one_hot(mask):
+    return jnp.where(mask, jnp.ones((), BF16), jnp.zeros((), BF16))
 
 
 def pack_kernel(labels_hbm, tokens_hbm, slots_ref, packed_hbm, labels_ref, tokens_ref, parts, sems):
@@ -121,18 +132,26 @@
     labels_in.wait()
     labels = labels_ref[...]
     column = jnp.transpose(jnp.broadcast_to(labels, (8, rows)))[:, 0:1]
-    earlier = lax.broadcasted_iota(jnp.int32, (rows, rows), 0) < lax.broadcasted_iota(
-        jnp.int32, (rows, rows), 1
-    )
-    same = jnp.where((column == labels) & earlier, 1, 0)
-    slots = labels * CAP + jnp.sum(same, axis=0, keepdims=True)
+    step = 128
+    earlier = lax.broadcasted_iota(jnp.int32, (step, step), 0) < lax.broadcasted_iota(
+        jnp.int32, (step, step), 1
+    )
+    ranks = []
+    for at in range(0, rows, step):
+        here = labels[:, at : at + step]
+        found = jnp.where((column[at : at + step] == here) & earlier, 1, 0)
+        if at:
+            before = jnp.where(column[:at] == here, 1, 0)
+            found += jnp.sum(before.reshape(at // step, step, step), axis=0)
+        ranks.append(jnp.sum(found, axis=0, keepdims=True))
+    slots = labels * CAP + jnp.concatenate(ranks, axis=1)
     slots_ref[...] = slots
     tokens_in.wait()
     tokens = tokens_ref[...]
+    place = numbers(lax.broadcasted_iota(jnp.int32, (block, rows), 0))
     out = []
     for i in range(count):
-        place = lax.broadcasted_iota(jnp.int32, (block, rows), 0) + i * block
-        chosen = jnp.where(place == slots, 1.0, 0.0).astype(BF16)
+        chosen = one_hot(place == numbers(slots - i * block))
         parts[i] = jnp.dot(chosen, tokens, preferred_element_type=F32).astype(BF16)
         out.append(
             pltpu.make_async_copy(
@@ -173,36 +192,63 @@
     )(labels, tokens)
 
 
-def down_kernel(rows_ref, weight_ref, out_ref):
-    sources, tile, features = rows_ref.shape
+def down_kernel(rows_hbm, weight_hbm, out_ref, rows_ref, weight_ref, sems):
+    sources, slots, features = rows_ref.shape
     rank = weight_ref.shape[1]
+    tile = QUAD * CAP
+    quads, parts = slots // tile, 4
+    share = sources // parts
+    weights_in = [
+        pltpu.make_async_copy(
+            weight_hbm.at[pl.ds(q * QUAD, QUAD)], weight_ref.at[pl.ds(q * QUAD, QUAD)], sems.at[q]
+        )
+        for q in range(quads)
+    ]
+    rows_in = [
+        pltpu.make_async_copy(
+            rows_hbm.at[pl.ds(p * share, share)],
+            rows_ref.at[pl.ds(p * share, share)],
+            sems.at[quads + p],
+        )
+        for p in range(parts)
+    ]
+    for copy in weights_in[:1] + rows_in[:1] + weights_in[1:] + rows_in[1:]:
+        copy.start()
     owner = lax.broadcasted_iota(jnp.int32, (1, tile, 1), 1) // CAP
-    product = lax.dot_general(
-        rows_ref[...].reshape(sources * tile, features),
-        weight_ref[...].reshape(QUAD * rank, features),
-        (((1,), (1,)), ((), ())),
-        preferred_element_type=F32,
-    ).reshape(sources, tile, QUAD * rank)
-    lowered = jnp.zeros((sources, tile, rank), F32)
-    for k in range(QUAD):
-        lowered = jnp.where(owner == k, product[:, :, k * rank : (k + 1) * rank], lowered)
-    lowered = lowered.reshape(sources // 2, 2, tile, rank)
-    out_ref[...] = jnp.concatenate([lowered[:, 0], lowered[:, 1]], axis=-1).astype(BF16)
+    for p in range(parts):
+        rows_in[p].wait()
+        for q in range(quads):
+            if p == 0:
+                weights_in[q].wait()
+            rows = rows_ref[p * share : (p + 1) * share, q * tile : (q + 1) * tile, :]
+            product = lax.dot_general(
+                rows.reshape(share * tile, features),
+                weight_ref[q * QUAD : (q + 1) * QUAD].reshape(QUAD * rank, features),
+                (((1,), (1,)), ((), ())),
+                preferred_element_type=F32,
+            ).reshape(share, tile, QUAD * rank)
+            lowered = jnp.zeros((share, tile, rank), F32)
+            for k in range(QUAD):
+                lowered = jnp.where(owner == k, product[:, :, k * rank : (k + 1) * rank], lowered)
+            lowered = lowered.reshape(share // 2, 2, tile, rank)
+            out_ref[p * share // 2 : (p + 1) * share // 2, q * tile : (q + 1) * tile, :] = (
+                jnp.concatenate([lowered[:, 0], lowered[:, 1]], axis=-1).astype(BF16)
+            )
 
 
 def lower(received, weight):
     sources, slots, features = received.shape
     rank = weight.shape[1]
-    tile = QUAD * CAP
     return pl.pallas_call(
         down_kernel,
-        grid=(slots // tile,),
-        in_specs=[
-            pl.BlockSpec((sources, tile, features), lambda i: (0, i, 0)),
-            pl.BlockSpec((QUAD, rank, features), lambda i: (i, 0, 0)),
+        in_specs=[HBM, HBM],
+        out_specs=VMEM,
+        out_shape=jax.ShapeDtypeStruct((sources // 2, slots, 2 * rank), BF16),
+        scratch_shapes=[
+            pltpu.VMEM(received.shape, BF16),
+            pltpu.VMEM(weight.shape, BF16),
+            pltpu.SemaphoreType.DMA((slots // (QUAD * CAP) + 4,)),
         ],
-        out_specs=pl.BlockSpec((sources // 2, tile, 2 * rank), lambda i: (0, i, 0)),
-        out_shape=jax.ShapeDtypeStruct((sources // 2, slots, 2 * rank), BF16),
         compiler_params=pltpu.CompilerParams(vmem_limit_bytes=WIDE),
         cost_estimate=pl.CostEstimate(
             flops=2 * sources * slots * features * rank * QUAD,
@@ -253,9 +299,9 @@
     column = jnp.transpose(jnp.broadcast_to(slots_ref[...], (8, rows)))[:, 0:1]
     block = 256
     total = base_ref[...]
+    place = numbers(lax.broadcasted_iota(jnp.int32, (rows, block), 1))
     for first in range(0, places, block):
-        place = lax.broadcasted_iota(jnp.int32, (rows, block), 1) + first
-        take = jnp.where(place == column, 1.0, 0.0).astype(BF16)
+        take = one_hot(place == numbers(column - first))
         total += jnp.dot(
             take, returned_ref[first : first + block], preferred_element_type=F32
         )

time: 156 us -> 152 us (0.974)
  waiting for transfers between devices: 47.2 us -> 33.3 us
  blocking collectives: 28.4 us -> 34.2 us
  Pallas kernels: 19.5 us -> 21.1 us
    ppermute x6 -> x8, waiting for transfers between devices: 34.5 us -> 14.6 us  [shift(): lax.ppermute(array, 'tensor', [(i, (i + step) % groups) for i in range(gr...]
    all_to_all x3, waiting for transfers between devices: 10.5 us -> 16.5 us  [exchange(): lax.all_to_all(array, axis, split_axis=0, concat_axis=0, tiled=True, axis...]
    ppermute x6 -> x8, starting transfers between devices: 21.9 us -> 26 us  [shift(): lax.ppermute(array, 'tensor', [(i, (i + step) % groups) for i in range(gr...]
    all_to_all x2, blocking collectives: 21.1 us -> 25.1 us  [exchange(): lax.all_to_all(array, axis, split_axis=0, concat_axis=0, tiled=True, axis...]
    all_to_all x3, starting transfers between devices: 31.6 us -> 28.2 us  [exchange(): lax.all_to_all(array, axis, split_axis=0, concat_axis=0, tiled=True, axis...]
    pallas_call x1, Pallas kernels: 4.77 us -> 6.47 us  [lower(): pl.pallas_call(down_kernel, in_specs=[HBM, HBM], out_specs=VMEM, out_shap...]
  transfers between devices with their start and end apart: 11 -> 13, of which waited for: 9 -> 12; matrix products, arithmetic and copies ran while one was open for 0% -> 1% of each run, Pallas kernels for 3% -> 3%
where the time goes in v4:
time: 152 us; the launch traced here: 151 us
  starting transfers between devices  59 us (39%)
  blocking collectives  34.2 us (23%)
  waiting for transfers between devices  33.3 us (22%)
  Pallas kernels  21.1 us (14%)
  local copies, waits for them, and re-layouts  1.86 us (1%)
    all_to_all x3, starting transfers between devices, exchange(): lax.all_to_all(array, axis, split_axis=0, concat_axis=0, tiled=True, axis...  28.2 us
    ppermute x8, starting transfers between devices, shift(): lax.ppermute(array, 'tensor', [(i, (i + step) % groups) for i in range(gr...  26 us
    all_to_all x2, blocking collectives, exchange(): lax.all_to_all(array, axis, split_axis=0, concat_axis=0, tiled=True, axis...  25.1 us
    all_to_all x3, waiting for transfers between devices, exchange(): lax.all_to_all(array, axis, split_axis=0, concat_axis=0, tiled=True, axis...  16.5 us
    ppermute x8, waiting for transfers between devices, shift(): lax.ppermute(array, 'tensor', [(i, (i + step) % groups) for i in range(gr...  14.6 us
    pallas_call x8, Pallas kernels, call(): pl.pallas_call(kernel, out_shape=out_shape, in_specs=[VMEM] * len(operand...  9.66 us
    pallas_call x1, Pallas kernels, lower(): pl.pallas_call(down_kernel, in_specs=[HBM, HBM], out_specs=VMEM, out_shap...  6.47 us
    pallas_call x1, Pallas kernels, pack(): pl.pallas_call(pack_kernel, out_shape=[jax.ShapeDtypeStruct((1, rows), jn...  4.95 us
  transfers between devices with their start and end apart: 13, of which 12 were waited for; matrix products, arithmetic and copies ran while one was open for 1% of the time, Pallas kernels for 3%

profile of v4, /device:TPU:1, one launch (start us, length us, event | category | flops | bytes accessed | tf_op | source)
XLA Modules:
  0.0 151.0 jit_solution(7204444078470232267)
XLA Ops:
  0.6 5.0 %pack.1 = (s32[1,1024]{1,0:T(1,128)}, bf16[2048,512]{1,0:T(8,128)(2,1)}) custom-call(s32[1,1024]{1,0:T(1,128)} %bitcast.36, bf16[1024,512]{1,0:T(8,128)(2,1)} %tokens_ref.3), custom_call_target="tpu_custom_call" | custom-call | flops 2147483648 | bytes 3145728 | tf_op jit(solution)/shard_map/pack/pallas_call | solution.py:171
  5.6 0.0 copy-start
  5.6 0.0 copy-start.1
  5.6 14.1 %all-to-all-start = ((bf16[32,64,512]{2,1,0:T(8,128)(2,1)}), bf16[32,64,512]{2,1,0:T(8,128)(2,1)}, u32[]{:S(2)}, u32[]{:S(2)}) async-start(bf16[32,64,512]{2,1,0:T(8,128)(2,1)} %bitcast.33), calls=%async_computation | async-start | bytes 4194304 | tf_op jit(solution)/shard_map/all_to_all | solution.py:325
  19.7 0.0 copy-done
  19.8 0.0 copy-done.1
  19.8 1.0 base.4
  20.8 1.5 %base.5 = bf16[5,1024,128]{2,1,0:T(8,128)(2,1)S(1)} custom-call(bf16[1024,512]{1,0:T(8,128)(2,1)S(1)} %copy-done.1, bf16[512,2048]{1,0:T(8,128)(2,1)S(1)} %copy-done), custom_call_target="tpu_custom_call" | custom-call | flops 671088640 | bytes 4456448 | tf_op jit(solution)/shard_map/base/pallas_call | solution.py:24
  22.3 2.9 %collective-permute-start = (bf16[5,1024,128]{2,1,0:T(8,128)(2,1)S(1)}, bf16[5,1024,128]{2,1,0:T(8,128)(2,1)S(1)}, u32[]{:S(2)}, u32[]{:S(2)}) collective-permute-start(bf16[5,1024,128]{2,1,0:T(8,128)(2,1)S(1)} %base.5), channel_id=1, source_target_pairs={{0,1},{1,0},{2,3},{3,2},{4,5},{5,4},{6,7},{7,6},{8,9},{9,8},{10,11... | collective-permute-start | bytes 3932168 | tf_op jit(solution)/shard_map/ppermute | solution.py:85
  25.2 1.9 %collective-permute-start.1 = (bf16[3,1024,128]{2,1,0:T(8,128)(2,1)S(1)}, bf16[3,1024,128]{2,1,0:T(8,128)(2,1)S(1)}, u32[]{:S(2)}, u32[]{:S(2)}) collective-permute-start(bf16[3,1024,128]{2,1,0:T(8,128)(2,1)S(1)} %base.4), channel_id=1, source_target_pairs={{0,1},{1,0},{2,3},{3,2},{4,5},{5,4},{6,7},{7,6},{8,9},{9,8},{10,11... | collective-permute-start | bytes 2359304 | tf_op jit(solution)/shard_map/ppermute | solution.py:82
  27.1 2.3 %collective-permute-done.1.rest_0_ = bf16[3,1024,128]{2,1,0:T(8,128)(2,1)S(1)} collective-permute-done((bf16[3,1024,128]{2,1,0:T(8,128)(2,1)S(1)}, bf16[3,1024,128]{2,1,0:T(8,128)(2,1)S(1)}, u32[]{:S(2)}, u32[]{:S(2)}) %collective-permute-start.1) | collective-permute-done | bytes 786464 | tf_op jit(solution)/shard_map/ppermute | solution.py:82
  29.4 1.0 base.7
  30.4 3.2 %collective-permute-start.2 = (bf16[512,128]{1,0:T(8,128)(2,1)S(1)}, bf16[512,128]{1,0:T(8,128)(2,1)S(1)}, u32[]{:S(2)}, u32[]{:S(2)}) collective-permute-start(bf16[512,128]{1,0:T(8,128)(2,1)S(1)} %bitcast.32), channel_id=1, source_target_pairs={{0,2},{1,3},{2,4},{3,5},{4,6},{5,7},{6,8},{7,9},{8,10},{9,11},{10,... | collective-permute-start | bytes 393224 | tf_op jit(solution)/shard_map/ppermute | solution.py:73
  33.6 3.8 %collective-permute-start.3 = (bf16[512,128]{1,0:T(8,128)(2,1)S(1)}, bf16[512,128]{1,0:T(8,128)(2,1)S(1)}, u32[]{:S(2)}, u32[]{:S(2)}) collective-permute-start(bf16[512,128]{1,0:T(8,128)(2,1)S(1)} %bitcast.31), channel_id=1, source_target_pairs={{0,14},{1,15},{2,0},{3,1},{4,2},{5,3},{6,4},{7,5},{8,6},{9,7},{10,... | collective-permute-start | bytes 393224 | tf_op jit(solution)/shard_map/ppermute | solution.py:73
  37.4 1.9 %collective-permute-done.2.up_ref = bf16[512,128]{1,0:T(8,128)(2,1)S(1)} collective-permute-done((bf16[512,128]{1,0:T(8,128)(2,1)S(1)}, bf16[512,128]{1,0:T(8,128)(2,1)S(1)}, u32[]{:S(2)}, u32[]{:S(2)}) %collective-permute-start.2) | collective-permute-done | bytes 131104 | tf_op jit(solution)/shard_map/ppermute | solution.py:73
  39.4 0.9 collective-permute-done.3.down_ref
  40.3 0.1 ring.1
  40.3 3.2 %collective-permute-start.4 = (bf16[1024,128]{1,0:T(8,128)(2,1)S(1)}, bf16[1024,128]{1,0:T(8,128)(2,1)S(1)}, u32[]{:S(2)}, u32[]{:S(2)}) collective-permute-start(bf16[1024,128]{1,0:T(8,128)(2,1)S(1)} %get-tuple-element.33), channel_id=1, source_target_pairs={{0,2},{1,3},{2,4},{3,5},{4,6},{5,7},{6,8},{7,9},{8,10},{9,11},{10,... | collective-permute-start | bytes 786440 | tf_op jit(solution)/shard_map/ppermute | solution.py:73
  43.5 4.1 %collective-permute-start.6 = (bf16[1024,128]{1,0:T(8,128)(2,1)S(1)}, bf16[1024,128]{1,0:T(8,128)(2,1)S(1)}, u32[]{:S(2)}, u32[]{:S(2)}) collective-permute-start(bf16[1024,128]{1,0:T(8,128)(2,1)S(1)} %get-tuple-element.35), channel_id=1, source_target_pairs={{0,14},{1,15},{2,0},{3,1},{4,2},{5,3},{6,4},{7,5},{8,6},{9,7},{10,... | collective-permute-start | bytes 786440 | tf_op jit(solution)/shard_map/ppermute | solution.py:73
  47.6 0.0 collective-permute-done.rest_0_
  47.6 1.6 %base.6 = (bf16[1,1024,128]{2,1,0:T(8,128)(2,1)S(1)}, bf16[1,1024,128]{2,1,0:T(8,128)(2,1)S(1)}, bf16[1,1024,128]{2,1,0:T(8,128)(2,1)S(1)}, bf16[1,1024,128]{2,1,0:T(8,128)(2,1)S(1)}, bf16[1,1024,128]{2,1,0:T(8,128)(2,1)S(1)}) custom-call(bf16[1024,512]{1,0:T(8,128)(2,1)S(1)} %copy-done.1, bf16[512,2048]{1,0:T(8,128)(2,1)S(1)} %copy-done, ...), custom_call_target="tpu_custom_call" | custom-call | flops 671088640 | bytes 5767168 | tf_op jit(solution)/shard_map/base/pallas_call | solution.py:24
  49.2 0.0 copy-start.2
  49.2 0.7 copy-done.2
  49.9 0.7 copy-done.4
  50.6 1.0 collective-permute-done.4
  51.6 0.1 fusion.4
  51.7 1.9 %collective-permute-start.5 = (bf16[1024,128]{1,0:T(8,128)(2,1)S(1)}, bf16[1024,128]{1,0:T(8,128)(2,1)S(1)}, u32[]{:S(2)}, u32[]{:S(2)}) collective-permute-start(bf16[1024,128]{1,0:T(8,128)(2,1)S(1)} %fusion.4), channel_id=1, source_target_pairs={{0,2},{1,3},{2,4},{3,5},{4,6},{5,7},{6,8},{7,9},{8,10},{9,11},{10,... | collective-permute-start | bytes 786440 | tf_op jit(solution)/shard_map/ppermute | solution.py:73
  53.6 0.1 collective-permute-done.6
  53.7 0.1 fusion.3
  53.8 4.5 %collective-permute-start.7 = (bf16[1024,128]{1,0:T(8,128)(2,1)S(1)}, bf16[1024,128]{1,0:T(8,128)(2,1)S(1)}, u32[]{:S(2)}, u32[]{:S(2)}) collective-permute-start(bf16[1024,128]{1,0:T(8,128)(2,1)S(1)} %fusion.3), channel_id=1, source_target_pairs={{0,14},{1,15},{2,0},{3,1},{4,2},{5,3},{6,4},{7,5},{8,6},{9,7},{10,... | collective-permute-start | bytes 786440 | tf_op jit(solution)/shard_map/ppermute | solution.py:73
  58.3 3.1 %collective-permute-done.5 = bf16[1024,128]{1,0:T(8,128)(2,1)S(1)} collective-permute-done((bf16[1024,128]{1,0:T(8,128)(2,1)S(1)}, bf16[1024,128]{1,0:T(8,128)(2,1)S(1)}, u32[]{:S(2)}, u32[]{:S(2)}) %collective-permute-start.5) | collective-permute-done | bytes 262176 | tf_op jit(solution)/shard_map/ppermute | solution.py:73
  61.4 1.1 collective-permute-done.7
  62.5 6.2 %all-to-all-done.rows_hbm = bf16[32,64,512]{2,1,0:T(8,128)(2,1)} async-done(((bf16[32,64,512]{2,1,0:T(8,128)(2,1)}), bf16[32,64,512]{2,1,0:T(8,128)(2,1)}, u32[]{:S(2)}, u32[]{:S(2)}) %all-to-all-start) | async-done | bytes 2097184 | tf_op jit(solution)/shard_map/all_to_all | solution.py:325
  68.6 6.5 %down.1 = bf16[16,64,128]{2,1,0:T(8,128)(2,1)} custom-call(bf16[32,64,512]{2,1,0:T(8,128)(2,1)} %all-to-all-done.rows_hbm, bf16[16,64,512]{2,1,0:T(8,128)(2,1)} %bitcast.35), custom_call_target="tpu_custom_call" | custom-call | flops 536870912 | bytes 3145728 | tf_op jit(solution)/shard_map/down/pallas_call | solution.py:242
  75.1 0.0 copy-start.6
  75.1 4.3 %all-gather = bf16[32,64,128]{2,1,0:T(8,128)(2,1)S(1)} all-gather(bf16[16,64,128]{2,1,0:T(8,128)(2,1)} %down.1), channel_id=2, replica_groups={{0,1},{2,3},{4,5},{6,7},{8,9},{10,11},{12,13},{14,15},{16,17},{18,19},{..., dimensions={0}, use_global_device_ids=true | all-gather | bytes 786432 | tf_op jit(solution)/shard_map/all_gather | solution.py:331
  79.4 0.0 copy-start.5
  79.5 0.0 copy-start.3
  79.5 14.6 %all_to_all.25 = bf16[8,64,128]{2,1,0:T(8,128)(2,1)S(1)} all-to-all(bf16[8,64,128]{2,1,0:T(8,128)(2,1)S(1)} %fusion.6), channel_id=1, replica_groups={{0,2,4,6,8,10,12,14},{1,3,5,7,9,11,13,15},{16,18,20,22,24,26,28,30},{17..., dimensions={0} | all-to-all | bytes 262144 | tf_op jit(solution)/shard_map/all_to_all | solution.py:325
  94.2 10.4 %all_to_all.26 = bf16[8,64,128]{2,1,0:T(8,128)(2,1)S(1)} all-to-all(bf16[8,64,128]{2,1,0:T(8,128)(2,1)S(1)} %broadcast_in_dim.2), channel_id=1, replica_groups={{0,2,4,6,8,10,12,14},{1,3,5,7,9,11,13,15},{16,18,20,22,24,26,28,30},{17..., dimensions={0} | all-to-all | bytes 262144 | tf_op jit(solution)/shard_map/all_to_all | solution.py:325
  104.6 4.9 %all_gather.11.lowered_ref = bf16[16,64,128]{2,1,0:T(8,128)(2,1)S(1)} all-gather(bf16[8,64,128]{2,1,0:T(8,128)(2,1)S(1)} %all_to_all.26), channel_id=1, replica_groups={{0,1},{2,3},{4,5},{6,7},{8,9},{10,11},{12,13},{14,15},{16,17},{18,19},{..., dimensions={0}, use_global_device_ids=true | all-gather | bytes 393216 | tf_op jit(solution)/shard_map/all_gather | solution.py:340
  109.5 0.0 copy-done.6
  109.5 1.3 up.1
  110.8 6.0 %all-to-all-start.3 = ((bf16[32,64,128]{2,1,0:T(8,128)(2,1)}), bf16[32,64,128]{2,1,0:T(8,128)(2,1)S(1)}, u32[]{:S(2)}, u32[]{:S(2)}) async-start(bf16[32,64,128]{2,1,0:T(8,128)(2,1)} %bitcast.9), calls=%async_computation.3 | async-start | bytes 1048576 | tf_op jit(solution)/shard_map/all_to_all | solution.py:325
  116.8 0.0 copy-done.5
  116.8 0.1 fusion
  116.9 0.0 copy-start.9
  116.9 2.1 %collective-permute-start.9 = (bf16[1024,128]{1,0:T(8,128)(2,1)S(1)}, bf16[1024,128]{1,0:T(8,128)(2,1)S(1)}, u32[]{:S(2)}, u32[]{:S(2)}) collective-permute-start(bf16[1024,128]{1,0:T(8,128)(2,1)S(1)} %fusion), channel_id=1, source_target_pairs={{0,14},{1,15},{2,0},{3,1},{4,2},{5,3},{6,4},{7,5},{8,6},{9,7},{10,... | collective-permute-start | bytes 786440 | tf_op jit(solution)/shard_map/ppermute | solution.py:73
  119.0 0.0 copy-done.3
  119.0 0.1 fusion.1
  119.0 3.2 %collective-permute-start.8 = (bf16[1024,128]{1,0:T(8,128)(2,1)S(1)}, bf16[1024,128]{1,0:T(8,128)(2,1)S(1)}, u32[]{:S(2)}, u32[]{:S(2)}) collective-permute-start(bf16[1024,128]{1,0:T(8,128)(2,1)S(1)} %fusion.1), channel_id=1, source_target_pairs={{0,2},{1,3},{2,4},{3,5},{4,6},{5,7},{6,8},{7,9},{8,10},{9,11},{10,... | collective-permute-start | bytes 786440 | tf_op jit(solution)/shard_map/ppermute | solution.py:73
  122.3 0.1 copy.13
  122.4 0.1 reshape.47.accepted_ref
  122.5 3.5 %collective-permute-done.9 = bf16[1024,128]{1,0:T(8,128)(2,1)S(1)} collective-permute-done((bf16[1024,128]{1,0:T(8,128)(2,1)S(1)}, bf16[1024,128]{1,0:T(8,128)(2,1)S(1)}, u32[]{:S(2)}, u32[]{:S(2)}) %collective-permute-start.9) | collective-permute-done | bytes 262176 | tf_op jit(solution)/shard_map/ppermute | solution.py:73
  126.0 3.1 %collective-permute-done.8 = bf16[1024,128]{1,0:T(8,128)(2,1)S(1)} collective-permute-done((bf16[1024,128]{1,0:T(8,128)(2,1)S(1)}, bf16[1024,128]{1,0:T(8,128)(2,1)S(1)}, u32[]{:S(2)}, u32[]{:S(2)}) %collective-permute-start.8) | collective-permute-done | bytes 262176 | tf_op jit(solution)/shard_map/ppermute | solution.py:73
  129.0 0.1 fusion.2.base_ref
  129.2 1.7 %all-to-all-done.3 = bf16[32,64,128]{2,1,0:T(8,128)(2,1)S(1)} async-done(((bf16[32,64,128]{2,1,0:T(8,128)(2,1)}), bf16[32,64,128]{2,1,0:T(8,128)(2,1)S(1)}, u32[]{:S(2)}, u32[]{:S(2)}) %all-to-all-start.3) | async-done | bytes 524320 | tf_op jit(solution)/shard_map/all_to_all | solution.py:325
  130.9 2.4 %finish.1 = (bf16[1024,128]{1,0:T(8,128)(2,1)}, bf16[128,128]{1,0:T(8,128)(2,1)}) custom-call(s32[1,1024]{1,0:T(1,128)S(1)} %copy-done.7, bf16[2048,128]{1,0:T(8,128)(2,1)S(1)} %bitcast.29, f32[1024,128]{1,0:T(8,128)S(1)} %fusion.2.base_ref, s32[1,128]{1,0:T(1,128)S(1)} %reshape.47.accepted_ref), custom_call_target="tpu_custom_call" | custom-call | flops 536870912 | bytes 1348096 | tf_op jit(solution)/shard_map/finish/pallas_call | solution.py:24
  133.3 8.1 %all-to-all-start.4 = ((bf16[32,4,128]{2,1,0:T(4,128)(2,1)}), bf16[32,4,128]{2,1,0:T(4,128)(2,1)S(1)}, u32[]{:S(2)}, u32[]{:S(2)}) async-start(bf16[32,4,128]{2,1,0:T(4,128)(2,1)} %bitcast.14), calls=%async_computation.4 | async-start | bytes 65536 | tf_op jit(solution)/shard_map/all_to_all | solution.py:325
  141.5 0.0 copy-done.9
  141.5 0.1 copy.14
  141.6 0.1 reshape.48.targets_ref
  141.7 8.6 %all-to-all-done.4 = bf16[32,4,128]{2,1,0:T(4,128)(2,1)S(1)} async-done(((bf16[32,4,128]{2,1,0:T(4,128)(2,1)}), bf16[32,4,128]{2,1,0:T(4,128)(2,1)S(1)}, u32[]{:S(2)}, u32[]{:S(2)}) %all-to-all-start.4) | async-done | bytes 32800 | tf_op jit(solution)/shard_map/all_to_all | solution.py:325
  150.3 0.8 cache.1
  (9 shorter events, 0.1 us)
Async XLA Ops:
  5.6 14.2 %copy-start = (bf16[512,2048]{1,0:T(8,128)(2,1)S(1)}, bf16[512,2048]{1,0:T(8,128)(2,1)}, u32[]{:S(2)}) copy-start(bf16[512,2048]{1,0:T(8,128)(2,1)} %weight_ref.8) | copy-start | bytes 6291460
  5.6 14.2 %copy-start.1 = (bf16[1024,512]{1,0:T(8,128)(2,1)S(1)}, bf16[1024,512]{1,0:T(8,128)(2,1)}, u32[]{:S(2)}) copy-start(bf16[1024,512]{1,0:T(8,128)(2,1)} %tokens_ref.3) | copy-start | bytes 3145732
  5.6 63.0 %all-to-all-start = ((bf16[32,64,512]{2,1,0:T(8,128)(2,1)}), bf16[32,64,512]{2,1,0:T(8,128)(2,1)}, u32[]{:S(2)}, u32[]{:S(2)}) async-start(bf16[32,64,512]{2,1,0:T(8,128)(2,1)} %bitcast.33), calls=%async_computation | async-start | bytes 4194304 | tf_op jit(solution)/shard_map/all_to_all | solution.py:325
  22.3 25.3 %collective-permute-start = (bf16[5,1024,128]{2,1,0:T(8,128)(2,1)S(1)}, bf16[5,1024,128]{2,1,0:T(8,128)(2,1)S(1)}, u32[]{:S(2)}, u32[]{:S(2)}) collective-permute-start(bf16[5,1024,128]{2,1,0:T(8,128)(2,1)S(1)} %base.5), channel_id=1, source_target_pairs={{0,1},{1,0},{2,3},{3,2},{4,5},{5,4},{6,7},{7,6},{8,9},{9,8},{10,11... | collective-permute-start | bytes 3932168 | tf_op jit(solution)/shard_map/ppermute | solution.py:85
  25.2 4.2 %collective-permute-start.1 = (bf16[3,1024,128]{2,1,0:T(8,128)(2,1)S(1)}, bf16[3,1024,128]{2,1,0:T(8,128)(2,1)S(1)}, u32[]{:S(2)}, u32[]{:S(2)}) collective-permute-start(bf16[3,1024,128]{2,1,0:T(8,128)(2,1)S(1)} %base.4), channel_id=1, source_target_pairs={{0,1},{1,0},{2,3},{3,2},{4,5},{5,4},{6,7},{7,6},{8,9},{9,8},{10,11... | collective-permute-start | bytes 2359304 | tf_op jit(solution)/shard_map/ppermute | solution.py:82
  30.4 9.0 %collective-permute-start.2 = (bf16[512,128]{1,0:T(8,128)(2,1)S(1)}, bf16[512,128]{1,0:T(8,128)(2,1)S(1)}, u32[]{:S(2)}, u32[]{:S(2)}) collective-permute-start(bf16[512,128]{1,0:T(8,128)(2,1)S(1)} %bitcast.32), channel_id=1, source_target_pairs={{0,2},{1,3},{2,4},{3,5},{4,6},{5,7},{6,8},{7,9},{8,10},{9,11},{10,... | collective-permute-start | bytes 393224 | tf_op jit(solution)/shard_map/ppermute | solution.py:73
  33.6 6.6 %collective-permute-start.3 = (bf16[512,128]{1,0:T(8,128)(2,1)S(1)}, bf16[512,128]{1,0:T(8,128)(2,1)S(1)}, u32[]{:S(2)}, u32[]{:S(2)}) collective-permute-start(bf16[512,128]{1,0:T(8,128)(2,1)S(1)} %bitcast.31), channel_id=1, source_target_pairs={{0,14},{1,15},{2,0},{3,1},{4,2},{5,3},{6,4},{7,5},{8,6},{9,7},{10,... | collective-permute-start | bytes 393224 | tf_op jit(solution)/shard_map/ppermute | solution.py:73
  40.3 11.3 %collective-permute-start.4 = (bf16[1024,128]{1,0:T(8,128)(2,1)S(1)}, bf16[1024,128]{1,0:T(8,128)(2,1)S(1)}, u32[]{:S(2)}, u32[]{:S(2)}) collective-permute-start(bf16[1024,128]{1,0:T(8,128)(2,1)S(1)} %get-tuple-element.33), channel_id=1, source_target_pairs={{0,2},{1,3},{2,4},{3,5},{4,6},{5,7},{6,8},{7,9},{8,10},{9,11},{10,... | collective-permute-start | bytes 786440 | tf_op jit(solution)/shard_map/ppermute | solution.py:73
  43.5 10.2 %collective-permute-start.6 = (bf16[1024,128]{1,0:T(8,128)(2,1)S(1)}, bf16[1024,128]{1,0:T(8,128)(2,1)S(1)}, u32[]{:S(2)}, u32[]{:S(2)}) collective-permute-start(bf16[1024,128]{1,0:T(8,128)(2,1)S(1)} %get-tuple-element.35), channel_id=1, source_target_pairs={{0,14},{1,15},{2,0},{3,1},{4,2},{5,3},{6,4},{7,5},{8,6},{9,7},{10,... | collective-permute-start | bytes 786440 | tf_op jit(solution)/shard_map/ppermute | solution.py:73
  49.2 0.7 copy-start.2
  49.9 0.7 copy-start.4
  51.7 9.7 %collective-permute-start.5 = (bf16[1024,128]{1,0:T(8,128)(2,1)S(1)}, bf16[1024,128]{1,0:T(8,128)(2,1)S(1)}, u32[]{:S(2)}, u32[]{:S(2)}) collective-permute-start(bf16[1024,128]{1,0:T(8,128)(2,1)S(1)} %fusion.4), channel_id=1, source_target_pairs={{0,2},{1,3},{2,4},{3,5},{4,6},{5,7},{6,8},{7,9},{8,10},{9,11},{10,... | collective-permute-start | bytes 786440 | tf_op jit(solution)/shard_map/ppermute | solution.py:73
  53.8 8.6 %collective-permute-start.7 = (bf16[1024,128]{1,0:T(8,128)(2,1)S(1)}, bf16[1024,128]{1,0:T(8,128)(2,1)S(1)}, u32[]{:S(2)}, u32[]{:S(2)}) collective-permute-start(bf16[1024,128]{1,0:T(8,128)(2,1)S(1)} %fusion.3), channel_id=1, source_target_pairs={{0,14},{1,15},{2,0},{3,1},{4,2},{5,3},{6,4},{7,5},{8,6},{9,7},{10,... | collective-permute-start | bytes 786440 | tf_op jit(solution)/shard_map/ppermute | solution.py:73
  75.1 34.4 %copy-start.6 = (bf16[16,64,128]{2,1,0:T(8,128)(2,1)S(1)}, bf16[16,64,128]{2,1,0:T(8,128)(2,1)}, u32[]{:S(2)}) copy-start(bf16[16,64,128]{2,1,0:T(8,128)(2,1)} %weight_ref.9) | copy-start | bytes 786436
  79.4 37.4 %copy-start.5 = (bf16[1,1024,128]{2,1,0:T(8,128)(2,1)S(1)}, bf16[1,1024,128]{2,1,0:T(8,128)(2,1)}, u32[]{:S(2)}) copy-start(bf16[1,1024,128]{2,1,0:T(8,128)(2,1)} %copy-done.4) | copy-start | bytes 786436
  79.5 39.5 %copy-start.3 = (bf16[1,1024,128]{2,1,0:T(8,128)(2,1)S(1)}, bf16[1,1024,128]{2,1,0:T(8,128)(2,1)}, u32[]{:S(2)}) copy-start(bf16[1,1024,128]{2,1,0:T(8,128)(2,1)} %copy-done.2) | copy-start | bytes 786436
  104.6 17.7 %copy-start.8 = (s32[1,32,4]{1,2,0:T(4,128)S(1)}, s32[1,32,4]{1,2,0:T(4,128)}, u32[]{:S(2)}) copy-start(s32[1,32,4]{1,2,0:T(4,128)} %param.12) | copy-start | bytes 1540
  110.8 20.1 %copy-start.7 = (s32[1,1024]{1,0:T(1,128)S(1)}, s32[1,1024]{1,0:T(1,128)}, u32[]{:S(2)}) copy-start(s32[1,1024]{1,0:T(1,128)} %get-tuple-element.24.slots_ref) | copy-start | bytes 12292
  110.8 20.1 %all-to-all-start.3 = ((bf16[32,64,128]{2,1,0:T(8,128)(2,1)}), bf16[32,64,128]{2,1,0:T(8,128)(2,1)S(1)}, u32[]{:S(2)}, u32[]{:S(2)}) async-start(bf16[32,64,128]{2,1,0:T(8,128)(2,1)} %bitcast.9), calls=%async_computation.3 | async-start | bytes 1048576 | tf_op jit(solution)/shard_map/all_to_all | solution.py:325
  116.9 24.6 %copy-start.9 = (s32[32,1,4]{0,2,1:T(4,128)S(1)}, s32[32,1,4]{0,2,1:T(4,128)}, u32[]{:S(2)}) copy-start(s32[32,1,4]{0,2,1:T(4,128)} %param.13) | copy-start | bytes 1540
  116.9 9.1 %collective-permute-start.9 = (bf16[1024,128]{1,0:T(8,128)(2,1)S(1)}, bf16[1024,128]{1,0:T(8,128)(2,1)S(1)}, u32[]{:S(2)}, u32[]{:S(2)}) collective-permute-start(bf16[1024,128]{1,0:T(8,128)(2,1)S(1)} %fusion), channel_id=1, source_target_pairs={{0,14},{1,15},{2,0},{3,1},{4,2},{5,3},{6,4},{7,5},{8,6},{9,7},{10,... | collective-permute-start | bytes 786440 | tf_op jit(solution)/shard_map/ppermute | solution.py:73
  119.0 10.0 %collective-permute-start.8 = (bf16[1024,128]{1,0:T(8,128)(2,1)S(1)}, bf16[1024,128]{1,0:T(8,128)(2,1)S(1)}, u32[]{:S(2)}, u32[]{:S(2)}) collective-permute-start(bf16[1024,128]{1,0:T(8,128)(2,1)S(1)} %fusion.1), channel_id=1, source_target_pairs={{0,2},{1,3},{2,4},{3,5},{4,6},{5,7},{6,8},{7,9},{8,10},{9,11},{10,... | collective-permute-start | bytes 786440 | tf_op jit(solution)/shard_map/ppermute | solution.py:73
  133.3 16.9 %all-to-all-start.4 = ((bf16[32,4,128]{2,1,0:T(4,128)(2,1)}), bf16[32,4,128]{2,1,0:T(4,128)(2,1)S(1)}, u32[]{:S(2)}, u32[]{:S(2)}) async-start(bf16[32,4,128]{2,1,0:T(4,128)(2,1)} %bitcast.14), calls=%async_computation.4 | async-start | bytes 65536 | tf_op jit(solution)/shard_map/all_to_all | solution.py:325

commit v5 on v4

--- a/solution.py
+++ b/solution.py
@@ -73,7 +73,7 @@
     return lax.ppermute(array, "tensor", [(i, (i + step) % groups) for i in range(groups)])
 
 
-def sum_base(tokens, weight, columns, groups, after):
+def sum_base(tokens, weight, columns, groups, after, down_weight):
     rows = tokens.shape[0]
     half = rows // 2
     swap = [(i, i ^ 1) for i in range(groups)]
@@ -101,9 +101,11 @@
     )
     up, down = shift(third, 1, groups), shift(fifth, -1, groups)
     up, down = shift(add(second[0], up), 1, groups), shift(add(sixth[0], down), -1, groups)
-    after, up, down = lax.optimization_barrier((after, up, down))
+    down_weight, up, down = lax.optimization_barrier((down_weight, up, down))
+    down_weight = turn(down_weight)
+    after, down_weight = lax.optimization_barrier((after, down_weight))
     up, down = shift(add(first[0], up), 1, groups), shift(add(seventh[0], down), -1, groups)
-    return after, [mine[0], up, down]
+    return after, down_weight, [mine[0], up, down]
 
 
 def ring_kernel(third_ref, fifth_ref, up_ref, down_ref, third_out, fifth_out):
@@ -192,64 +194,71 @@
     )(labels, tokens)
 
 
-def down_kernel(rows_hbm, weight_hbm, out_ref, rows_ref, weight_ref, sems):
+def turn_kernel(weight_ref, out_ref):
+    for quad in range(out_ref.shape[0]):
+        for k in range(QUAD):
+            turned = jnp.transpose(weight_ref[quad * QUAD + k])
+            rank = turned.shape[1]
+            out_ref[quad, :, k * rank : (k + 1) * rank] = turned
+
+
+def turn(weight):
+    adapters, rank, features = weight.shape
+    return call(
+        turn_kernel,
+        jax.ShapeDtypeStruct((adapters // QUAD, features, QUAD * rank), BF16),
+        (weight,),
+        0,
+        name="turn",
+    )
+
+
+def down_kernel(rows_hbm, weight_ref, out_ref, rows_ref, sems):
     sources, slots, features = rows_ref.shape
-    rank = weight_ref.shape[1]
+    rank = weight_ref.shape[2] // QUAD
     tile = QUAD * CAP
-    quads, parts = slots // tile, 4
+    parts = sems.shape[0]
     share = sources // parts
-    weights_in = [
-        pltpu.make_async_copy(
-            weight_hbm.at[pl.ds(q * QUAD, QUAD)], weight_ref.at[pl.ds(q * QUAD, QUAD)], sems.at[q]
-        )
-        for q in range(quads)
-    ]
     rows_in = [
         pltpu.make_async_copy(
-            rows_hbm.at[pl.ds(p * share, share)],
-            rows_ref.at[pl.ds(p * share, share)],
-            sems.at[quads + p],
+            rows_hbm.at[pl.ds(p * share, share)], rows_ref.at[pl.ds(p * share, share)], sems.at[p]
         )
         for p in range(parts)
     ]
-    for copy in weights_in[:1] + rows_in[:1] + weights_in[1:] + rows_in[1:]:
+    for copy in rows_in:
         copy.start()
     owner = lax.broadcasted_iota(jnp.int32, (1, tile, 1), 1) // CAP
     for p in range(parts):
         rows_in[p].wait()
-        for q in range(quads):
-            if p == 0:
-                weights_in[q].wait()
-            rows = rows_ref[p * share : (p + 1) * share, q * tile : (q + 1) * tile, :]
-            product = lax.dot_general(
+        for quad in range(slots // tile):
+            rows = rows_ref[p * share : (p + 1) * share, quad * tile : (quad + 1) * tile, :]
+            product = jnp.dot(
                 rows.reshape(share * tile, features),
-                weight_ref[q * QUAD : (q + 1) * QUAD].reshape(QUAD * rank, features),
-                (((1,), (1,)), ((), ())),
+                weight_ref[quad],
                 preferred_element_type=F32,
             ).reshape(share, tile, QUAD * rank)
             lowered = jnp.zeros((share, tile, rank), F32)
             for k in range(QUAD):
                 lowered = jnp.where(owner == k, product[:, :, k * rank : (k + 1) * rank], lowered)
             lowered = lowered.reshape(share // 2, 2, tile, rank)
-            out_ref[p * share // 2 : (p + 1) * share // 2, q * tile : (q + 1) * tile, :] = (
-                jnp.concatenate([lowered[:, 0], lowered[:, 1]], axis=-1).astype(BF16)
-            )
+            out_ref[
+                p * share // 2 : (p + 1) * share // 2, quad * tile : (quad + 1) * tile, :
+            ] = jnp.concatenate([lowered[:, 0], lowered[:, 1]], axis=-1).astype(BF16)
 
 
 def lower(received, weight):
     sources, slots, features = received.shape
-    rank = weight.shape[1]
+    rank = weight.shape[2] // QUAD
     return pl.pallas_call(
         down_kernel,
-        in_specs=[HBM, HBM],
+        in_specs=[HBM, VMEM],
         out_specs=VMEM,
         out_shape=jax.ShapeDtypeStruct((sources // 2, slots, 2 * rank), BF16),
         scratch_shapes=[
             pltpu.VMEM(received.shape, BF16),
-            pltpu.VMEM(weight.shape, BF16),
-            pltpu.SemaphoreType.DMA((slots // (QUAD * CAP) + 4,)),
+            pltpu.SemaphoreType.DMA((4,)),
         ],
-        compiler_params=pltpu.CompilerParams(vmem_limit_bytes=WIDE),
+        compiler_params=pltpu.CompilerParams(vmem_limit_bytes=LIMIT),
         cost_estimate=pl.CostEstimate(
             flops=2 * sources * slots * features * rank * QUAD,
             bytes_accessed=2 * (sources * slots * features + slots // CAP * rank * features),
@@ -363,9 +372,16 @@
     received = exchange(packed.reshape(owners, here, features), "adapter")
 
     tokens, slots = lax.optimization_barrier((tokens, slots))
-    received, base = sum_base(tokens, key_value_weight, columns, groups, received)
-
-    partial_rank = lower(received, jnp.swapaxes(adapter_down_weight, 1, 2))
+    received, down_weight, base = sum_base(
+        tokens,
+        key_value_weight,
+        columns,
+        groups,
+        received,
+        jnp.swapaxes(adapter_down_weight, 1, 2),
+    )
+
+    partial_rank = lower(received, down_weight)
     lowered = sum_over_tensor(partial_rank, core, pairs, chips)
     update = raise_rank(lowered, adapter_up_weight)
     returned = exchange(update.reshape(owners, here, columns), "adapter")

time: 152 us -> 149 us (0.980)
  waiting for transfers between devices: 33.3 us -> 30.8 us
    pallas_call x1, Pallas kernels: 6.47 us -> 3.86 us  [lower(): pl.pallas_call(down_kernel, in_specs=[HBM, VMEM], out_specs=VMEM, out_sha...]
    all_to_all x3, waiting for transfers between devices: 16.5 us -> 13.9 us  [exchange(): lax.all_to_all(array, axis, split_axis=0, concat_axis=0, tiled=True, axis...]
    pallas_call x8 -> x9, Pallas kernels: 9.66 us -> 10.8 us  [call(): pl.pallas_call(kernel, out_shape=out_shape, in_specs=[VMEM] * len(operand...]
  transfers between devices with their start and end apart: 13 -> 13, of which waited for: 12 -> 12; matrix products, arithmetic and copies ran while one was open for 1% -> 1% of each run, Pallas kernels for 3% -> 4%
where the time goes in v5:
time: 149 us; the launch traced here: 148 us
  starting transfers between devices  59.2 us (40%)
  blocking collectives  34 us (23%)
  waiting for transfers between devices  30.8 us (21%)
  Pallas kernels  19.6 us (13%)
  local copies, waits for them, and re-layouts  3.06 us (2%)
    all_to_all x3, starting transfers between devices, exchange(): lax.all_to_all(array, axis, split_axis=0, concat_axis=0, tiled=True, axis...  28.4 us
    ppermute x8, starting transfers between devices, shift(): lax.ppermute(array, 'tensor', [(i, (i + step) % groups) for i in range(gr...  25.9 us
    all_to_all x2, blocking collectives, exchange(): lax.all_to_all(array, axis, split_axis=0, concat_axis=0, tiled=True, axis...  25.1 us
    ppermute x8, waiting for transfers between devices, shift(): lax.ppermute(array, 'tensor', [(i, (i + step) % groups) for i in range(gr...  14.7 us
    all_to_all x3, waiting for transfers between devices, exchange(): lax.all_to_all(array, axis, split_axis=0, concat_axis=0, tiled=True, axis...  13.9 us
    pallas_call x9, Pallas kernels, call(): pl.pallas_call(kernel, out_shape=out_shape, in_specs=[VMEM] * len(operand...  10.8 us
    pallas_call x1, Pallas kernels, pack(): pl.pallas_call(pack_kernel, out_shape=[jax.ShapeDtypeStruct((1, rows), jn...  4.95 us
    all_gather x1, blocking collectives, sum_over_tensor(): lax.all_gather(mine, 'tensor', axis=0, axis_index_groups=pairs, tiled=True)  4.93 us
  transfers between devices with their start and end apart: 13, of which 12 were waited for; matrix products, arithmetic and copies ran while one was open for 1% of the time, Pallas kernels for 4%

profile of v5, /device:TPU:1, one launch (start us, length us, event | category | flops | bytes accessed | tf_op | source)
XLA Modules:
  0.0 148.2 jit_solution(6614319443613703163)
XLA Ops:
  0.6 5.0 %pack.1 = (s32[1,1024]{1,0:T(1,128)}, bf16[2048,512]{1,0:T(8,128)(2,1)}) custom-call(s32[1,1024]{1,0:T(1,128)} %bitcast.36, bf16[1024,512]{1,0:T(8,128)(2,1)} %tokens_ref.3), custom_call_target="tpu_custom_call" | custom-call | flops 2147483648 | bytes 3145728 | tf_op jit(solution)/shard_map/pack/pallas_call | solution.py:173
  5.6 0.0 copy-start
  5.6 0.0 copy-start.1
  5.6 14.1 %all-to-all-start = ((bf16[32,64,512]{2,1,0:T(8,128)(2,1)}), bf16[32,64,512]{2,1,0:T(8,128)(2,1)}, u32[]{:S(2)}, u32[]{:S(2)}) async-start(bf16[32,64,512]{2,1,0:T(8,128)(2,1)} %bitcast.34), calls=%async_computation | async-start | bytes 4194304 | tf_op jit(solution)/shard_map/all_to_all | solution.py:334
  19.7 0.0 copy-done
  19.8 0.0 copy-done.1
  19.8 1.0 base.4
  20.8 1.6 %base.5 = bf16[5,1024,128]{2,1,0:T(8,128)(2,1)S(1)} custom-call(bf16[1024,512]{1,0:T(8,128)(2,1)S(1)} %copy-done.1, bf16[512,2048]{1,0:T(8,128)(2,1)S(1)} %copy-done), custom_call_target="tpu_custom_call" | custom-call | flops 671088640 | bytes 4456448 | tf_op jit(solution)/shard_map/base/pallas_call | solution.py:24
  22.3 2.9 %collective-permute-start = (bf16[5,1024,128]{2,1,0:T(8,128)(2,1)S(1)}, bf16[5,1024,128]{2,1,0:T(8,128)(2,1)S(1)}, u32[]{:S(2)}, u32[]{:S(2)}) collective-permute-start(bf16[5,1024,128]{2,1,0:T(8,128)(2,1)S(1)} %base.5), channel_id=1, source_target_pairs={{0,1},{1,0},{2,3},{3,2},{4,5},{5,4},{6,7},{7,6},{8,9},{9,8},{10,11... | collective-permute-start | bytes 3932168 | tf_op jit(solution)/shard_map/ppermute | solution.py:85
  25.2 1.9 %collective-permute-start.1 = (bf16[3,1024,128]{2,1,0:T(8,128)(2,1)S(1)}, bf16[3,1024,128]{2,1,0:T(8,128)(2,1)S(1)}, u32[]{:S(2)}, u32[]{:S(2)}) collective-permute-start(bf16[3,1024,128]{2,1,0:T(8,128)(2,1)S(1)} %base.4), channel_id=1, source_target_pairs={{0,1},{1,0},{2,3},{3,2},{4,5},{5,4},{6,7},{7,6},{8,9},{9,8},{10,11... | collective-permute-start | bytes 2359304 | tf_op jit(solution)/shard_map/ppermute | solution.py:82
  27.2 2.3 %collective-permute-done.1.rest_0_ = bf16[3,1024,128]{2,1,0:T(8,128)(2,1)S(1)} collective-permute-done((bf16[3,1024,128]{2,1,0:T(8,128)(2,1)S(1)}, bf16[3,1024,128]{2,1,0:T(8,128)(2,1)S(1)}, u32[]{:S(2)}, u32[]{:S(2)}) %collective-permute-start.1) | collective-permute-done | bytes 786464 | tf_op jit(solution)/shard_map/ppermute | solution.py:82
  29.4 1.0 base.7
  30.4 3.2 %collective-permute-start.2 = (bf16[512,128]{1,0:T(8,128)(2,1)S(1)}, bf16[512,128]{1,0:T(8,128)(2,1)S(1)}, u32[]{:S(2)}, u32[]{:S(2)}) collective-permute-start(bf16[512,128]{1,0:T(8,128)(2,1)S(1)} %bitcast.33), channel_id=1, source_target_pairs={{0,2},{1,3},{2,4},{3,5},{4,6},{5,7},{6,8},{7,9},{8,10},{9,11},{10,... | collective-permute-start | bytes 393224 | tf_op jit(solution)/shard_map/ppermute | solution.py:73
  33.6 3.8 %collective-permute-start.3 = (bf16[512,128]{1,0:T(8,128)(2,1)S(1)}, bf16[512,128]{1,0:T(8,128)(2,1)S(1)}, u32[]{:S(2)}, u32[]{:S(2)}) collective-permute-start(bf16[512,128]{1,0:T(8,128)(2,1)S(1)} %bitcast.32), channel_id=1, source_target_pairs={{0,14},{1,15},{2,0},{3,1},{4,2},{5,3},{6,4},{7,5},{8,6},{9,7},{10,... | collective-permute-start | bytes 393224 | tf_op jit(solution)/shard_map/ppermute | solution.py:73
  37.4 1.9 %collective-permute-done.2.up_ref = bf16[512,128]{1,0:T(8,128)(2,1)S(1)} collective-permute-done((bf16[512,128]{1,0:T(8,128)(2,1)S(1)}, bf16[512,128]{1,0:T(8,128)(2,1)S(1)}, u32[]{:S(2)}, u32[]{:S(2)}) %collective-permute-start.2) | collective-permute-done | bytes 131104 | tf_op jit(solution)/shard_map/ppermute | solution.py:73
  39.4 0.9 collective-permute-done.3.down_ref
  40.3 0.1 ring.1
  40.3 3.2 %collective-permute-start.4 = (bf16[1024,128]{1,0:T(8,128)(2,1)S(1)}, bf16[1024,128]{1,0:T(8,128)(2,1)S(1)}, u32[]{:S(2)}, u32[]{:S(2)}) collective-permute-start(bf16[1024,128]{1,0:T(8,128)(2,1)S(1)} %get-tuple-element.35), channel_id=1, source_target_pairs={{0,2},{1,3},{2,4},{3,5},{4,6},{5,7},{6,8},{7,9},{8,10},{9,11},{10,... | collective-permute-start | bytes 786440 | tf_op jit(solution)/shard_map/ppermute | solution.py:73
  43.5 4.1 %collective-permute-start.6 = (bf16[1024,128]{1,0:T(8,128)(2,1)S(1)}, bf16[1024,128]{1,0:T(8,128)(2,1)S(1)}, u32[]{:S(2)}, u32[]{:S(2)}) collective-permute-start(bf16[1024,128]{1,0:T(8,128)(2,1)S(1)} %get-tuple-element.37), channel_id=1, source_target_pairs={{0,14},{1,15},{2,0},{3,1},{4,2},{5,3},{6,4},{7,5},{8,6},{9,7},{10,... | collective-permute-start | bytes 786440 | tf_op jit(solution)/shard_map/ppermute | solution.py:73
  47.6 0.0 collective-permute-done.rest_0_
  47.6 1.6 %base.6 = (bf16[1,1024,128]{2,1,0:T(8,128)(2,1)S(1)}, bf16[1,1024,128]{2,1,0:T(8,128)(2,1)S(1)}, bf16[1,1024,128]{2,1,0:T(8,128)(2,1)S(1)}, bf16[1,1024,128]{2,1,0:T(8,128)(2,1)S(1)}, bf16[1,1024,128]{2,1,0:T(8,128)(2,1)S(1)}) custom-call(bf16[1024,512]{1,0:T(8,128)(2,1)S(1)} %copy-done.1, bf16[512,2048]{1,0:T(8,128)(2,1)S(1)} %copy-done, ...), custom_call_target="tpu_custom_call" | custom-call | flops 671088640 | bytes 5767168 | tf_op jit(solution)/shard_map/base/pallas_call | solution.py:24
  49.2 0.0 copy-start.3
  49.2 0.7 copy-done.3
  49.9 0.7 copy-done.5
  50.6 1.0 collective-permute-done.4
  51.6 0.1 fusion.4
  51.7 1.9 %collective-permute-start.5 = (bf16[1024,128]{1,0:T(8,128)(2,1)S(1)}, bf16[1024,128]{1,0:T(8,128)(2,1)S(1)}, u32[]{:S(2)}, u32[]{:S(2)}) collective-permute-start(bf16[1024,128]{1,0:T(8,128)(2,1)S(1)} %fusion.4), channel_id=1, source_target_pairs={{0,2},{1,3},{2,4},{3,5},{4,6},{5,7},{6,8},{7,9},{8,10},{9,11},{10,... | collective-permute-start | bytes 786440 | tf_op jit(solution)/shard_map/ppermute | solution.py:73
  53.6 0.1 collective-permute-done.6
  53.7 0.1 fusion.3
  53.8 4.5 %collective-permute-start.7 = (bf16[1024,128]{1,0:T(8,128)(2,1)S(1)}, bf16[1024,128]{1,0:T(8,128)(2,1)S(1)}, u32[]{:S(2)}, u32[]{:S(2)}) collective-permute-start(bf16[1024,128]{1,0:T(8,128)(2,1)S(1)} %fusion.3), channel_id=1, source_target_pairs={{0,14},{1,15},{2,0},{3,1},{4,2},{5,3},{6,4},{7,5},{8,6},{9,7},{10,... | collective-permute-start | bytes 786440 | tf_op jit(solution)/shard_map/ppermute | solution.py:73
  58.3 3.1 %collective-permute-done.5 = bf16[1024,128]{1,0:T(8,128)(2,1)S(1)} collective-permute-done((bf16[1024,128]{1,0:T(8,128)(2,1)S(1)}, bf16[1024,128]{1,0:T(8,128)(2,1)S(1)}, u32[]{:S(2)}, u32[]{:S(2)}) %collective-permute-start.5) | collective-permute-done | bytes 262176 | tf_op jit(solution)/shard_map/ppermute | solution.py:73
  61.4 1.1 collective-permute-done.7
  62.5 1.2 copy-done.2
  63.7 1.2 turn.1.weight_ref
  64.9 3.8 %all-to-all-done.rows_hbm = bf16[32,64,512]{2,1,0:T(8,128)(2,1)} async-done(((bf16[32,64,512]{2,1,0:T(8,128)(2,1)}), bf16[32,64,512]{2,1,0:T(8,128)(2,1)}, u32[]{:S(2)}, u32[]{:S(2)}) %all-to-all-start) | async-done | bytes 2097184 | tf_op jit(solution)/shard_map/all_to_all | solution.py:334
  68.6 3.9 %down.1 = bf16[16,64,128]{2,1,0:T(8,128)(2,1)S(1)} custom-call(bf16[32,64,512]{2,1,0:T(8,128)(2,1)} %all-to-all-done.rows_hbm, bf16[4,512,256]{2,1,0:T(8,128)(2,1)S(1)} %turn.1.weight_ref), custom_call_target="tpu_custom_call" | custom-call | flops 536870912 | bytes 3145728 | tf_op jit(solution)/shard_map/down/pallas_call | solution.py:252
  72.5 0.0 copy-start.7
  72.5 4.0 %all-gather = bf16[32,64,128]{2,1,0:T(8,128)(2,1)S(1)} all-gather(bf16[16,64,128]{2,1,0:T(8,128)(2,1)S(1)} %down.1), channel_id=2, replica_groups={{0,1},{2,3},{4,5},{6,7},{8,9},{10,11},{12,13},{14,15},{16,17},{18,19},{..., dimensions={0}, use_global_device_ids=true | all-gather | bytes 786432 | tf_op jit(solution)/shard_map/all_gather | solution.py:340
  76.6 0.0 copy-start.6
  76.6 0.0 copy-start.4
  76.7 14.6 %all_to_all.25 = bf16[8,64,128]{2,1,0:T(8,128)(2,1)S(1)} all-to-all(bf16[8,64,128]{2,1,0:T(8,128)(2,1)S(1)} %fusion.6), channel_id=1, replica_groups={{0,2,4,6,8,10,12,14},{1,3,5,7,9,11,13,15},{16,18,20,22,24,26,28,30},{17..., dimensions={0} | all-to-all | bytes 262144 | tf_op jit(solution)/shard_map/all_to_all | solution.py:334
  91.3 10.4 %all_to_all.26 = bf16[8,64,128]{2,1,0:T(8,128)(2,1)S(1)} all-to-all(bf16[8,64,128]{2,1,0:T(8,128)(2,1)S(1)} %broadcast_in_dim.2), channel_id=1, replica_groups={{0,2,4,6,8,10,12,14},{1,3,5,7,9,11,13,15},{16,18,20,22,24,26,28,30},{17..., dimensions={0} | all-to-all | bytes 262144 | tf_op jit(solution)/shard_map/all_to_all | solution.py:334
  101.8 4.9 %all_gather.11.lowered_ref = bf16[16,64,128]{2,1,0:T(8,128)(2,1)S(1)} all-gather(bf16[8,64,128]{2,1,0:T(8,128)(2,1)S(1)} %all_to_all.26), channel_id=1, replica_groups={{0,1},{2,3},{4,5},{6,7},{8,9},{10,11},{12,13},{14,15},{16,17},{18,19},{..., dimensions={0}, use_global_device_ids=true | all-gather | bytes 393216 | tf_op jit(solution)/shard_map/all_gather | solution.py:349
  106.7 0.0 copy-done.7
  106.7 1.3 up.1
  108.0 6.2 %all-to-all-start.3 = ((bf16[32,64,128]{2,1,0:T(8,128)(2,1)}), bf16[32,64,128]{2,1,0:T(8,128)(2,1)S(1)}, u32[]{:S(2)}, u32[]{:S(2)}) async-start(bf16[32,64,128]{2,1,0:T(8,128)(2,1)} %bitcast.9), calls=%async_computation.3 | async-start | bytes 1048576 | tf_op jit(solution)/shard_map/all_to_all | solution.py:334
  114.2 0.0 copy-done.6
  114.2 0.1 fusion
  114.2 0.0 copy-start.10
  114.3 2.1 %collective-permute-start.9 = (bf16[1024,128]{1,0:T(8,128)(2,1)S(1)}, bf16[1024,128]{1,0:T(8,128)(2,1)S(1)}, u32[]{:S(2)}, u32[]{:S(2)}) collective-permute-start(bf16[1024,128]{1,0:T(8,128)(2,1)S(1)} %fusion), channel_id=1, source_target_pairs={{0,14},{1,15},{2,0},{3,1},{4,2},{5,3},{6,4},{7,5},{8,6},{9,7},{10,... | collective-permute-start | bytes 786440 | tf_op jit(solution)/shard_map/ppermute | solution.py:73
  116.3 0.1 fusion.1
  116.4 3.2 %collective-permute-start.8 = (bf16[1024,128]{1,0:T(8,128)(2,1)S(1)}, bf16[1024,128]{1,0:T(8,128)(2,1)S(1)}, u32[]{:S(2)}, u32[]{:S(2)}) collective-permute-start(bf16[1024,128]{1,0:T(8,128)(2,1)S(1)} %fusion.1), channel_id=1, source_target_pairs={{0,2},{1,3},{2,4},{3,5},{4,6},{5,7},{6,8},{7,9},{8,10},{9,11},{10,... | collective-permute-start | bytes 786440 | tf_op jit(solution)/shard_map/ppermute | solution.py:73
  119.7 0.1 copy.13
  119.7 0.1 reshape.47.accepted_ref
  119.8 3.5 %collective-permute-done.9 = bf16[1024,128]{1,0:T(8,128)(2,1)S(1)} collective-permute-done((bf16[1024,128]{1,0:T(8,128)(2,1)S(1)}, bf16[1024,128]{1,0:T(8,128)(2,1)S(1)}, u32[]{:S(2)}, u32[]{:S(2)}) %collective-permute-start.9) | collective-permute-done | bytes 262176 | tf_op jit(solution)/shard_map/ppermute | solution.py:73
  123.4 3.1 %collective-permute-done.8 = bf16[1024,128]{1,0:T(8,128)(2,1)S(1)} collective-permute-done((bf16[1024,128]{1,0:T(8,128)(2,1)S(1)}, bf16[1024,128]{1,0:T(8,128)(2,1)S(1)}, u32[]{:S(2)}, u32[]{:S(2)}) %collective-permute-start.8) | collective-permute-done | bytes 262176 | tf_op jit(solution)/shard_map/ppermute | solution.py:73
  126.4 0.1 fusion.2.base_ref
  126.5 1.6 %all-to-all-done.3 = bf16[32,64,128]{2,1,0:T(8,128)(2,1)S(1)} async-done(((bf16[32,64,128]{2,1,0:T(8,128)(2,1)}), bf16[32,64,128]{2,1,0:T(8,128)(2,1)S(1)}, u32[]{:S(2)}, u32[]{:S(2)}) %all-to-all-start.3) | async-done | bytes 524320 | tf_op jit(solution)/shard_map/all_to_all | solution.py:334
  128.1 2.4 %finish.1 = (bf16[1024,128]{1,0:T(8,128)(2,1)}, bf16[128,128]{1,0:T(8,128)(2,1)}) custom-call(s32[1,1024]{1,0:T(1,128)S(1)} %copy-done.8, bf16[2048,128]{1,0:T(8,128)(2,1)S(1)} %bitcast.30, f32[1024,128]{1,0:T(8,128)S(1)} %fusion.2.base_ref, s32[1,128]{1,0:T(1,128)S(1)} %reshape.47.accepted_ref), custom_call_target="tpu_custom_call" | custom-call | flops 536870912 | bytes 1348096 | tf_op jit(solution)/shard_map/finish/pallas_call | solution.py:24
  130.5 8.1 %all-to-all-start.4 = ((bf16[32,4,128]{2,1,0:T(4,128)(2,1)}), bf16[32,4,128]{2,1,0:T(4,128)(2,1)S(1)}, u32[]{:S(2)}, u32[]{:S(2)}) async-start(bf16[32,4,128]{2,1,0:T(4,128)(2,1)} %bitcast.14), calls=%async_computation.4 | async-start | bytes 65536 | tf_op jit(solution)/shard_map/all_to_all | solution.py:334
  138.7 0.1 copy.14
  138.8 0.1 reshape.48.targets_ref
  138.9 8.6 %all-to-all-done.4 = bf16[32,4,128]{2,1,0:T(4,128)(2,1)S(1)} async-done(((bf16[32,4,128]{2,1,0:T(4,128)(2,1)}), bf16[32,4,128]{2,1,0:T(4,128)(2,1)S(1)}, u32[]{:S(2)}, u32[]{:S(2)}) %all-to-all-start.4) | async-done | bytes 32800 | tf_op jit(solution)/shard_map/all_to_all | solution.py:334
  147.5 0.8 cache.1
  (12 shorter events, 0.1 us)
Async XLA Ops:
  5.6 14.2 %copy-start = (bf16[512,2048]{1,0:T(8,128)(2,1)S(1)}, bf16[512,2048]{1,0:T(8,128)(2,1)}, u32[]{:S(2)}) copy-start(bf16[512,2048]{1,0:T(8,128)(2,1)} %weight_ref.8) | copy-start | bytes 6291460
  5.6 14.2 %copy-start.1 = (bf16[1024,512]{1,0:T(8,128)(2,1)S(1)}, bf16[1024,512]{1,0:T(8,128)(2,1)}, u32[]{:S(2)}) copy-start(bf16[1024,512]{1,0:T(8,128)(2,1)} %tokens_ref.3) | copy-start | bytes 3145732
  5.6 63.0 %all-to-all-start = ((bf16[32,64,512]{2,1,0:T(8,128)(2,1)}), bf16[32,64,512]{2,1,0:T(8,128)(2,1)}, u32[]{:S(2)}, u32[]{:S(2)}) async-start(bf16[32,64,512]{2,1,0:T(8,128)(2,1)} %bitcast.34), calls=%async_computation | async-start | bytes 4194304 | tf_op jit(solution)/shard_map/all_to_all | solution.py:334
  22.3 25.3 %collective-permute-start = (bf16[5,1024,128]{2,1,0:T(8,128)(2,1)S(1)}, bf16[5,1024,128]{2,1,0:T(8,128)(2,1)S(1)}, u32[]{:S(2)}, u32[]{:S(2)}) collective-permute-start(bf16[5,1024,128]{2,1,0:T(8,128)(2,1)S(1)} %base.5), channel_id=1, source_target_pairs={{0,1},{1,0},{2,3},{3,2},{4,5},{5,4},{6,7},{7,6},{8,9},{9,8},{10,11... | collective-permute-start | bytes 3932168 | tf_op jit(solution)/shard_map/ppermute | solution.py:85
  25.2 4.2 %collective-permute-start.1 = (bf16[3,1024,128]{2,1,0:T(8,128)(2,1)S(1)}, bf16[3,1024,128]{2,1,0:T(8,128)(2,1)S(1)}, u32[]{:S(2)}, u32[]{:S(2)}) collective-permute-start(bf16[3,1024,128]{2,1,0:T(8,128)(2,1)S(1)} %base.4), channel_id=1, source_target_pairs={{0,1},{1,0},{2,3},{3,2},{4,5},{5,4},{6,7},{7,6},{8,9},{9,8},{10,11... | collective-permute-start | bytes 2359304 | tf_op jit(solution)/shard_map/ppermute | solution.py:82
  30.4 9.0 %collective-permute-start.2 = (bf16[512,128]{1,0:T(8,128)(2,1)S(1)}, bf16[512,128]{1,0:T(8,128)(2,1)S(1)}, u32[]{:S(2)}, u32[]{:S(2)}) collective-permute-start(bf16[512,128]{1,0:T(8,128)(2,1)S(1)} %bitcast.33), channel_id=1, source_target_pairs={{0,2},{1,3},{2,4},{3,5},{4,6},{5,7},{6,8},{7,9},{8,10},{9,11},{10,... | collective-permute-start | bytes 393224 | tf_op jit(solution)/shard_map/ppermute | solution.py:73
  33.6 6.6 %collective-permute-start.3 = (bf16[512,128]{1,0:T(8,128)(2,1)S(1)}, bf16[512,128]{1,0:T(8,128)(2,1)S(1)}, u32[]{:S(2)}, u32[]{:S(2)}) collective-permute-start(bf16[512,128]{1,0:T(8,128)(2,1)S(1)} %bitcast.32), channel_id=1, source_target_pairs={{0,14},{1,15},{2,0},{3,1},{4,2},{5,3},{6,4},{7,5},{8,6},{9,7},{10,... | collective-permute-start | bytes 393224 | tf_op jit(solution)/shard_map/ppermute | solution.py:73
  40.3 11.3 %collective-permute-start.4 = (bf16[1024,128]{1,0:T(8,128)(2,1)S(1)}, bf16[1024,128]{1,0:T(8,128)(2,1)S(1)}, u32[]{:S(2)}, u32[]{:S(2)}) collective-permute-start(bf16[1024,128]{1,0:T(8,128)(2,1)S(1)} %get-tuple-element.35), channel_id=1, source_target_pairs={{0,2},{1,3},{2,4},{3,5},{4,6},{5,7},{6,8},{7,9},{8,10},{9,11},{10,... | collective-permute-start | bytes 786440 | tf_op jit(solution)/shard_map/ppermute | solution.py:73
  43.5 10.2 %collective-permute-start.6 = (bf16[1024,128]{1,0:T(8,128)(2,1)S(1)}, bf16[1024,128]{1,0:T(8,128)(2,1)S(1)}, u32[]{:S(2)}, u32[]{:S(2)}) collective-permute-start(bf16[1024,128]{1,0:T(8,128)(2,1)S(1)} %get-tuple-element.37), channel_id=1, source_target_pairs={{0,14},{1,15},{2,0},{3,1},{4,2},{5,3},{6,4},{7,5},{8,6},{9,7},{10,... | collective-permute-start | bytes 786440 | tf_op jit(solution)/shard_map/ppermute | solution.py:73
  49.2 0.7 copy-start.3
  49.9 0.7 copy-start.5
  51.7 9.7 %collective-permute-start.5 = (bf16[1024,128]{1,0:T(8,128)(2,1)S(1)}, bf16[1024,128]{1,0:T(8,128)(2,1)S(1)}, u32[]{:S(2)}, u32[]{:S(2)}) collective-permute-start(bf16[1024,128]{1,0:T(8,128)(2,1)S(1)} %fusion.4), channel_id=1, source_target_pairs={{0,2},{1,3},{2,4},{3,5},{4,6},{5,7},{6,8},{7,9},{8,10},{9,11},{10,... | collective-permute-start | bytes 786440 | tf_op jit(solution)/shard_map/ppermute | solution.py:73
  53.8 8.6 %collective-permute-start.7 = (bf16[1024,128]{1,0:T(8,128)(2,1)S(1)}, bf16[1024,128]{1,0:T(8,128)(2,1)S(1)}, u32[]{:S(2)}, u32[]{:S(2)}) collective-permute-start(bf16[1024,128]{1,0:T(8,128)(2,1)S(1)} %fusion.3), channel_id=1, source_target_pairs={{0,14},{1,15},{2,0},{3,1},{4,2},{5,3},{6,4},{7,5},{8,6},{9,7},{10,... | collective-permute-start | bytes 786440 | tf_op jit(solution)/shard_map/ppermute | solution.py:73
  62.5 1.2 copy-start.2
  72.5 34.2 %copy-start.7 = (bf16[16,64,128]{2,1,0:T(8,128)(2,1)S(1)}, bf16[16,64,128]{2,1,0:T(8,128)(2,1)}, u32[]{:S(2)}) copy-start(bf16[16,64,128]{2,1,0:T(8,128)(2,1)} %weight_ref.9) | copy-start | bytes 786436
  76.6 37.6 %copy-start.6 = (bf16[1,1024,128]{2,1,0:T(8,128)(2,1)S(1)}, bf16[1,1024,128]{2,1,0:T(8,128)(2,1)}, u32[]{:S(2)}) copy-start(bf16[1,1024,128]{2,1,0:T(8,128)(2,1)} %copy-done.5) | copy-start | bytes 786436
  76.6 39.7 %copy-start.4 = (bf16[1,1024,128]{2,1,0:T(8,128)(2,1)S(1)}, bf16[1,1024,128]{2,1,0:T(8,128)(2,1)}, u32[]{:S(2)}) copy-start(bf16[1,1024,128]{2,1,0:T(8,128)(2,1)} %copy-done.3) | copy-start | bytes 786436
  101.8 17.9 %copy-start.9 = (s32[1,32,4]{1,2,0:T(4,128)S(1)}, s32[1,32,4]{1,2,0:T(4,128)}, u32[]{:S(2)}) copy-start(s32[1,32,4]{1,2,0:T(4,128)} %param.12) | copy-start | bytes 1540
  108.0 20.1 %copy-start.8 = (s32[1,1024]{1,0:T(1,128)S(1)}, s32[1,1024]{1,0:T(1,128)}, u32[]{:S(2)}) copy-start(s32[1,1024]{1,0:T(1,128)} %get-tuple-element.26.slots_ref) | copy-start | bytes 12292
  108.0 20.1 %all-to-all-start.3 = ((bf16[32,64,128]{2,1,0:T(8,128)(2,1)}), bf16[32,64,128]{2,1,0:T(8,128)(2,1)S(1)}, u32[]{:S(2)}, u32[]{:S(2)}) async-start(bf16[32,64,128]{2,1,0:T(8,128)(2,1)} %bitcast.9), calls=%async_computation.3 | async-start | bytes 1048576 | tf_op jit(solution)/shard_map/all_to_all | solution.py:334
  114.2 24.4 %copy-start.10 = (s32[32,1,4]{0,2,1:T(4,128)S(1)}, s32[32,1,4]{0,2,1:T(4,128)}, u32[]{:S(2)}) copy-start(s32[32,1,4]{0,2,1:T(4,128)} %param.13) | copy-start | bytes 1540
  114.3 9.1 %collective-permute-start.9 = (bf16[1024,128]{1,0:T(8,128)(2,1)S(1)}, bf16[1024,128]{1,0:T(8,128)(2,1)S(1)}, u32[]{:S(2)}, u32[]{:S(2)}) collective-permute-start(bf16[1024,128]{1,0:T(8,128)(2,1)S(1)} %fusion), channel_id=1, source_target_pairs={{0,14},{1,15},{2,0},{3,1},{4,2},{5,3},{6,4},{7,5},{8,6},{9,7},{10,... | collective-permute-start | bytes 786440 | tf_op jit(solution)/shard_map/ppermute | solution.py:73
  116.4 10.0 %collective-permute-start.8 = (bf16[1024,128]{1,0:T(8,128)(2,1)S(1)}, bf16[1024,128]{1,0:T(8,128)(2,1)S(1)}, u32[]{:S(2)}, u32[]{:S(2)}) collective-permute-start(bf16[1024,128]{1,0:T(8,128)(2,1)S(1)} %fusion.1), channel_id=1, source_target_pairs={{0,2},{1,3},{2,4},{3,5},{4,6},{5,7},{6,8},{7,9},{8,10},{9,11},{10,... | collective-permute-start | bytes 786440 | tf_op jit(solution)/shard_map/ppermute | solution.py:73
  130.5 16.9 %all-to-all-start.4 = ((bf16[32,4,128]{2,1,0:T(4,128)(2,1)}), bf16[32,4,128]{2,1,0:T(4,128)(2,1)S(1)}, u32[]{:S(2)}, u32[]{:S(2)}) async-start(bf16[32,4,128]{2,1,0:T(4,128)(2,1)} %bitcast.14), calls=%async_computation.4 | async-start | bytes 65536 | tf_op jit(solution)/shard_map/all_to_all | solution.py:334

commit v6 on v5

--- a/solution.py
+++ b/solution.py
@@ -150,10 +150,12 @@
     slots_ref[...] = slots
     tokens_in.wait()
     tokens = tokens_ref[...]
-    place = numbers(lax.broadcasted_iota(jnp.int32, (block, rows), 0))
+    place = numbers(lax.broadcasted_iota(jnp.int32, (block // 2, rows), 0))
     out = []
     for i in range(count):
-        chosen = one_hot(place == numbers(slots - i * block))
+        chosen = jnp.concatenate(
+            [one_hot(place == numbers(slots - at)) for at in (i * block, i * block + block // 2)]
+        )
         parts[i] = jnp.dot(chosen, tokens, preferred_element_type=F32).astype(BF16)
         out.append(
             pltpu.make_async_copy(
@@ -168,7 +170,7 @@
 def pack(labels, tokens):
     rows, features = tokens.shape
     slots = ADAPTER_COUNT * CAP
-    block = 256
+    block = 512
     count = slots // block
     return pl.pallas_call(
         pack_kernel,
@@ -214,49 +216,45 @@
 
 
 def down_kernel(rows_hbm, weight_ref, out_ref, rows_ref, sems):
-    sources, slots, features = rows_ref.shape
+    quads, sources, tile, features = rows_ref.shape
     rank = weight_ref.shape[2] // QUAD
-    tile = QUAD * CAP
-    parts = sems.shape[0]
-    share = sources // parts
     rows_in = [
         pltpu.make_async_copy(
-            rows_hbm.at[pl.ds(p * share, share)], rows_ref.at[pl.ds(p * share, share)], sems.at[p]
+            rows_hbm.at[:, pl.ds(quad * tile, tile), :], rows_ref.at[quad], sems.at[quad]
         )
-        for p in range(parts)
+        for quad in range(quads)
     ]
     for copy in rows_in:
         copy.start()
     owner = lax.broadcasted_iota(jnp.int32, (1, tile, 1), 1) // CAP
-    for p in range(parts):
-        rows_in[p].wait()
-        for quad in range(slots // tile):
-            rows = rows_ref[p * share : (p + 1) * share, quad * tile : (quad + 1) * tile, :]
-            product = jnp.dot(
-                rows.reshape(share * tile, features),
-                weight_ref[quad],
-                preferred_element_type=F32,
-            ).reshape(share, tile, QUAD * rank)
-            lowered = jnp.zeros((share, tile, rank), F32)
-            for k in range(QUAD):
-                lowered = jnp.where(owner == k, product[:, :, k * rank : (k + 1) * rank], lowered)
-            lowered = lowered.reshape(share // 2, 2, tile, rank)
-            out_ref[
-                p * share // 2 : (p + 1) * share // 2, quad * tile : (quad + 1) * tile, :
-            ] = jnp.concatenate([lowered[:, 0], lowered[:, 1]], axis=-1).astype(BF16)
+    for quad in range(quads):
+        rows_in[quad].wait()
+        product = jnp.dot(
+            rows_ref[quad].reshape(sources * tile, features),
+            weight_ref[quad],
+            preferred_element_type=F32,
+        ).reshape(sources, tile, QUAD * rank)
+        lowered = jnp.zeros((sources, tile, rank), F32)
+        for k in range(QUAD):
+            lowered = jnp.where(owner == k, product[:, :, k * rank : (k + 1) * rank], lowered)
+        lowered = lowered.reshape(sources // 2, 2, tile, rank)
+        out_ref[:, quad * tile : (quad + 1) * tile, :] = jnp.concatenate(
+            [lowered[:, 0], lowered[:, 1]], axis=-1
+        ).astype(BF16)
 
 
 def lower(received, weight):
     sources, slots, features = received.shape
     rank = weight.shape[2] // QUAD
+    tile = QUAD * CAP
     return pl.pallas_call(
         down_kernel,
         in_specs=[HBM, VMEM],
         out_specs=VMEM,
         out_shape=jax.ShapeDtypeStruct((sources // 2, slots, 2 * rank), BF16),
         scratch_shapes=[
-            pltpu.VMEM(received.shape, BF16),
-            pltpu.SemaphoreType.DMA((4,)),
+            pltpu.VMEM((slots // tile, sources, tile, features), BF16),
+            pltpu.SemaphoreType.DMA((slots // tile,)),
         ],
         compiler_params=pltpu.CompilerParams(vmem_limit_bytes=LIMIT),
         cost_estimate=pl.CostEstimate(
@@ -273,21 +271,19 @@
     rank = wide // 2
     tile = QUAD * CAP
     columns = weight_ref.shape[2]
-    shape = (pairs, tile, QUAD * rank)
+    shape = (2 * pairs, tile, QUAD * rank)
     owner = lax.broadcasted_iota(jnp.int32, shape, 1) // CAP
     lane = lax.broadcasted_iota(jnp.int32, shape, 2) // rank
-    own = (owner == lane).reshape(pairs * tile, QUAD * rank)
+    own = (owner == lane).reshape(2 * pairs * tile, QUAD * rank)
     for quad in range(slots // tile):
         both = lowered_ref[:, quad * tile : (quad + 1) * tile, :].reshape(pairs * tile, wide)
         weight = weight_ref[quad * QUAD : (quad + 1) * QUAD].reshape(QUAD * rank, columns)
+        lowered = jnp.concatenate([both[:, :rank], both[:, rank:]], axis=0)
+        spread = jnp.where(own, jnp.concatenate([lowered] * QUAD, axis=-1), 0)
+        update = jnp.dot(spread.astype(BF16), weight, preferred_element_type=F32).astype(BF16)
+        update = update.reshape(2, pairs, tile, columns)
         for half in range(2):
-            lowered = both[:, half * rank : (half + 1) * rank]
-            spread = jnp.where(own, jnp.concatenate([lowered] * QUAD, axis=-1), 0)
-            out_ref[:, half, quad * tile : (quad + 1) * tile, :] = (
-                jnp.dot(spread.astype(BF16), weight, preferred_element_type=F32)
-                .astype(BF16)
-                .reshape(pairs, tile, columns)
-            )
+            out_ref[:, half, quad * tile : (quad + 1) * tile, :] = update[half]
 
 
 def raise_rank(lowered, weight):

time: 149 us -> 149 us (level)
  no operation moved by 1% of the time
where the time goes in v6:
time: 149 us; the launch traced here: 148 us
  starting transfers between devices  59.2 us (40%)
  blocking collectives  34 us (23%)
  waiting for transfers between devices  30.8 us (21%)
  Pallas kernels  19.7 us (13%)
  local copies, waits for them, and re-layouts  3.06 us (2%)
    all_to_all x3, starting transfers between devices, exchange(): lax.all_to_all(array, axis, split_axis=0, concat_axis=0, tiled=True, axis...  28.4 us
    ppermute x8, starting transfers between devices, shift(): lax.ppermute(array, 'tensor', [(i, (i + step) % groups) for i in range(gr...  26 us
    all_to_all x2, blocking collectives, exchange(): lax.all_to_all(array, axis, split_axis=0, concat_axis=0, tiled=True, axis...  25.1 us
    ppermute x8, waiting for transfers between devices, shift(): lax.ppermute(array, 'tensor', [(i, (i + step) % groups) for i in range(gr...  14.7 us
    all_to_all x3, waiting for transfers between devices, exchange(): lax.all_to_all(array, axis, split_axis=0, concat_axis=0, tiled=True, axis...  13.9 us
    pallas_call x9, Pallas kernels, call(): pl.pallas_call(kernel, out_shape=out_shape, in_specs=[VMEM] * len(operand...  10.8 us
    pallas_call x1, Pallas kernels, pack(): pl.pallas_call(pack_kernel, out_shape=[jax.ShapeDtypeStruct((1, rows), jn...  5.01 us
    all_gather x1, blocking collectives, sum_over_tensor(): lax.all_gather(mine, 'tensor', axis=0, axis_index_groups=pairs, tiled=True)  4.93 us
  transfers between devices with their start and end apart: 13, of which 12 were waited for; matrix products, arithmetic and copies ran while one was open for 1% of the time, Pallas kernels for 4%

profile of v6, /device:TPU:1, one launch (start us, length us, event | category | flops | bytes accessed | tf_op | source)
XLA Modules:
  0.0 148.3 jit_solution(10155122788911969827)
XLA Ops:
  0.6 5.0 %pack.1 = (s32[1,1024]{1,0:T(1,128)}, bf16[2048,512]{1,0:T(8,128)(2,1)}) custom-call(s32[1,1024]{1,0:T(1,128)} %bitcast.36, bf16[1024,512]{1,0:T(8,128)(2,1)} %tokens_ref.3), custom_call_target="tpu_custom_call" | custom-call | flops 2147483648 | bytes 3145728 | tf_op jit(solution)/shard_map/pack/pallas_call | solution.py:175
  5.6 0.0 copy-start
  5.7 0.0 copy-start.1
  5.7 14.1 %all-to-all-start = ((bf16[32,64,512]{2,1,0:T(8,128)(2,1)}), bf16[32,64,512]{2,1,0:T(8,128)(2,1)}, u32[]{:S(2)}, u32[]{:S(2)}) async-start(bf16[32,64,512]{2,1,0:T(8,128)(2,1)} %bitcast.34), calls=%async_computation | async-start | bytes 4194304 | tf_op jit(solution)/shard_map/all_to_all | solution.py:330
  19.8 0.0 copy-done
  19.8 0.0 copy-done.1
  19.8 1.0 base.4
  20.8 1.5 %base.5 = bf16[5,1024,128]{2,1,0:T(8,128)(2,1)S(1)} custom-call(bf16[1024,512]{1,0:T(8,128)(2,1)S(1)} %copy-done.1, bf16[512,2048]{1,0:T(8,128)(2,1)S(1)} %copy-done), custom_call_target="tpu_custom_call" | custom-call | flops 671088640 | bytes 4456448 | tf_op jit(solution)/shard_map/base/pallas_call | solution.py:24
  22.4 2.9 %collective-permute-start = (bf16[5,1024,128]{2,1,0:T(8,128)(2,1)S(1)}, bf16[5,1024,128]{2,1,0:T(8,128)(2,1)S(1)}, u32[]{:S(2)}, u32[]{:S(2)}) collective-permute-start(bf16[5,1024,128]{2,1,0:T(8,128)(2,1)S(1)} %base.5), channel_id=1, source_target_pairs={{0,1},{1,0},{2,3},{3,2},{4,5},{5,4},{6,7},{7,6},{8,9},{9,8},{10,11... | collective-permute-start | bytes 3932168 | tf_op jit(solution)/shard_map/ppermute | solution.py:85
  25.3 1.9 %collective-permute-start.1 = (bf16[3,1024,128]{2,1,0:T(8,128)(2,1)S(1)}, bf16[3,1024,128]{2,1,0:T(8,128)(2,1)S(1)}, u32[]{:S(2)}, u32[]{:S(2)}) collective-permute-start(bf16[3,1024,128]{2,1,0:T(8,128)(2,1)S(1)} %base.4), channel_id=1, source_target_pairs={{0,1},{1,0},{2,3},{3,2},{4,5},{5,4},{6,7},{7,6},{8,9},{9,8},{10,11... | collective-permute-start | bytes 2359304 | tf_op jit(solution)/shard_map/ppermute | solution.py:82
  27.2 2.3 %collective-permute-done.1.rest_0_ = bf16[3,1024,128]{2,1,0:T(8,128)(2,1)S(1)} collective-permute-done((bf16[3,1024,128]{2,1,0:T(8,128)(2,1)S(1)}, bf16[3,1024,128]{2,1,0:T(8,128)(2,1)S(1)}, u32[]{:S(2)}, u32[]{:S(2)}) %collective-permute-start.1) | collective-permute-done | bytes 786464 | tf_op jit(solution)/shard_map/ppermute | solution.py:82
  29.5 1.0 base.7
  30.5 3.2 %collective-permute-start.2 = (bf16[512,128]{1,0:T(8,128)(2,1)S(1)}, bf16[512,128]{1,0:T(8,128)(2,1)S(1)}, u32[]{:S(2)}, u32[]{:S(2)}) collective-permute-start(bf16[512,128]{1,0:T(8,128)(2,1)S(1)} %bitcast.33), channel_id=1, source_target_pairs={{0,2},{1,3},{2,4},{3,5},{4,6},{5,7},{6,8},{7,9},{8,10},{9,11},{10,... | collective-permute-start | bytes 393224 | tf_op jit(solution)/shard_map/ppermute | solution.py:73
  33.7 3.8 %collective-permute-start.3 = (bf16[512,128]{1,0:T(8,128)(2,1)S(1)}, bf16[512,128]{1,0:T(8,128)(2,1)S(1)}, u32[]{:S(2)}, u32[]{:S(2)}) collective-permute-start(bf16[512,128]{1,0:T(8,128)(2,1)S(1)} %bitcast.32), channel_id=1, source_target_pairs={{0,14},{1,15},{2,0},{3,1},{4,2},{5,3},{6,4},{7,5},{8,6},{9,7},{10,... | collective-permute-start | bytes 393224 | tf_op jit(solution)/shard_map/ppermute | solution.py:73
  37.5 1.9 %collective-permute-done.2.up_ref = bf16[512,128]{1,0:T(8,128)(2,1)S(1)} collective-permute-done((bf16[512,128]{1,0:T(8,128)(2,1)S(1)}, bf16[512,128]{1,0:T(8,128)(2,1)S(1)}, u32[]{:S(2)}, u32[]{:S(2)}) %collective-permute-start.2) | collective-permute-done | bytes 131104 | tf_op jit(solution)/shard_map/ppermute | solution.py:73
  39.4 0.9 collective-permute-done.3.down_ref
  40.3 0.1 ring.1
  40.4 3.2 %collective-permute-start.4 = (bf16[1024,128]{1,0:T(8,128)(2,1)S(1)}, bf16[1024,128]{1,0:T(8,128)(2,1)S(1)}, u32[]{:S(2)}, u32[]{:S(2)}) collective-permute-start(bf16[1024,128]{1,0:T(8,128)(2,1)S(1)} %get-tuple-element.35), channel_id=1, source_target_pairs={{0,2},{1,3},{2,4},{3,5},{4,6},{5,7},{6,8},{7,9},{8,10},{9,11},{10,... | collective-permute-start | bytes 786440 | tf_op jit(solution)/shard_map/ppermute | solution.py:73
  43.6 4.1 %collective-permute-start.6 = (bf16[1024,128]{1,0:T(8,128)(2,1)S(1)}, bf16[1024,128]{1,0:T(8,128)(2,1)S(1)}, u32[]{:S(2)}, u32[]{:S(2)}) collective-permute-start(bf16[1024,128]{1,0:T(8,128)(2,1)S(1)} %get-tuple-element.37), channel_id=1, source_target_pairs={{0,14},{1,15},{2,0},{3,1},{4,2},{5,3},{6,4},{7,5},{8,6},{9,7},{10,... | collective-permute-start | bytes 786440 | tf_op jit(solution)/shard_map/ppermute | solution.py:73
  47.7 0.0 collective-permute-done.rest_0_
  47.7 1.6 %base.6 = (bf16[1,1024,128]{2,1,0:T(8,128)(2,1)S(1)}, bf16[1,1024,128]{2,1,0:T(8,128)(2,1)S(1)}, bf16[1,1024,128]{2,1,0:T(8,128)(2,1)S(1)}, bf16[1,1024,128]{2,1,0:T(8,128)(2,1)S(1)}, bf16[1,1024,128]{2,1,0:T(8,128)(2,1)S(1)}) custom-call(bf16[1024,512]{1,0:T(8,128)(2,1)S(1)} %copy-done.1, bf16[512,2048]{1,0:T(8,128)(2,1)S(1)} %copy-done, ...), custom_call_target="tpu_custom_call" | custom-call | flops 671088640 | bytes 5767168 | tf_op jit(solution)/shard_map/base/pallas_call | solution.py:24
  49.2 0.0 copy-start.3
  49.3 0.7 copy-done.3
  50.0 0.7 copy-done.5
  50.7 1.0 collective-permute-done.4
  51.7 0.1 fusion.4
  51.7 1.9 %collective-permute-start.5 = (bf16[1024,128]{1,0:T(8,128)(2,1)S(1)}, bf16[1024,128]{1,0:T(8,128)(2,1)S(1)}, u32[]{:S(2)}, u32[]{:S(2)}) collective-permute-start(bf16[1024,128]{1,0:T(8,128)(2,1)S(1)} %fusion.4), channel_id=1, source_target_pairs={{0,2},{1,3},{2,4},{3,5},{4,6},{5,7},{6,8},{7,9},{8,10},{9,11},{10,... | collective-permute-start | bytes 786440 | tf_op jit(solution)/shard_map/ppermute | solution.py:73
  53.7 0.1 collective-permute-done.6
  53.8 0.1 fusion.3
  53.9 4.5 %collective-permute-start.7 = (bf16[1024,128]{1,0:T(8,128)(2,1)S(1)}, bf16[1024,128]{1,0:T(8,128)(2,1)S(1)}, u32[]{:S(2)}, u32[]{:S(2)}) collective-permute-start(bf16[1024,128]{1,0:T(8,128)(2,1)S(1)} %fusion.3), channel_id=1, source_target_pairs={{0,14},{1,15},{2,0},{3,1},{4,2},{5,3},{6,4},{7,5},{8,6},{9,7},{10,... | collective-permute-start | bytes 786440 | tf_op jit(solution)/shard_map/ppermute | solution.py:73
  58.4 3.1 %collective-permute-done.5 = bf16[1024,128]{1,0:T(8,128)(2,1)S(1)} collective-permute-done((bf16[1024,128]{1,0:T(8,128)(2,1)S(1)}, bf16[1024,128]{1,0:T(8,128)(2,1)S(1)}, u32[]{:S(2)}, u32[]{:S(2)}) %collective-permute-start.5) | collective-permute-done | bytes 262176 | tf_op jit(solution)/shard_map/ppermute | solution.py:73
  61.4 1.1 collective-permute-done.7
  62.5 1.2 copy-done.2
  63.7 1.2 turn.1.weight_ref
  64.9 3.8 %all-to-all-done.rows_hbm = bf16[32,64,512]{2,1,0:T(8,128)(2,1)} async-done(((bf16[32,64,512]{2,1,0:T(8,128)(2,1)}), bf16[32,64,512]{2,1,0:T(8,128)(2,1)}, u32[]{:S(2)}, u32[]{:S(2)}) %all-to-all-start) | async-done | bytes 2097184 | tf_op jit(solution)/shard_map/all_to_all | solution.py:330
  68.7 3.9 %down.1 = bf16[16,64,128]{2,1,0:T(8,128)(2,1)S(1)} custom-call(bf16[32,64,512]{2,1,0:T(8,128)(2,1)} %all-to-all-done.rows_hbm, bf16[4,512,256]{2,1,0:T(8,128)(2,1)S(1)} %turn.1.weight_ref), custom_call_target="tpu_custom_call" | custom-call | flops 536870912 | bytes 3145728 | tf_op jit(solution)/shard_map/down/pallas_call | solution.py:250
  72.5 0.0 copy-start.7
  72.6 4.0 %all-gather = bf16[32,64,128]{2,1,0:T(8,128)(2,1)S(1)} all-gather(bf16[16,64,128]{2,1,0:T(8,128)(2,1)S(1)} %down.1), channel_id=2, replica_groups={{0,1},{2,3},{4,5},{6,7},{8,9},{10,11},{12,13},{14,15},{16,17},{18,19},{..., dimensions={0}, use_global_device_ids=true | all-gather | bytes 786432 | tf_op jit(solution)/shard_map/all_gather | solution.py:336
  76.6 0.0 copy-start.6
  76.7 0.0 copy-start.4
  76.7 14.6 %all_to_all.25 = bf16[8,64,128]{2,1,0:T(8,128)(2,1)S(1)} all-to-all(bf16[8,64,128]{2,1,0:T(8,128)(2,1)S(1)} %fusion.6), channel_id=1, replica_groups={{0,2,4,6,8,10,12,14},{1,3,5,7,9,11,13,15},{16,18,20,22,24,26,28,30},{17..., dimensions={0} | all-to-all | bytes 262144 | tf_op jit(solution)/shard_map/all_to_all | solution.py:330
  91.4 10.4 %all_to_all.26 = bf16[8,64,128]{2,1,0:T(8,128)(2,1)S(1)} all-to-all(bf16[8,64,128]{2,1,0:T(8,128)(2,1)S(1)} %broadcast_in_dim.2), channel_id=1, replica_groups={{0,2,4,6,8,10,12,14},{1,3,5,7,9,11,13,15},{16,18,20,22,24,26,28,30},{17..., dimensions={0} | all-to-all | bytes 262144 | tf_op jit(solution)/shard_map/all_to_all | solution.py:330
  101.8 4.9 %all_gather.11.lowered_ref = bf16[16,64,128]{2,1,0:T(8,128)(2,1)S(1)} all-gather(bf16[8,64,128]{2,1,0:T(8,128)(2,1)S(1)} %all_to_all.26), channel_id=1, replica_groups={{0,1},{2,3},{4,5},{6,7},{8,9},{10,11},{12,13},{14,15},{16,17},{18,19},{..., dimensions={0}, use_global_device_ids=true | all-gather | bytes 393216 | tf_op jit(solution)/shard_map/all_gather | solution.py:345
  106.7 0.0 copy-done.7
  106.7 1.3 up.1
  108.0 6.2 %all-to-all-start.3 = ((bf16[32,64,128]{2,1,0:T(8,128)(2,1)}), bf16[32,64,128]{2,1,0:T(8,128)(2,1)S(1)}, u32[]{:S(2)}, u32[]{:S(2)}) async-start(bf16[32,64,128]{2,1,0:T(8,128)(2,1)} %bitcast.9), calls=%async_computation.3 | async-start | bytes 1048576 | tf_op jit(solution)/shard_map/all_to_all | solution.py:330
  114.2 0.1 fusion
  114.3 0.0 copy-start.10
  114.3 2.1 %collective-permute-start.9 = (bf16[1024,128]{1,0:T(8,128)(2,1)S(1)}, bf16[1024,128]{1,0:T(8,128)(2,1)S(1)}, u32[]{:S(2)}, u32[]{:S(2)}) collective-permute-start(bf16[1024,128]{1,0:T(8,128)(2,1)S(1)} %fusion), channel_id=1, source_target_pairs={{0,14},{1,15},{2,0},{3,1},{4,2},{5,3},{6,4},{7,5},{8,6},{9,7},{10,... | collective-permute-start | bytes 786440 | tf_op jit(solution)/shard_map/ppermute | solution.py:73
  116.4 0.1 fusion.1
  116.5 3.2 %collective-permute-start.8 = (bf16[1024,128]{1,0:T(8,128)(2,1)S(1)}, bf16[1024,128]{1,0:T(8,128)(2,1)S(1)}, u32[]{:S(2)}, u32[]{:S(2)}) collective-permute-start(bf16[1024,128]{1,0:T(8,128)(2,1)S(1)} %fusion.1), channel_id=1, source_target_pairs={{0,2},{1,3},{2,4},{3,5},{4,6},{5,7},{6,8},{7,9},{8,10},{9,11},{10,... | collective-permute-start | bytes 786440 | tf_op jit(solution)/shard_map/ppermute | solution.py:73
  119.7 0.1 copy.13
  119.8 0.1 reshape.47.accepted_ref
  119.9 3.5 %collective-permute-done.9 = bf16[1024,128]{1,0:T(8,128)(2,1)S(1)} collective-permute-done((bf16[1024,128]{1,0:T(8,128)(2,1)S(1)}, bf16[1024,128]{1,0:T(8,128)(2,1)S(1)}, u32[]{:S(2)}, u32[]{:S(2)}) %collective-permute-start.9) | collective-permute-done | bytes 262176 | tf_op jit(solution)/shard_map/ppermute | solution.py:73
  123.4 3.1 %collective-permute-done.8 = bf16[1024,128]{1,0:T(8,128)(2,1)S(1)} collective-permute-done((bf16[1024,128]{1,0:T(8,128)(2,1)S(1)}, bf16[1024,128]{1,0:T(8,128)(2,1)S(1)}, u32[]{:S(2)}, u32[]{:S(2)}) %collective-permute-start.8) | collective-permute-done | bytes 262176 | tf_op jit(solution)/shard_map/ppermute | solution.py:73
  126.5 0.1 fusion.2.base_ref
  126.6 1.6 %all-to-all-done.3 = bf16[32,64,128]{2,1,0:T(8,128)(2,1)S(1)} async-done(((bf16[32,64,128]{2,1,0:T(8,128)(2,1)}), bf16[32,64,128]{2,1,0:T(8,128)(2,1)S(1)}, u32[]{:S(2)}, u32[]{:S(2)}) %all-to-all-start.3) | async-done | bytes 524320 | tf_op jit(solution)/shard_map/all_to_all | solution.py:330
  128.2 2.4 %finish.1 = (bf16[1024,128]{1,0:T(8,128)(2,1)}, bf16[128,128]{1,0:T(8,128)(2,1)}) custom-call(s32[1,1024]{1,0:T(1,128)S(1)} %copy-done.8, bf16[2048,128]{1,0:T(8,128)(2,1)S(1)} %bitcast.30, f32[1024,128]{1,0:T(8,128)S(1)} %fusion.2.base_ref, s32[1,128]{1,0:T(1,128)S(1)} %reshape.47.accepted_ref), custom_call_target="tpu_custom_call" | custom-call | flops 536870912 | bytes 1348096 | tf_op jit(solution)/shard_map/finish/pallas_call | solution.py:24
  130.6 8.1 %all-to-all-start.4 = ((bf16[32,4,128]{2,1,0:T(4,128)(2,1)}), bf16[32,4,128]{2,1,0:T(4,128)(2,1)S(1)}, u32[]{:S(2)}, u32[]{:S(2)}) async-start(bf16[32,4,128]{2,1,0:T(4,128)(2,1)} %bitcast.14), calls=%async_computation.4 | async-start | bytes 65536 | tf_op jit(solution)/shard_map/all_to_all | solution.py:330
  138.7 0.0 copy-done.10
  138.7 0.1 copy.14
  138.8 0.1 reshape.48.targets_ref
  138.9 8.6 %all-to-all-done.4 = bf16[32,4,128]{2,1,0:T(4,128)(2,1)S(1)} async-done(((bf16[32,4,128]{2,1,0:T(4,128)(2,1)}), bf16[32,4,128]{2,1,0:T(4,128)(2,1)S(1)}, u32[]{:S(2)}, u32[]{:S(2)}) %all-to-all-start.4) | async-done | bytes 32800 | tf_op jit(solution)/shard_map/all_to_all | solution.py:330
  147.5 0.8 cache.1
  (12 shorter events, 0.1 us)
Async XLA Ops:
  5.6 14.2 %copy-start = (bf16[512,2048]{1,0:T(8,128)(2,1)S(1)}, bf16[512,2048]{1,0:T(8,128)(2,1)}, u32[]{:S(2)}) copy-start(bf16[512,2048]{1,0:T(8,128)(2,1)} %weight_ref.8) | copy-start | bytes 6291460
  5.7 14.2 %copy-start.1 = (bf16[1024,512]{1,0:T(8,128)(2,1)S(1)}, bf16[1024,512]{1,0:T(8,128)(2,1)}, u32[]{:S(2)}) copy-start(bf16[1024,512]{1,0:T(8,128)(2,1)} %tokens_ref.3) | copy-start | bytes 3145732
  5.7 63.0 %all-to-all-start = ((bf16[32,64,512]{2,1,0:T(8,128)(2,1)}), bf16[32,64,512]{2,1,0:T(8,128)(2,1)}, u32[]{:S(2)}, u32[]{:S(2)}) async-start(bf16[32,64,512]{2,1,0:T(8,128)(2,1)} %bitcast.34), calls=%async_computation | async-start | bytes 4194304 | tf_op jit(solution)/shard_map/all_to_all | solution.py:330
  22.4 25.3 %collective-permute-start = (bf16[5,1024,128]{2,1,0:T(8,128)(2,1)S(1)}, bf16[5,1024,128]{2,1,0:T(8,128)(2,1)S(1)}, u32[]{:S(2)}, u32[]{:S(2)}) collective-permute-start(bf16[5,1024,128]{2,1,0:T(8,128)(2,1)S(1)} %base.5), channel_id=1, source_target_pairs={{0,1},{1,0},{2,3},{3,2},{4,5},{5,4},{6,7},{7,6},{8,9},{9,8},{10,11... | collective-permute-start | bytes 3932168 | tf_op jit(solution)/shard_map/ppermute | solution.py:85
  25.3 4.2 %collective-permute-start.1 = (bf16[3,1024,128]{2,1,0:T(8,128)(2,1)S(1)}, bf16[3,1024,128]{2,1,0:T(8,128)(2,1)S(1)}, u32[]{:S(2)}, u32[]{:S(2)}) collective-permute-start(bf16[3,1024,128]{2,1,0:T(8,128)(2,1)S(1)} %base.4), channel_id=1, source_target_pairs={{0,1},{1,0},{2,3},{3,2},{4,5},{5,4},{6,7},{7,6},{8,9},{9,8},{10,11... | collective-permute-start | bytes 2359304 | tf_op jit(solution)/shard_map/ppermute | solution.py:82
  30.5 9.0 %collective-permute-start.2 = (bf16[512,128]{1,0:T(8,128)(2,1)S(1)}, bf16[512,128]{1,0:T(8,128)(2,1)S(1)}, u32[]{:S(2)}, u32[]{:S(2)}) collective-permute-start(bf16[512,128]{1,0:T(8,128)(2,1)S(1)} %bitcast.33), channel_id=1, source_target_pairs={{0,2},{1,3},{2,4},{3,5},{4,6},{5,7},{6,8},{7,9},{8,10},{9,11},{10,... | collective-permute-start | bytes 393224 | tf_op jit(solution)/shard_map/ppermute | solution.py:73
  33.7 6.6 %collective-permute-start.3 = (bf16[512,128]{1,0:T(8,128)(2,1)S(1)}, bf16[512,128]{1,0:T(8,128)(2,1)S(1)}, u32[]{:S(2)}, u32[]{:S(2)}) collective-permute-start(bf16[512,128]{1,0:T(8,128)(2,1)S(1)} %bitcast.32), channel_id=1, source_target_pairs={{0,14},{1,15},{2,0},{3,1},{4,2},{5,3},{6,4},{7,5},{8,6},{9,7},{10,... | collective-permute-start | bytes 393224 | tf_op jit(solution)/shard_map/ppermute | solution.py:73
  40.4 11.3 %collective-permute-start.4 = (bf16[1024,128]{1,0:T(8,128)(2,1)S(1)}, bf16[1024,128]{1,0:T(8,128)(2,1)S(1)}, u32[]{:S(2)}, u32[]{:S(2)}) collective-permute-start(bf16[1024,128]{1,0:T(8,128)(2,1)S(1)} %get-tuple-element.35), channel_id=1, source_target_pairs={{0,2},{1,3},{2,4},{3,5},{4,6},{5,7},{6,8},{7,9},{8,10},{9,11},{10,... | collective-permute-start | bytes 786440 | tf_op jit(solution)/shard_map/ppermute | solution.py:73
  43.6 10.2 %collective-permute-start.6 = (bf16[1024,128]{1,0:T(8,128)(2,1)S(1)}, bf16[1024,128]{1,0:T(8,128)(2,1)S(1)}, u32[]{:S(2)}, u32[]{:S(2)}) collective-permute-start(bf16[1024,128]{1,0:T(8,128)(2,1)S(1)} %get-tuple-element.37), channel_id=1, source_target_pairs={{0,14},{1,15},{2,0},{3,1},{4,2},{5,3},{6,4},{7,5},{8,6},{9,7},{10,... | collective-permute-start | bytes 786440 | tf_op jit(solution)/shard_map/ppermute | solution.py:73
  49.2 0.7 copy-start.3
  49.9 0.7 copy-start.5
  51.7 9.7 %collective-permute-start.5 = (bf16[1024,128]{1,0:T(8,128)(2,1)S(1)}, bf16[1024,128]{1,0:T(8,128)(2,1)S(1)}, u32[]{:S(2)}, u32[]{:S(2)}) collective-permute-start(bf16[1024,128]{1,0:T(8,128)(2,1)S(1)} %fusion.4), channel_id=1, source_target_pairs={{0,2},{1,3},{2,4},{3,5},{4,6},{5,7},{6,8},{7,9},{8,10},{9,11},{10,... | collective-permute-start | bytes 786440 | tf_op jit(solution)/shard_map/ppermute | solution.py:73
  53.9 8.6 %collective-permute-start.7 = (bf16[1024,128]{1,0:T(8,128)(2,1)S(1)}, bf16[1024,128]{1,0:T(8,128)(2,1)S(1)}, u32[]{:S(2)}, u32[]{:S(2)}) collective-permute-start(bf16[1024,128]{1,0:T(8,128)(2,1)S(1)} %fusion.3), channel_id=1, source_target_pairs={{0,14},{1,15},{2,0},{3,1},{4,2},{5,3},{6,4},{7,5},{8,6},{9,7},{10,... | collective-permute-start | bytes 786440 | tf_op jit(solution)/shard_map/ppermute | solution.py:73
  62.5 1.2 copy-start.2
  72.5 34.2 %copy-start.7 = (bf16[16,64,128]{2,1,0:T(8,128)(2,1)S(1)}, bf16[16,64,128]{2,1,0:T(8,128)(2,1)}, u32[]{:S(2)}) copy-start(bf16[16,64,128]{2,1,0:T(8,128)(2,1)} %weight_ref.9) | copy-start | bytes 786436
  76.6 37.6 %copy-start.6 = (bf16[1,1024,128]{2,1,0:T(8,128)(2,1)S(1)}, bf16[1,1024,128]{2,1,0:T(8,128)(2,1)}, u32[]{:S(2)}) copy-start(bf16[1,1024,128]{2,1,0:T(8,128)(2,1)} %copy-done.5) | copy-start | bytes 786436
  76.7 39.7 %copy-start.4 = (bf16[1,1024,128]{2,1,0:T(8,128)(2,1)S(1)}, bf16[1,1024,128]{2,1,0:T(8,128)(2,1)}, u32[]{:S(2)}) copy-start(bf16[1,1024,128]{2,1,0:T(8,128)(2,1)} %copy-done.3) | copy-start | bytes 786436
  101.8 17.9 %copy-start.9 = (s32[1,32,4]{1,2,0:T(4,128)S(1)}, s32[1,32,4]{1,2,0:T(4,128)}, u32[]{:S(2)}) copy-start(s32[1,32,4]{1,2,0:T(4,128)} %param.12) | copy-start | bytes 1540
  108.0 20.1 %copy-start.8 = (s32[1,1024]{1,0:T(1,128)S(1)}, s32[1,1024]{1,0:T(1,128)}, u32[]{:S(2)}) copy-start(s32[1,1024]{1,0:T(1,128)} %get-tuple-element.26.slots_ref) | copy-start | bytes 12292
  108.0 20.1 %all-to-all-start.3 = ((bf16[32,64,128]{2,1,0:T(8,128)(2,1)}), bf16[32,64,128]{2,1,0:T(8,128)(2,1)S(1)}, u32[]{:S(2)}, u32[]{:S(2)}) async-start(bf16[32,64,128]{2,1,0:T(8,128)(2,1)} %bitcast.9), calls=%async_computation.3 | async-start | bytes 1048576 | tf_op jit(solution)/shard_map/all_to_all | solution.py:330
  114.3 24.4 %copy-start.10 = (s32[32,1,4]{0,2,1:T(4,128)S(1)}, s32[32,1,4]{0,2,1:T(4,128)}, u32[]{:S(2)}) copy-start(s32[32,1,4]{0,2,1:T(4,128)} %param.13) | copy-start | bytes 1540
  114.3 9.1 %collective-permute-start.9 = (bf16[1024,128]{1,0:T(8,128)(2,1)S(1)}, bf16[1024,128]{1,0:T(8,128)(2,1)S(1)}, u32[]{:S(2)}, u32[]{:S(2)}) collective-permute-start(bf16[1024,128]{1,0:T(8,128)(2,1)S(1)} %fusion), channel_id=1, source_target_pairs={{0,14},{1,15},{2,0},{3,1},{4,2},{5,3},{6,4},{7,5},{8,6},{9,7},{10,... | collective-permute-start | bytes 786440 | tf_op jit(solution)/shard_map/ppermute | solution.py:73
  116.5 10.0 %collective-permute-start.8 = (bf16[1024,128]{1,0:T(8,128)(2,1)S(1)}, bf16[1024,128]{1,0:T(8,128)(2,1)S(1)}, u32[]{:S(2)}, u32[]{:S(2)}) collective-permute-start(bf16[1024,128]{1,0:T(8,128)(2,1)S(1)} %fusion.1), channel_id=1, source_target_pairs={{0,2},{1,3},{2,4},{3,5},{4,6},{5,7},{6,8},{7,9},{8,10},{9,11},{10,... | collective-permute-start | bytes 786440 | tf_op jit(solution)/shard_map/ppermute | solution.py:73
  130.6 16.9 %all-to-all-start.4 = ((bf16[32,4,128]{2,1,0:T(4,128)(2,1)}), bf16[32,4,128]{2,1,0:T(4,128)(2,1)S(1)}, u32[]{:S(2)}, u32[]{:S(2)}) async-start(bf16[32,4,128]{2,1,0:T(4,128)(2,1)} %bitcast.14), calls=%async_computation.4 | async-start | bytes 65536 | tf_op jit(solution)/shard_map/all_to_all | solution.py:330

commit v7 on v6

--- a/solution.py
+++ b/solution.py
@@ -149,22 +149,25 @@
     slots = labels * CAP + jnp.concatenate(ranks, axis=1)
     slots_ref[...] = slots
     tokens_in.wait()
-    tokens = tokens_ref[...]
     place = numbers(lax.broadcasted_iota(jnp.int32, (block // 2, rows), 0))
-    out = []
-    for i in range(count):
+
+    def copy_out(i):
+        at = pl.multiple_of(i * block, block)
+        return pltpu.make_async_copy(
+            parts.at[i], packed_hbm.at[pl.ds(at, block), :], sems.at[i]
+        )
+
+    @pl.loop(0, count)
+    def _(i):
         chosen = jnp.concatenate(
-            [one_hot(place == numbers(slots - at)) for at in (i * block, i * block + block // 2)]
+            [one_hot(place == numbers(slots - (i * block + at))) for at in (0, block // 2)]
         )
-        parts[i] = jnp.dot(chosen, tokens, preferred_element_type=F32).astype(BF16)
-        out.append(
-            pltpu.make_async_copy(
-                parts.at[i], packed_hbm.at[pl.ds(i * block, block), :], sems.at[i]
-            )
-        )
-        out[-1].start()
-    for copy in out:
-        copy.wait()
+        parts[i] = jnp.dot(chosen, tokens_ref[...], preferred_element_type=F32).astype(BF16)
+        copy_out(i).start()
+
+    @pl.loop(0, count)
+    def _(i):
+        copy_out(i).wait()
 
 
 def pack(labels, tokens):
@@ -226,21 +229,28 @@
     ]
     for copy in rows_in:
         copy.start()
-    owner = lax.broadcasted_iota(jnp.int32, (1, tile, 1), 1) // CAP
+    wide = QUAD * rank
+    shape = (sources, tile, wide)
+    owner = lax.broadcasted_iota(jnp.int32, shape, 1) // CAP
+    own = owner == lax.broadcasted_iota(jnp.int32, shape, 2) // rank
+    shape = (2 * wide, 2 * rank)
+    line, lane = lax.broadcasted_iota(jnp.int32, shape, 0), lax.broadcasted_iota(jnp.int32, shape, 1)
+    fold = jnp.where(line // wide * rank + line % rank == lane, 1.0, 0.0).astype(BF16)
     for quad in range(quads):
         rows_in[quad].wait()
         product = jnp.dot(
             rows_ref[quad].reshape(sources * tile, features),
             weight_ref[quad],
             preferred_element_type=F32,
-        ).reshape(sources, tile, QUAD * rank)
-        lowered = jnp.zeros((sources, tile, rank), F32)
-        for k in range(QUAD):
-            lowered = jnp.where(owner == k, product[:, :, k * rank : (k + 1) * rank], lowered)
-        lowered = lowered.reshape(sources // 2, 2, tile, rank)
-        out_ref[:, quad * tile : (quad + 1) * tile, :] = jnp.concatenate(
-            [lowered[:, 0], lowered[:, 1]], axis=-1
-        ).astype(BF16)
+        ).reshape(sources, tile, wide)
+        lowered = jnp.where(own, product, 0.0).astype(BF16).reshape(sources // 2, 2, tile, wide)
+        lowered = jnp.concatenate([lowered[:, 0], lowered[:, 1]], axis=-1)
+        lowered = lowered.reshape(sources // 2 * tile, 2 * wide)
+        out_ref[:, quad * tile : (quad + 1) * tile, :] = (
+            jnp.dot(lowered, fold, preferred_element_type=F32)
+            .astype(BF16)
+            .reshape(sources // 2, tile, 2 * rank)
+        )
 
 
 def lower(received, weight):
@@ -298,10 +308,34 @@
     )
 
 
-def finish_kernel(slots_ref, returned_ref, base_ref, accepted_ref, out_ref, chosen_ref):
+def as_column(row):
+    return jnp.transpose(jnp.broadcast_to(row, (8, row.shape[1])))[:, 0:1]
+
+
+def prepare_kernel(slots_ref, accepted_ref, base_ref, take_ref, base_out):
+    count, places = take_ref.shape
+    rows = base_ref.shape[0]
+    mine = lax.broadcasted_iota(jnp.int32, (count, rows), 1) == as_column(accepted_ref[...])
+    slot = jnp.sum(jnp.where(mine, slots_ref[...], 0), axis=1, keepdims=True)
+    place = lax.broadcasted_iota(jnp.int32, (count, places), 1)
+    take_ref[...] = jnp.where(place == slot, 1.0, 0.0).astype(BF16)
+    base_out[...] = jnp.dot(
+        jnp.where(mine, 1.0, 0.0),
+        base_ref[...],
+        preferred_element_type=F32,
+        precision=lax.Precision.HIGHEST,
+    )
+
+
+def choose_kernel(take_ref, returned_ref, base_ref, chosen_ref):
+    update = jnp.dot(take_ref[...], returned_ref[...], preferred_element_type=F32)
+    chosen_ref[...] = (base_ref[...] + update).astype(BF16)
+
+
+def finish_kernel(slots_ref, returned_ref, base_ref, out_ref):
     rows = out_ref.shape[0]
     places = returned_ref.shape[0]
-    column = jnp.transpose(jnp.broadcast_to(slots_ref[...], (8, rows)))[:, 0:1]
+    column = as_column(slots_ref[...])
     block = 256
     total = base_ref[...]
     place = numbers(lax.broadcasted_iota(jnp.int32, (rows, block), 1))
@@ -310,13 +344,7 @@
         total += jnp.dot(
             take, returned_ref[first : first + block], preferred_element_type=F32
         )
-    key_value = total.astype(BF16)
-    out_ref[...] = key_value
-    count = chosen_ref.shape[0]
-    place = lax.broadcasted_iota(jnp.int32, (count, rows), 1)
-    column = jnp.transpose(jnp.broadcast_to(accepted_ref[...], (8, count)))[:, 0:1]
-    take = jnp.where(place == column, 1.0, 0.0).astype(BF16)
-    chosen_ref[...] = jnp.dot(take, key_value, preferred_element_type=F32).astype(BF16)
+    out_ref[...] = total.astype(BF16)
 
 
 def cache_kernel(targets_ref, moved_ref, out_ref):
@@ -384,17 +412,33 @@
     base = sum(part.astype(F32) for part in base)
     accepted = accepted_branch_rows.reshape(1, -1)
     count = accepted.shape[1]
-    key_value, chosen = call(
+    take, base_chosen = call(
+        prepare_kernel,
+        [
+            jax.ShapeDtypeStruct((count, owners * here), BF16),
+            jax.ShapeDtypeStruct((count, columns), F32),
+        ],
+        (slots, accepted, base),
+        2 * count * rows * columns,
+        name="prepare",
+    )
+    returned = returned.reshape(owners * here, columns)
+    chosen = call(
+        choose_kernel,
+        jax.ShapeDtypeStruct((count, columns), BF16),
+        (take, returned, base_chosen),
+        2 * count * owners * here * columns,
+        name="choose",
+    )
+    moved = exchange(chosen.reshape(owners, -1, columns), "adapter").reshape(-1, columns)
+    returned, chosen = lax.optimization_barrier((returned, chosen))
+    key_value = call(
         finish_kernel,
-        [
-            jax.ShapeDtypeStruct((rows, columns), BF16),
-            jax.ShapeDtypeStruct((count, columns), BF16),
-        ],
-        (slots, returned.reshape(owners * here, columns), base, accepted),
+        jax.ShapeDtypeStruct((rows, columns), BF16),
+        (slots, returned, base),
         2 * rows * owners * here * columns,
         name="finish",
     )
-    moved = exchange(chosen.reshape(owners, -1, columns), "adapter").reshape(-1, columns)
     decode_cache = call(
         cache_kernel,
         jax.ShapeDtypeStruct((moved.shape[0], columns), BF16),

time: 149 us -> 149 us (level)
  waiting for transfers between devices: 30.8 us -> 27.5 us
  Pallas kernels: 19.7 us -> 21.6 us
    all_to_all x3, waiting for transfers between devices: 13.9 us -> 10.7 us  [exchange(): lax.all_to_all(array, axis, split_axis=0, concat_axis=0, tiled=True, axis...]
    pallas_call x9 -> x11, Pallas kernels: 10.8 us -> 12.6 us  [call(): pl.pallas_call(kernel, out_shape=out_shape, in_specs=[VMEM] * len(operand...]
  transfers between devices with their start and end apart: 13 -> 13, of which waited for: 12 -> 12; matrix products, arithmetic and copies ran while one was open for 1% -> 1% of each run, Pallas kernels for 4% -> 7%
where the time goes in v7:
time: 149 us; the launch traced here: 147 us
  starting transfers between devices  59.2 us (40%)
  blocking collectives  34 us (23%)
  waiting for transfers between devices  27.5 us (18%)
  Pallas kernels  21.6 us (14%)
  local copies, waits for them, and re-layouts  3.06 us (2%)
    all_to_all x3, starting transfers between devices, exchange(): lax.all_to_all(array, axis, split_axis=0, concat_axis=0, tiled=True, axis...  28.2 us
    ppermute x8, starting transfers between devices, shift(): lax.ppermute(array, 'tensor', [(i, (i + step) % groups) for i in range(gr...  26.1 us
    all_to_all x2, blocking collectives, exchange(): lax.all_to_all(array, axis, split_axis=0, concat_axis=0, tiled=True, axis...  25.1 us
    ppermute x8, waiting for transfers between devices, shift(): lax.ppermute(array, 'tensor', [(i, (i + step) % groups) for i in range(gr...  14.5 us
    pallas_call x11, Pallas kernels, call(): pl.pallas_call(kernel, out_shape=out_shape, in_specs=[VMEM] * len(operand...  12.6 us
    all_to_all x3, waiting for transfers between devices, exchange(): lax.all_to_all(array, axis, split_axis=0, concat_axis=0, tiled=True, axis...  10.7 us
    pallas_call x1, Pallas kernels, pack(): pl.pallas_call(pack_kernel, out_shape=[jax.ShapeDtypeStruct((1, rows), jn...  5.53 us
    all_gather x1, blocking collectives, sum_over_tensor(): lax.all_gather(mine, 'tensor', axis=0, axis_index_groups=pairs, tiled=True)  4.93 us
  transfers between devices with their start and end apart: 13, of which 12 were waited for; matrix products, arithmetic and copies ran while one was open for 1% of the time, Pallas kernels for 7%

profile of v7, /device:TPU:1, one launch (start us, length us, event | category | flops | bytes accessed | tf_op | source)
XLA Modules:
  0.0 146.9 jit_solution(8466389804490844893)
XLA Ops:
  0.6 5.5 %pack.1 = (s32[1,1024]{1,0:T(1,128)}, bf16[2048,512]{1,0:T(8,128)(2,1)}) custom-call(s32[1,1024]{1,0:T(1,128)} %bitcast.37, bf16[1024,512]{1,0:T(8,128)(2,1)} %tokens_ref.3), custom_call_target="tpu_custom_call" | custom-call | flops 2147483648 | bytes 3145728 | tf_op jit(solution)/shard_map/pack/pallas_call | solution.py:178
  6.2 0.0 copy-start
  6.2 0.0 copy-start.1
  6.2 14.1 %all-to-all-start = ((bf16[32,64,512]{2,1,0:T(8,128)(2,1)}), bf16[32,64,512]{2,1,0:T(8,128)(2,1)}, u32[]{:S(2)}, u32[]{:S(2)}) async-start(bf16[32,64,512]{2,1,0:T(8,128)(2,1)} %bitcast.35), calls=%async_computation | async-start | bytes 4194304 | tf_op jit(solution)/shard_map/all_to_all | solution.py:358
  20.3 0.0 copy-done
  20.3 0.0 copy-done.1
  20.3 1.0 base.4
  21.4 1.5 %base.5 = bf16[5,1024,128]{2,1,0:T(8,128)(2,1)S(1)} custom-call(bf16[1024,512]{1,0:T(8,128)(2,1)S(1)} %copy-done.1, bf16[512,2048]{1,0:T(8,128)(2,1)S(1)} %copy-done), custom_call_target="tpu_custom_call" | custom-call | flops 671088640 | bytes 4456448 | tf_op jit(solution)/shard_map/base/pallas_call | solution.py:24
  22.9 2.9 %collective-permute-start = (bf16[5,1024,128]{2,1,0:T(8,128)(2,1)S(1)}, bf16[5,1024,128]{2,1,0:T(8,128)(2,1)S(1)}, u32[]{:S(2)}, u32[]{:S(2)}) collective-permute-start(bf16[5,1024,128]{2,1,0:T(8,128)(2,1)S(1)} %base.5), channel_id=1, source_target_pairs={{0,1},{1,0},{2,3},{3,2},{4,5},{5,4},{6,7},{7,6},{8,9},{9,8},{10,11... | collective-permute-start | bytes 3932168 | tf_op jit(solution)/shard_map/ppermute | solution.py:85
  25.8 1.9 %collective-permute-start.1 = (bf16[3,1024,128]{2,1,0:T(8,128)(2,1)S(1)}, bf16[3,1024,128]{2,1,0:T(8,128)(2,1)S(1)}, u32[]{:S(2)}, u32[]{:S(2)}) collective-permute-start(bf16[3,1024,128]{2,1,0:T(8,128)(2,1)S(1)} %base.4), channel_id=1, source_target_pairs={{0,1},{1,0},{2,3},{3,2},{4,5},{5,4},{6,7},{7,6},{8,9},{9,8},{10,11... | collective-permute-start | bytes 2359304 | tf_op jit(solution)/shard_map/ppermute | solution.py:82
  27.7 2.3 %collective-permute-done.1.rest_0_ = bf16[3,1024,128]{2,1,0:T(8,128)(2,1)S(1)} collective-permute-done((bf16[3,1024,128]{2,1,0:T(8,128)(2,1)S(1)}, bf16[3,1024,128]{2,1,0:T(8,128)(2,1)S(1)}, u32[]{:S(2)}, u32[]{:S(2)}) %collective-permute-start.1) | collective-permute-done | bytes 786464 | tf_op jit(solution)/shard_map/ppermute | solution.py:82
  30.0 1.0 base.7
  31.0 3.2 %collective-permute-start.2 = (bf16[512,128]{1,0:T(8,128)(2,1)S(1)}, bf16[512,128]{1,0:T(8,128)(2,1)S(1)}, u32[]{:S(2)}, u32[]{:S(2)}) collective-permute-start(bf16[512,128]{1,0:T(8,128)(2,1)S(1)} %bitcast.34), channel_id=1, source_target_pairs={{0,2},{1,3},{2,4},{3,5},{4,6},{5,7},{6,8},{7,9},{8,10},{9,11},{10,... | collective-permute-start | bytes 393224 | tf_op jit(solution)/shard_map/ppermute | solution.py:73
  34.2 3.8 %collective-permute-start.3 = (bf16[512,128]{1,0:T(8,128)(2,1)S(1)}, bf16[512,128]{1,0:T(8,128)(2,1)S(1)}, u32[]{:S(2)}, u32[]{:S(2)}) collective-permute-start(bf16[512,128]{1,0:T(8,128)(2,1)S(1)} %bitcast.33), channel_id=1, source_target_pairs={{0,14},{1,15},{2,0},{3,1},{4,2},{5,3},{6,4},{7,5},{8,6},{9,7},{10,... | collective-permute-start | bytes 393224 | tf_op jit(solution)/shard_map/ppermute | solution.py:73
  38.0 1.9 %collective-permute-done.2.up_ref = bf16[512,128]{1,0:T(8,128)(2,1)S(1)} collective-permute-done((bf16[512,128]{1,0:T(8,128)(2,1)S(1)}, bf16[512,128]{1,0:T(8,128)(2,1)S(1)}, u32[]{:S(2)}, u32[]{:S(2)}) %collective-permute-start.2) | collective-permute-done | bytes 131104 | tf_op jit(solution)/shard_map/ppermute | solution.py:73
  39.9 0.9 collective-permute-done.3.down_ref
  40.9 0.1 ring.1
  40.9 3.2 %collective-permute-start.4 = (bf16[1024,128]{1,0:T(8,128)(2,1)S(1)}, bf16[1024,128]{1,0:T(8,128)(2,1)S(1)}, u32[]{:S(2)}, u32[]{:S(2)}) collective-permute-start(bf16[1024,128]{1,0:T(8,128)(2,1)S(1)} %get-tuple-element.36), channel_id=1, source_target_pairs={{0,2},{1,3},{2,4},{3,5},{4,6},{5,7},{6,8},{7,9},{8,10},{9,11},{10,... | collective-permute-start | bytes 786440 | tf_op jit(solution)/shard_map/ppermute | solution.py:73
  44.1 4.1 %collective-permute-start.6 = (bf16[1024,128]{1,0:T(8,128)(2,1)S(1)}, bf16[1024,128]{1,0:T(8,128)(2,1)S(1)}, u32[]{:S(2)}, u32[]{:S(2)}) collective-permute-start(bf16[1024,128]{1,0:T(8,128)(2,1)S(1)} %get-tuple-element.38), channel_id=1, source_target_pairs={{0,14},{1,15},{2,0},{3,1},{4,2},{5,3},{6,4},{7,5},{8,6},{9,7},{10,... | collective-permute-start | bytes 786440 | tf_op jit(solution)/shard_map/ppermute | solution.py:73
  48.2 0.0 collective-permute-done.rest_0_
  48.2 1.6 %base.6 = (bf16[1,1024,128]{2,1,0:T(8,128)(2,1)S(1)}, bf16[1,1024,128]{2,1,0:T(8,128)(2,1)S(1)}, bf16[1,1024,128]{2,1,0:T(8,128)(2,1)S(1)}, bf16[1,1024,128]{2,1,0:T(8,128)(2,1)S(1)}, bf16[1,1024,128]{2,1,0:T(8,128)(2,1)S(1)}) custom-call(bf16[1024,512]{1,0:T(8,128)(2,1)S(1)} %copy-done.1, bf16[512,2048]{1,0:T(8,128)(2,1)S(1)} %copy-done, ...), custom_call_target="tpu_custom_call" | custom-call | flops 671088640 | bytes 5767168 | tf_op jit(solution)/shard_map/base/pallas_call | solution.py:24
  49.8 0.0 copy-start.3
  49.8 0.7 copy-done.3
  50.5 0.7 copy-done.5
  51.2 1.0 collective-permute-done.4
  52.2 0.1 fusion.4
  52.3 1.9 %collective-permute-start.5 = (bf16[1024,128]{1,0:T(8,128)(2,1)S(1)}, bf16[1024,128]{1,0:T(8,128)(2,1)S(1)}, u32[]{:S(2)}, u32[]{:S(2)}) collective-permute-start(bf16[1024,128]{1,0:T(8,128)(2,1)S(1)} %fusion.4), channel_id=1, source_target_pairs={{0,2},{1,3},{2,4},{3,5},{4,6},{5,7},{6,8},{7,9},{8,10},{9,11},{10,... | collective-permute-start | bytes 786440 | tf_op jit(solution)/shard_map/ppermute | solution.py:73
  54.2 0.1 collective-permute-done.6
  54.3 0.1 fusion.3
  54.4 4.5 %collective-permute-start.7 = (bf16[1024,128]{1,0:T(8,128)(2,1)S(1)}, bf16[1024,128]{1,0:T(8,128)(2,1)S(1)}, u32[]{:S(2)}, u32[]{:S(2)}) collective-permute-start(bf16[1024,128]{1,0:T(8,128)(2,1)S(1)} %fusion.3), channel_id=1, source_target_pairs={{0,14},{1,15},{2,0},{3,1},{4,2},{5,3},{6,4},{7,5},{8,6},{9,7},{10,... | collective-permute-start | bytes 786440 | tf_op jit(solution)/shard_map/ppermute | solution.py:73
  58.9 3.1 %collective-permute-done.5 = bf16[1024,128]{1,0:T(8,128)(2,1)S(1)} collective-permute-done((bf16[1024,128]{1,0:T(8,128)(2,1)S(1)}, bf16[1024,128]{1,0:T(8,128)(2,1)S(1)}, u32[]{:S(2)}, u32[]{:S(2)}) %collective-permute-start.5) | collective-permute-done | bytes 262176 | tf_op jit(solution)/shard_map/ppermute | solution.py:73
  62.0 1.1 collective-permute-done.7
  63.0 1.2 copy-done.2
  64.3 1.2 turn.1.weight_ref
  65.4 3.8 %all-to-all-done.rows_hbm = bf16[32,64,512]{2,1,0:T(8,128)(2,1)} async-done(((bf16[32,64,512]{2,1,0:T(8,128)(2,1)}), bf16[32,64,512]{2,1,0:T(8,128)(2,1)}, u32[]{:S(2)}, u32[]{:S(2)}) %all-to-all-start) | async-done | bytes 2097184 | tf_op jit(solution)/shard_map/all_to_all | solution.py:358
  69.2 3.5 %down.1 = bf16[16,64,128]{2,1,0:T(8,128)(2,1)S(1)} custom-call(bf16[32,64,512]{2,1,0:T(8,128)(2,1)} %all-to-all-done.rows_hbm, bf16[4,512,256]{2,1,0:T(8,128)(2,1)S(1)} %turn.1.weight_ref), custom_call_target="tpu_custom_call" | custom-call | flops 536870912 | bytes 3145728 | tf_op jit(solution)/shard_map/down/pallas_call | solution.py:260
  72.7 0.0 copy-start.7
  72.7 4.0 %all-gather = bf16[32,64,128]{2,1,0:T(8,128)(2,1)S(1)} all-gather(bf16[16,64,128]{2,1,0:T(8,128)(2,1)S(1)} %down.1), channel_id=2, replica_groups={{0,1},{2,3},{4,5},{6,7},{8,9},{10,11},{12,13},{14,15},{16,17},{18,19},{..., dimensions={0}, use_global_device_ids=true | all-gather | bytes 786432 | tf_op jit(solution)/shard_map/all_gather | solution.py:364
  76.8 0.0 copy-start.6
  76.9 14.6 %all_to_all.25 = bf16[8,64,128]{2,1,0:T(8,128)(2,1)S(1)} all-to-all(bf16[8,64,128]{2,1,0:T(8,128)(2,1)S(1)} %fusion.6), channel_id=1, replica_groups={{0,2,4,6,8,10,12,14},{1,3,5,7,9,11,13,15},{16,18,20,22,24,26,28,30},{17..., dimensions={0} | all-to-all | bytes 262144 | tf_op jit(solution)/shard_map/all_to_all | solution.py:358
  91.5 10.4 %all_to_all.26 = bf16[8,64,128]{2,1,0:T(8,128)(2,1)S(1)} all-to-all(bf16[8,64,128]{2,1,0:T(8,128)(2,1)S(1)} %broadcast_in_dim.2), channel_id=1, replica_groups={{0,2,4,6,8,10,12,14},{1,3,5,7,9,11,13,15},{16,18,20,22,24,26,28,30},{17..., dimensions={0} | all-to-all | bytes 262144 | tf_op jit(solution)/shard_map/all_to_all | solution.py:358
  102.0 4.9 %all_gather.11.lowered_ref = bf16[16,64,128]{2,1,0:T(8,128)(2,1)S(1)} all-gather(bf16[8,64,128]{2,1,0:T(8,128)(2,1)S(1)} %all_to_all.26), channel_id=1, replica_groups={{0,1},{2,3},{4,5},{6,7},{8,9},{10,11},{12,13},{14,15},{16,17},{18,19},{..., dimensions={0}, use_global_device_ids=true | all-gather | bytes 393216 | tf_op jit(solution)/shard_map/all_gather | solution.py:373
  106.9 1.3 up.1
  108.2 6.0 %all-to-all-start.3 = ((bf16[32,64,128]{2,1,0:T(8,128)(2,1)}), bf16[32,64,128]{2,1,0:T(8,128)(2,1)S(1)}, u32[]{:S(2)}, u32[]{:S(2)}) async-start(bf16[32,64,128]{2,1,0:T(8,128)(2,1)} %bitcast.9), calls=%async_computation.3 | async-start | bytes 1048576 | tf_op jit(solution)/shard_map/all_to_all | solution.py:358
  114.2 0.1 fusion
  114.3 0.0 copy-start.10
  114.3 2.1 %collective-permute-start.9 = (bf16[1024,128]{1,0:T(8,128)(2,1)S(1)}, bf16[1024,128]{1,0:T(8,128)(2,1)S(1)}, u32[]{:S(2)}, u32[]{:S(2)}) collective-permute-start(bf16[1024,128]{1,0:T(8,128)(2,1)S(1)} %fusion), channel_id=1, source_target_pairs={{0,14},{1,15},{2,0},{3,1},{4,2},{5,3},{6,4},{7,5},{8,6},{9,7},{10,... | collective-permute-start | bytes 786440 | tf_op jit(solution)/shard_map/ppermute | solution.py:73
  116.3 0.0 copy-done.4
  116.4 0.1 fusion.1
  116.4 3.4 %collective-permute-start.8 = (bf16[1024,128]{1,0:T(8,128)(2,1)S(1)}, bf16[1024,128]{1,0:T(8,128)(2,1)S(1)}, u32[]{:S(2)}, u32[]{:S(2)}) collective-permute-start(bf16[1024,128]{1,0:T(8,128)(2,1)S(1)} %fusion.1), channel_id=1, source_target_pairs={{0,2},{1,3},{2,4},{3,5},{4,6},{5,7},{6,8},{7,9},{8,10},{9,11},{10,... | collective-permute-start | bytes 786440 | tf_op jit(solution)/shard_map/ppermute | solution.py:73
  119.9 0.1 copy.13
  119.9 0.1 reshape.47.accepted_ref
  120.0 3.3 %collective-permute-done.9 = bf16[1024,128]{1,0:T(8,128)(2,1)S(1)} collective-permute-done((bf16[1024,128]{1,0:T(8,128)(2,1)S(1)}, bf16[1024,128]{1,0:T(8,128)(2,1)S(1)}, u32[]{:S(2)}, u32[]{:S(2)}) %collective-permute-start.9) | collective-permute-done | bytes 262176 | tf_op jit(solution)/shard_map/ppermute | solution.py:73
  123.4 3.1 %collective-permute-done.8 = bf16[1024,128]{1,0:T(8,128)(2,1)S(1)} collective-permute-done((bf16[1024,128]{1,0:T(8,128)(2,1)S(1)}, bf16[1024,128]{1,0:T(8,128)(2,1)S(1)}, u32[]{:S(2)}, u32[]{:S(2)}) %collective-permute-start.8) | collective-permute-done | bytes 262176 | tf_op jit(solution)/shard_map/ppermute | solution.py:73
  126.4 0.1 fusion.2.base_ref
  126.6 0.9 prepare.1
  127.5 0.8 all-to-all-done.3
  128.3 0.9 choose.1
  129.2 8.1 %all-to-all-start.4 = ((bf16[32,4,128]{2,1,0:T(4,128)(2,1)}), bf16[32,4,128]{2,1,0:T(4,128)(2,1)S(1)}, u32[]{:S(2)}, u32[]{:S(2)}) async-start(bf16[32,4,128]{2,1,0:T(4,128)(2,1)} %bitcast.14), calls=%async_computation.4 | async-start | bytes 65536 | tf_op jit(solution)/shard_map/all_to_all | solution.py:358
  137.4 0.1 copy.14
  137.5 0.1 reshape.48.targets_ref
  137.6 2.4 %finish.1 = bf16[1024,128]{1,0:T(8,128)(2,1)} custom-call(s32[1,1024]{1,0:T(1,128)S(1)} %copy-done.8, bf16[2048,128]{1,0:T(8,128)(2,1)S(1)} %bitcast.30, f32[1024,128]{1,0:T(8,128)S(1)} %fusion.2.base_ref), custom_call_target="tpu_custom_call" | custom-call | flops 536870912 | bytes 1314816 | tf_op jit(solution)/shard_map/finish/pallas_call | solution.py:24
  140.0 6.1 %all-to-all-done.4 = bf16[32,4,128]{2,1,0:T(4,128)(2,1)S(1)} async-done(((bf16[32,4,128]{2,1,0:T(4,128)(2,1)}), bf16[32,4,128]{2,1,0:T(4,128)(2,1)S(1)}, u32[]{:S(2)}, u32[]{:S(2)}) %all-to-all-start.4) | async-done | bytes 32800 | tf_op jit(solution)/shard_map/all_to_all | solution.py:358
  146.1 0.8 cache.1
  (14 shorter events, 0.1 us)
Async XLA Ops:
  6.2 14.2 %copy-start = (bf16[512,2048]{1,0:T(8,128)(2,1)S(1)}, bf16[512,2048]{1,0:T(8,128)(2,1)}, u32[]{:S(2)}) copy-start(bf16[512,2048]{1,0:T(8,128)(2,1)} %weight_ref.8) | copy-start | bytes 6291460
  6.2 14.2 %copy-start.1 = (bf16[1024,512]{1,0:T(8,128)(2,1)S(1)}, bf16[1024,512]{1,0:T(8,128)(2,1)}, u32[]{:S(2)}) copy-start(bf16[1024,512]{1,0:T(8,128)(2,1)} %tokens_ref.3) | copy-start | bytes 3145732
  6.2 63.0 %all-to-all-start = ((bf16[32,64,512]{2,1,0:T(8,128)(2,1)}), bf16[32,64,512]{2,1,0:T(8,128)(2,1)}, u32[]{:S(2)}, u32[]{:S(2)}) async-start(bf16[32,64,512]{2,1,0:T(8,128)(2,1)} %bitcast.35), calls=%async_computation | async-start | bytes 4194304 | tf_op jit(solution)/shard_map/all_to_all | solution.py:358
  22.9 25.3 %collective-permute-start = (bf16[5,1024,128]{2,1,0:T(8,128)(2,1)S(1)}, bf16[5,1024,128]{2,1,0:T(8,128)(2,1)S(1)}, u32[]{:S(2)}, u32[]{:S(2)}) collective-permute-start(bf16[5,1024,128]{2,1,0:T(8,128)(2,1)S(1)} %base.5), channel_id=1, source_target_pairs={{0,1},{1,0},{2,3},{3,2},{4,5},{5,4},{6,7},{7,6},{8,9},{9,8},{10,11... | collective-permute-start | bytes 3932168 | tf_op jit(solution)/shard_map/ppermute | solution.py:85
  25.8 4.2 %collective-permute-start.1 = (bf16[3,1024,128]{2,1,0:T(8,128)(2,1)S(1)}, bf16[3,1024,128]{2,1,0:T(8,128)(2,1)S(1)}, u32[]{:S(2)}, u32[]{:S(2)}) collective-permute-start(bf16[3,1024,128]{2,1,0:T(8,128)(2,1)S(1)} %base.4), channel_id=1, source_target_pairs={{0,1},{1,0},{2,3},{3,2},{4,5},{5,4},{6,7},{7,6},{8,9},{9,8},{10,11... | collective-permute-start | bytes 2359304 | tf_op jit(solution)/shard_map/ppermute | solution.py:82
  31.0 9.0 %collective-permute-start.2 = (bf16[512,128]{1,0:T(8,128)(2,1)S(1)}, bf16[512,128]{1,0:T(8,128)(2,1)S(1)}, u32[]{:S(2)}, u32[]{:S(2)}) collective-permute-start(bf16[512,128]{1,0:T(8,128)(2,1)S(1)} %bitcast.34), channel_id=1, source_target_pairs={{0,2},{1,3},{2,4},{3,5},{4,6},{5,7},{6,8},{7,9},{8,10},{9,11},{10,... | collective-permute-start | bytes 393224 | tf_op jit(solution)/shard_map/ppermute | solution.py:73
  34.2 6.6 %collective-permute-start.3 = (bf16[512,128]{1,0:T(8,128)(2,1)S(1)}, bf16[512,128]{1,0:T(8,128)(2,1)S(1)}, u32[]{:S(2)}, u32[]{:S(2)}) collective-permute-start(bf16[512,128]{1,0:T(8,128)(2,1)S(1)} %bitcast.33), channel_id=1, source_target_pairs={{0,14},{1,15},{2,0},{3,1},{4,2},{5,3},{6,4},{7,5},{8,6},{9,7},{10,... | collective-permute-start | bytes 393224 | tf_op jit(solution)/shard_map/ppermute | solution.py:73
  40.9 11.3 %collective-permute-start.4 = (bf16[1024,128]{1,0:T(8,128)(2,1)S(1)}, bf16[1024,128]{1,0:T(8,128)(2,1)S(1)}, u32[]{:S(2)}, u32[]{:S(2)}) collective-permute-start(bf16[1024,128]{1,0:T(8,128)(2,1)S(1)} %get-tuple-element.36), channel_id=1, source_target_pairs={{0,2},{1,3},{2,4},{3,5},{4,6},{5,7},{6,8},{7,9},{8,10},{9,11},{10,... | collective-permute-start | bytes 786440 | tf_op jit(solution)/shard_map/ppermute | solution.py:73
  44.1 10.2 %collective-permute-start.6 = (bf16[1024,128]{1,0:T(8,128)(2,1)S(1)}, bf16[1024,128]{1,0:T(8,128)(2,1)S(1)}, u32[]{:S(2)}, u32[]{:S(2)}) collective-permute-start(bf16[1024,128]{1,0:T(8,128)(2,1)S(1)} %get-tuple-element.38), channel_id=1, source_target_pairs={{0,14},{1,15},{2,0},{3,1},{4,2},{5,3},{6,4},{7,5},{8,6},{9,7},{10,... | collective-permute-start | bytes 786440 | tf_op jit(solution)/shard_map/ppermute | solution.py:73
  49.8 0.7 copy-start.3
  50.5 0.7 copy-start.5
  52.3 9.7 %collective-permute-start.5 = (bf16[1024,128]{1,0:T(8,128)(2,1)S(1)}, bf16[1024,128]{1,0:T(8,128)(2,1)S(1)}, u32[]{:S(2)}, u32[]{:S(2)}) collective-permute-start(bf16[1024,128]{1,0:T(8,128)(2,1)S(1)} %fusion.4), channel_id=1, source_target_pairs={{0,2},{1,3},{2,4},{3,5},{4,6},{5,7},{6,8},{7,9},{8,10},{9,11},{10,... | collective-permute-start | bytes 786440 | tf_op jit(solution)/shard_map/ppermute | solution.py:73
  54.4 8.6 %collective-permute-start.7 = (bf16[1024,128]{1,0:T(8,128)(2,1)S(1)}, bf16[1024,128]{1,0:T(8,128)(2,1)S(1)}, u32[]{:S(2)}, u32[]{:S(2)}) collective-permute-start(bf16[1024,128]{1,0:T(8,128)(2,1)S(1)} %fusion.3), channel_id=1, source_target_pairs={{0,14},{1,15},{2,0},{3,1},{4,2},{5,3},{6,4},{7,5},{8,6},{9,7},{10,... | collective-permute-start | bytes 786440 | tf_op jit(solution)/shard_map/ppermute | solution.py:73
  63.0 1.2 copy-start.2
  72.7 34.2 %copy-start.7 = (bf16[16,64,128]{2,1,0:T(8,128)(2,1)S(1)}, bf16[16,64,128]{2,1,0:T(8,128)(2,1)}, u32[]{:S(2)}) copy-start(bf16[16,64,128]{2,1,0:T(8,128)(2,1)} %weight_ref.9) | copy-start | bytes 786436
  76.8 37.4 %copy-start.6 = (bf16[1,1024,128]{2,1,0:T(8,128)(2,1)S(1)}, bf16[1,1024,128]{2,1,0:T(8,128)(2,1)}, u32[]{:S(2)}) copy-start(bf16[1,1024,128]{2,1,0:T(8,128)(2,1)} %copy-done.5) | copy-start | bytes 786436
  76.8 39.5 %copy-start.4 = (bf16[1,1024,128]{2,1,0:T(8,128)(2,1)S(1)}, bf16[1,1024,128]{2,1,0:T(8,128)(2,1)}, u32[]{:S(2)}) copy-start(bf16[1,1024,128]{2,1,0:T(8,128)(2,1)} %copy-done.3) | copy-start | bytes 786436
  102.0 17.9 %copy-start.9 = (s32[1,32,4]{1,2,0:T(4,128)S(1)}, s32[1,32,4]{1,2,0:T(4,128)}, u32[]{:S(2)}) copy-start(s32[1,32,4]{1,2,0:T(4,128)} %param.12) | copy-start | bytes 1540
  108.2 18.4 %copy-start.8 = (s32[1,1024]{1,0:T(1,128)S(1)}, s32[1,1024]{1,0:T(1,128)}, u32[]{:S(2)}) copy-start(s32[1,1024]{1,0:T(1,128)} %get-tuple-element.27.slots_ref) | copy-start | bytes 12292
  108.2 20.1 %all-to-all-start.3 = ((bf16[32,64,128]{2,1,0:T(8,128)(2,1)}), bf16[32,64,128]{2,1,0:T(8,128)(2,1)S(1)}, u32[]{:S(2)}, u32[]{:S(2)}) async-start(bf16[32,64,128]{2,1,0:T(8,128)(2,1)} %bitcast.9), calls=%async_computation.3 | async-start | bytes 1048576 | tf_op jit(solution)/shard_map/all_to_all | solution.py:358
  114.3 23.1 %copy-start.10 = (s32[32,1,4]{0,2,1:T(4,128)S(1)}, s32[32,1,4]{0,2,1:T(4,128)}, u32[]{:S(2)}) copy-start(s32[32,1,4]{0,2,1:T(4,128)} %param.13) | copy-start | bytes 1540
  114.3 9.1 %collective-permute-start.9 = (bf16[1024,128]{1,0:T(8,128)(2,1)S(1)}, bf16[1024,128]{1,0:T(8,128)(2,1)S(1)}, u32[]{:S(2)}, u32[]{:S(2)}) collective-permute-start(bf16[1024,128]{1,0:T(8,128)(2,1)S(1)} %fusion), channel_id=1, source_target_pairs={{0,14},{1,15},{2,0},{3,1},{4,2},{5,3},{6,4},{7,5},{8,6},{9,7},{10,... | collective-permute-start | bytes 786440 | tf_op jit(solution)/shard_map/ppermute | solution.py:73
  116.4 10.0 %collective-permute-start.8 = (bf16[1024,128]{1,0:T(8,128)(2,1)S(1)}, bf16[1024,128]{1,0:T(8,128)(2,1)S(1)}, u32[]{:S(2)}, u32[]{:S(2)}) collective-permute-start(bf16[1024,128]{1,0:T(8,128)(2,1)S(1)} %fusion.1), channel_id=1, source_target_pairs={{0,2},{1,3},{2,4},{3,5},{4,6},{5,7},{6,8},{7,9},{8,10},{9,11},{10,... | collective-permute-start | bytes 786440 | tf_op jit(solution)/shard_map/ppermute | solution.py:73
  129.2 16.9 %all-to-all-start.4 = ((bf16[32,4,128]{2,1,0:T(4,128)(2,1)}), bf16[32,4,128]{2,1,0:T(4,128)(2,1)S(1)}, u32[]{:S(2)}, u32[]{:S(2)}) async-start(bf16[32,4,128]{2,1,0:T(4,128)(2,1)} %bitcast.14), calls=%async_computation.4 | async-start | bytes 65536 | tf_op jit(solution)/shard_map/all_to_all | solution.py:358

commit v8 on v7

--- a/solution.py
+++ b/solution.py
@@ -102,7 +102,7 @@
     up, down = shift(third, 1, groups), shift(fifth, -1, groups)
     up, down = shift(add(second[0], up), 1, groups), shift(add(sixth[0], down), -1, groups)
     down_weight, up, down = lax.optimization_barrier((down_weight, up, down))
-    down_weight = turn(down_weight)
+    down_weight = keep(down_weight)
     after, down_weight = lax.optimization_barrier((after, down_weight))
     up, down = shift(add(first[0], up), 1, groups), shift(add(seventh[0], down), -1, groups)
     return after, down_weight, [mine[0], up, down]
@@ -149,25 +149,22 @@
     slots = labels * CAP + jnp.concatenate(ranks, axis=1)
     slots_ref[...] = slots
     tokens_in.wait()
+    tokens = tokens_ref[...]
     place = numbers(lax.broadcasted_iota(jnp.int32, (block // 2, rows), 0))
-
-    def copy_out(i):
-        at = pl.multiple_of(i * block, block)
-        return pltpu.make_async_copy(
-            parts.at[i], packed_hbm.at[pl.ds(at, block), :], sems.at[i]
+    out = []
+    for i in range(count):
+        chosen = jnp.concatenate(
+            [one_hot(place == numbers(slots - at)) for at in (i * block, i * block + block // 2)]
         )
-
-    @pl.loop(0, count)
-    def _(i):
-        chosen = jnp.concatenate(
-            [one_hot(place == numbers(slots - (i * block + at))) for at in (0, block // 2)]
+        parts[i] = jnp.dot(chosen, tokens, preferred_element_type=F32).astype(BF16)
+        out.append(
+            pltpu.make_async_copy(
+                parts.at[i], packed_hbm.at[pl.ds(i * block, block), :], sems.at[i]
+            )
         )
-        parts[i] = jnp.dot(chosen, tokens_ref[...], preferred_element_type=F32).astype(BF16)
-        copy_out(i).start()
-
-    @pl.loop(0, count)
-    def _(i):
-        copy_out(i).wait()
+        out[-1].start()
+    for copy in out:
+        copy.wait()
 
 
 def pack(labels, tokens):
@@ -199,28 +196,18 @@
     )(labels, tokens)
 
 
-def turn_kernel(weight_ref, out_ref):
-    for quad in range(out_ref.shape[0]):
-        for k in range(QUAD):
-            turned = jnp.transpose(weight_ref[quad * QUAD + k])
-            rank = turned.shape[1]
-            out_ref[quad, :, k * rank : (k + 1) * rank] = turned
-
-
-def turn(weight):
-    adapters, rank, features = weight.shape
-    return call(
-        turn_kernel,
-        jax.ShapeDtypeStruct((adapters // QUAD, features, QUAD * rank), BF16),
-        (weight,),
-        0,
-        name="turn",
-    )
+def keep_kernel(weight_ref, out_ref):
+    out_ref[...] = weight_ref[...]
+
+
+def keep(weight):
+    shape = jax.ShapeDtypeStruct(weight.shape, weight.dtype)
+    return call(keep_kernel, shape, (weight,), 0, name="keep")
 
 
 def down_kernel(rows_hbm, weight_ref, out_ref, rows_ref, sems):
     quads, sources, tile, features = rows_ref.shape
-    rank = weight_ref.shape[2] // QUAD
+    rank = weight_ref.shape[1]
     rows_in = [
         pltpu.make_async_copy(
             rows_hbm.at[:, pl.ds(quad * tile, tile), :], rows_ref.at[quad], sems.at[quad]
@@ -229,33 +216,27 @@
     ]
     for copy in rows_in:
         copy.start()
-    wide = QUAD * rank
-    shape = (sources, tile, wide)
-    owner = lax.broadcasted_iota(jnp.int32, shape, 1) // CAP
-    own = owner == lax.broadcasted_iota(jnp.int32, shape, 2) // rank
-    shape = (2 * wide, 2 * rank)
-    line, lane = lax.broadcasted_iota(jnp.int32, shape, 0), lax.broadcasted_iota(jnp.int32, shape, 1)
-    fold = jnp.where(line // wide * rank + line % rank == lane, 1.0, 0.0).astype(BF16)
+    owner = lax.broadcasted_iota(jnp.int32, (1, tile, 1), 1) // CAP
     for quad in range(quads):
         rows_in[quad].wait()
-        product = jnp.dot(
+        product = lax.dot_general(
             rows_ref[quad].reshape(sources * tile, features),
-            weight_ref[quad],
+            weight_ref[quad * QUAD : (quad + 1) * QUAD].reshape(QUAD * rank, features),
+            (((1,), (1,)), ((), ())),
             preferred_element_type=F32,
-        ).reshape(sources, tile, wide)
-        lowered = jnp.where(own, product, 0.0).astype(BF16).reshape(sources // 2, 2, tile, wide)
-        lowered = jnp.concatenate([lowered[:, 0], lowered[:, 1]], axis=-1)
-        lowered = lowered.reshape(sources // 2 * tile, 2 * wide)
-        out_ref[:, quad * tile : (quad + 1) * tile, :] = (
-            jnp.dot(lowered, fold, preferred_element_type=F32)
-            .astype(BF16)
-            .reshape(sources // 2, tile, 2 * rank)
-        )
+        ).reshape(sources, tile, QUAD * rank)
+        lowered = jnp.zeros((sources, tile, rank), F32)
+        for k in range(QUAD):
+            lowered = jnp.where(owner == k, product[:, :, k * rank : (k + 1) * rank], lowered)
+        lowered = lowered.reshape(sources // 2, 2, tile, rank)
+        out_ref[:, quad * tile : (quad + 1) * tile, :] = jnp.concatenate(
+            [lowered[:, 0], lowered[:, 1]], axis=-1
+        ).astype(BF16)
 
 
 def lower(received, weight):
     sources, slots, features = received.shape
-    rank = weight.shape[2] // QUAD
+    rank = weight.shape[1]
     tile = QUAD * CAP
     return pl.pallas_call(
         down_kernel,

time: 149 us -> 149 us (level)
  transfers between devices with their start and end apart: 13 -> 13, of which waited for: 12 -> 12; matrix products, arithmetic and copies ran while one was open for 1% -> 1% of each run, Pallas kernels for 7% -> 6%
where the time goes in v8:
time: 149 us; the launch traced here: 147 us
  starting transfers between devices  59.2 us (40%)
  blocking collectives  34 us (23%)
  waiting for transfers between devices  28.6 us (19%)
  Pallas kernels  20.5 us (14%)
  local copies, waits for them, and re-layouts  3.06 us (2%)
    all_to_all x3, starting transfers between devices, exchange(): lax.all_to_all(array, axis, split_axis=0, concat_axis=0, tiled=True, axis...  28.2 us
    ppermute x8, starting transfers between devices, shift(): lax.ppermute(array, 'tensor', [(i, (i + step) % groups) for i in range(gr...  26.1 us
    all_to_all x2, blocking collectives, exchange(): lax.all_to_all(array, axis, split_axis=0, concat_axis=0, tiled=True, axis...  25.1 us
    ppermute x8, waiting for transfers between devices, shift(): lax.ppermute(array, 'tensor', [(i, (i + step) % groups) for i in range(gr...  14.5 us
    all_to_all x3, waiting for transfers between devices, exchange(): lax.all_to_all(array, axis, split_axis=0, concat_axis=0, tiled=True, axis...  11.8 us
    pallas_call x11, Pallas kernels, call(): pl.pallas_call(kernel, out_shape=out_shape, in_specs=[VMEM] * len(operand...  11.5 us
    pallas_call x1, Pallas kernels, pack(): pl.pallas_call(pack_kernel, out_shape=[jax.ShapeDtypeStruct((1, rows), jn...  5.01 us
    all_gather x1, blocking collectives, sum_over_tensor(): lax.all_gather(mine, 'tensor', axis=0, axis_index_groups=pairs, tiled=True)  4.93 us
  transfers between devices with their start and end apart: 13, of which 12 were waited for; matrix products, arithmetic and copies ran while one was open for 1% of the time, Pallas kernels for 6%

profile of v8, /device:TPU:1, one launch (start us, length us, event | category | flops | bytes accessed | tf_op | source)
XLA Modules:
  0.0 146.9 jit_solution(2727984310036684125)
XLA Ops:
  0.6 5.0 %pack.1 = (s32[1,1024]{1,0:T(1,128)}, bf16[2048,512]{1,0:T(8,128)(2,1)}) custom-call(s32[1,1024]{1,0:T(1,128)} %bitcast.37, bf16[1024,512]{1,0:T(8,128)(2,1)} %tokens_ref.3), custom_call_target="tpu_custom_call" | custom-call | flops 2147483648 | bytes 3145728 | tf_op jit(solution)/shard_map/pack/pallas_call | solution.py:175
  5.6 0.0 copy-start
  5.7 0.0 copy-start.1
  5.7 14.1 %all-to-all-start = ((bf16[32,64,512]{2,1,0:T(8,128)(2,1)}), bf16[32,64,512]{2,1,0:T(8,128)(2,1)}, u32[]{:S(2)}, u32[]{:S(2)}) async-start(bf16[32,64,512]{2,1,0:T(8,128)(2,1)} %bitcast.35), calls=%async_computation | async-start | bytes 4194304 | tf_op jit(solution)/shard_map/all_to_all | solution.py:339
  19.8 0.0 copy-done
  19.8 0.0 copy-done.1
  19.8 1.0 base.4
  20.8 1.5 %base.5 = bf16[5,1024,128]{2,1,0:T(8,128)(2,1)S(1)} custom-call(bf16[1024,512]{1,0:T(8,128)(2,1)S(1)} %copy-done.1, bf16[512,2048]{1,0:T(8,128)(2,1)S(1)} %copy-done), custom_call_target="tpu_custom_call" | custom-call | flops 671088640 | bytes 4456448 | tf_op jit(solution)/shard_map/base/pallas_call | solution.py:24
  22.4 2.9 %collective-permute-start = (bf16[5,1024,128]{2,1,0:T(8,128)(2,1)S(1)}, bf16[5,1024,128]{2,1,0:T(8,128)(2,1)S(1)}, u32[]{:S(2)}, u32[]{:S(2)}) collective-permute-start(bf16[5,1024,128]{2,1,0:T(8,128)(2,1)S(1)} %base.5), channel_id=1, source_target_pairs={{0,1},{1,0},{2,3},{3,2},{4,5},{5,4},{6,7},{7,6},{8,9},{9,8},{10,11... | collective-permute-start | bytes 3932168 | tf_op jit(solution)/shard_map/ppermute | solution.py:85
  25.3 1.9 %collective-permute-start.1 = (bf16[3,1024,128]{2,1,0:T(8,128)(2,1)S(1)}, bf16[3,1024,128]{2,1,0:T(8,128)(2,1)S(1)}, u32[]{:S(2)}, u32[]{:S(2)}) collective-permute-start(bf16[3,1024,128]{2,1,0:T(8,128)(2,1)S(1)} %base.4), channel_id=1, source_target_pairs={{0,1},{1,0},{2,3},{3,2},{4,5},{5,4},{6,7},{7,6},{8,9},{9,8},{10,11... | collective-permute-start | bytes 2359304 | tf_op jit(solution)/shard_map/ppermute | solution.py:82
  27.2 2.3 %collective-permute-done.1.rest_0_ = bf16[3,1024,128]{2,1,0:T(8,128)(2,1)S(1)} collective-permute-done((bf16[3,1024,128]{2,1,0:T(8,128)(2,1)S(1)}, bf16[3,1024,128]{2,1,0:T(8,128)(2,1)S(1)}, u32[]{:S(2)}, u32[]{:S(2)}) %collective-permute-start.1) | collective-permute-done | bytes 786464 | tf_op jit(solution)/shard_map/ppermute | solution.py:82
  29.5 1.0 base.7
  30.5 3.2 %collective-permute-start.2 = (bf16[512,128]{1,0:T(8,128)(2,1)S(1)}, bf16[512,128]{1,0:T(8,128)(2,1)S(1)}, u32[]{:S(2)}, u32[]{:S(2)}) collective-permute-start(bf16[512,128]{1,0:T(8,128)(2,1)S(1)} %bitcast.34), channel_id=1, source_target_pairs={{0,2},{1,3},{2,4},{3,5},{4,6},{5,7},{6,8},{7,9},{8,10},{9,11},{10,... | collective-permute-start | bytes 393224 | tf_op jit(solution)/shard_map/ppermute | solution.py:73
  33.7 3.8 %collective-permute-start.3 = (bf16[512,128]{1,0:T(8,128)(2,1)S(1)}, bf16[512,128]{1,0:T(8,128)(2,1)S(1)}, u32[]{:S(2)}, u32[]{:S(2)}) collective-permute-start(bf16[512,128]{1,0:T(8,128)(2,1)S(1)} %bitcast.33), channel_id=1, source_target_pairs={{0,14},{1,15},{2,0},{3,1},{4,2},{5,3},{6,4},{7,5},{8,6},{9,7},{10,... | collective-permute-start | bytes 393224 | tf_op jit(solution)/shard_map/ppermute | solution.py:73
  37.5 1.9 %collective-permute-done.2.up_ref = bf16[512,128]{1,0:T(8,128)(2,1)S(1)} collective-permute-done((bf16[512,128]{1,0:T(8,128)(2,1)S(1)}, bf16[512,128]{1,0:T(8,128)(2,1)S(1)}, u32[]{:S(2)}, u32[]{:S(2)}) %collective-permute-start.2) | collective-permute-done | bytes 131104 | tf_op jit(solution)/shard_map/ppermute | solution.py:73
  39.4 0.9 collective-permute-done.3.down_ref
  40.3 0.1 ring.1
  40.4 3.2 %collective-permute-start.4 = (bf16[1024,128]{1,0:T(8,128)(2,1)S(1)}, bf16[1024,128]{1,0:T(8,128)(2,1)S(1)}, u32[]{:S(2)}, u32[]{:S(2)}) collective-permute-start(bf16[1024,128]{1,0:T(8,128)(2,1)S(1)} %get-tuple-element.36), channel_id=1, source_target_pairs={{0,2},{1,3},{2,4},{3,5},{4,6},{5,7},{6,8},{7,9},{8,10},{9,11},{10,... | collective-permute-start | bytes 786440 | tf_op jit(solution)/shard_map/ppermute | solution.py:73
  43.6 4.1 %collective-permute-start.6 = (bf16[1024,128]{1,0:T(8,128)(2,1)S(1)}, bf16[1024,128]{1,0:T(8,128)(2,1)S(1)}, u32[]{:S(2)}, u32[]{:S(2)}) collective-permute-start(bf16[1024,128]{1,0:T(8,128)(2,1)S(1)} %get-tuple-element.38), channel_id=1, source_target_pairs={{0,14},{1,15},{2,0},{3,1},{4,2},{5,3},{6,4},{7,5},{8,6},{9,7},{10,... | collective-permute-start | bytes 786440 | tf_op jit(solution)/shard_map/ppermute | solution.py:73
  47.7 0.0 collective-permute-done.rest_0_
  47.7 1.6 %base.6 = (bf16[1,1024,128]{2,1,0:T(8,128)(2,1)S(1)}, bf16[1,1024,128]{2,1,0:T(8,128)(2,1)S(1)}, bf16[1,1024,128]{2,1,0:T(8,128)(2,1)S(1)}, bf16[1,1024,128]{2,1,0:T(8,128)(2,1)S(1)}, bf16[1,1024,128]{2,1,0:T(8,128)(2,1)S(1)}) custom-call(bf16[1024,512]{1,0:T(8,128)(2,1)S(1)} %copy-done.1, bf16[512,2048]{1,0:T(8,128)(2,1)S(1)} %copy-done, ...), custom_call_target="tpu_custom_call" | custom-call | flops 671088640 | bytes 5767168 | tf_op jit(solution)/shard_map/base/pallas_call | solution.py:24
  49.3 0.7 copy-done.3
  50.0 0.7 copy-done.5
  50.7 1.0 collective-permute-done.4
  51.7 0.1 fusion.4
  51.7 1.9 %collective-permute-start.5 = (bf16[1024,128]{1,0:T(8,128)(2,1)S(1)}, bf16[1024,128]{1,0:T(8,128)(2,1)S(1)}, u32[]{:S(2)}, u32[]{:S(2)}) collective-permute-start(bf16[1024,128]{1,0:T(8,128)(2,1)S(1)} %fusion.4), channel_id=1, source_target_pairs={{0,2},{1,3},{2,4},{3,5},{4,6},{5,7},{6,8},{7,9},{8,10},{9,11},{10,... | collective-permute-start | bytes 786440 | tf_op jit(solution)/shard_map/ppermute | solution.py:73
  53.7 0.1 collective-permute-done.6
  53.8 0.1 fusion.3
  53.9 4.5 %collective-permute-start.7 = (bf16[1024,128]{1,0:T(8,128)(2,1)S(1)}, bf16[1024,128]{1,0:T(8,128)(2,1)S(1)}, u32[]{:S(2)}, u32[]{:S(2)}) collective-permute-start(bf16[1024,128]{1,0:T(8,128)(2,1)S(1)} %fusion.3), channel_id=1, source_target_pairs={{0,14},{1,15},{2,0},{3,1},{4,2},{5,3},{6,4},{7,5},{8,6},{9,7},{10,... | collective-permute-start | bytes 786440 | tf_op jit(solution)/shard_map/ppermute | solution.py:73
  58.4 3.1 %collective-permute-done.5 = bf16[1024,128]{1,0:T(8,128)(2,1)S(1)} collective-permute-done((bf16[1024,128]{1,0:T(8,128)(2,1)S(1)}, bf16[1024,128]{1,0:T(8,128)(2,1)S(1)}, u32[]{:S(2)}, u32[]{:S(2)}) %collective-permute-start.5) | collective-permute-done | bytes 262176 | tf_op jit(solution)/shard_map/ppermute | solution.py:73
  61.4 1.1 collective-permute-done.7
  62.5 1.2 copy-done.2
  63.7 0.1 keep.1.weight_ref
  63.8 4.9 %all-to-all-done.rows_hbm = bf16[32,64,512]{2,1,0:T(8,128)(2,1)} async-done(((bf16[32,64,512]{2,1,0:T(8,128)(2,1)}), bf16[32,64,512]{2,1,0:T(8,128)(2,1)}, u32[]{:S(2)}, u32[]{:S(2)}) %all-to-all-start) | async-done | bytes 2097184 | tf_op jit(solution)/shard_map/all_to_all | solution.py:339
  68.7 4.0 %down.1 = bf16[16,64,128]{2,1,0:T(8,128)(2,1)S(1)} custom-call(bf16[32,64,512]{2,1,0:T(8,128)(2,1)} %all-to-all-done.rows_hbm, bf16[16,64,512]{2,1,0:T(8,128)(2,1)S(1)} %keep.1.weight_ref), custom_call_target="tpu_custom_call" | custom-call | flops 536870912 | bytes 3145728 | tf_op jit(solution)/shard_map/down/pallas_call | solution.py:241
  72.7 0.0 copy-start.7
  72.7 4.0 %all-gather = bf16[32,64,128]{2,1,0:T(8,128)(2,1)S(1)} all-gather(bf16[16,64,128]{2,1,0:T(8,128)(2,1)S(1)} %down.1), channel_id=2, replica_groups={{0,1},{2,3},{4,5},{6,7},{8,9},{10,11},{12,13},{14,15},{16,17},{18,19},{..., dimensions={0}, use_global_device_ids=true | all-gather | bytes 786432 | tf_op jit(solution)/shard_map/all_gather | solution.py:345
  76.8 0.0 copy-start.6
  76.8 0.0 copy-start.4
  76.8 14.6 %all_to_all.25 = bf16[8,64,128]{2,1,0:T(8,128)(2,1)S(1)} all-to-all(bf16[8,64,128]{2,1,0:T(8,128)(2,1)S(1)} %fusion.6), channel_id=1, replica_groups={{0,2,4,6,8,10,12,14},{1,3,5,7,9,11,13,15},{16,18,20,22,24,26,28,30},{17..., dimensions={0} | all-to-all | bytes 262144 | tf_op jit(solution)/shard_map/all_to_all | solution.py:339
  91.5 10.4 %all_to_all.26 = bf16[8,64,128]{2,1,0:T(8,128)(2,1)S(1)} all-to-all(bf16[8,64,128]{2,1,0:T(8,128)(2,1)S(1)} %broadcast_in_dim.2), channel_id=1, replica_groups={{0,2,4,6,8,10,12,14},{1,3,5,7,9,11,13,15},{16,18,20,22,24,26,28,30},{17..., dimensions={0} | all-to-all | bytes 262144 | tf_op jit(solution)/shard_map/all_to_all | solution.py:339
  101.9 4.9 %all_gather.11.lowered_ref = bf16[16,64,128]{2,1,0:T(8,128)(2,1)S(1)} all-gather(bf16[8,64,128]{2,1,0:T(8,128)(2,1)S(1)} %all_to_all.26), channel_id=1, replica_groups={{0,1},{2,3},{4,5},{6,7},{8,9},{10,11},{12,13},{14,15},{16,17},{18,19},{..., dimensions={0}, use_global_device_ids=true | all-gather | bytes 393216 | tf_op jit(solution)/shard_map/all_gather | solution.py:354
  106.9 1.3 up.1
  108.2 6.0 %all-to-all-start.3 = ((bf16[32,64,128]{2,1,0:T(8,128)(2,1)}), bf16[32,64,128]{2,1,0:T(8,128)(2,1)S(1)}, u32[]{:S(2)}, u32[]{:S(2)}) async-start(bf16[32,64,128]{2,1,0:T(8,128)(2,1)} %bitcast.9), calls=%async_computation.3 | async-start | bytes 1048576 | tf_op jit(solution)/shard_map/all_to_all | solution.py:339
  114.2 0.1 fusion
  114.3 0.0 copy-start.10
  114.3 2.1 %collective-permute-start.9 = (bf16[1024,128]{1,0:T(8,128)(2,1)S(1)}, bf16[1024,128]{1,0:T(8,128)(2,1)S(1)}, u32[]{:S(2)}, u32[]{:S(2)}) collective-permute-start(bf16[1024,128]{1,0:T(8,128)(2,1)S(1)} %fusion), channel_id=1, source_target_pairs={{0,14},{1,15},{2,0},{3,1},{4,2},{5,3},{6,4},{7,5},{8,6},{9,7},{10,... | collective-permute-start | bytes 786440 | tf_op jit(solution)/shard_map/ppermute | solution.py:73
  116.3 0.1 fusion.1
  116.4 3.4 %collective-permute-start.8 = (bf16[1024,128]{1,0:T(8,128)(2,1)S(1)}, bf16[1024,128]{1,0:T(8,128)(2,1)S(1)}, u32[]{:S(2)}, u32[]{:S(2)}) collective-permute-start(bf16[1024,128]{1,0:T(8,128)(2,1)S(1)} %fusion.1), channel_id=1, source_target_pairs={{0,2},{1,3},{2,4},{3,5},{4,6},{5,7},{6,8},{7,9},{8,10},{9,11},{10,... | collective-permute-start | bytes 786440 | tf_op jit(solution)/shard_map/ppermute | solution.py:73
  119.8 0.0 copy-done.9
  119.8 0.1 copy.13
  119.9 0.1 reshape.47.accepted_ref
  120.0 3.3 %collective-permute-done.9 = bf16[1024,128]{1,0:T(8,128)(2,1)S(1)} collective-permute-done((bf16[1024,128]{1,0:T(8,128)(2,1)S(1)}, bf16[1024,128]{1,0:T(8,128)(2,1)S(1)}, u32[]{:S(2)}, u32[]{:S(2)}) %collective-permute-start.9) | collective-permute-done | bytes 262176 | tf_op jit(solution)/shard_map/ppermute | solution.py:73
  123.4 3.1 %collective-permute-done.8 = bf16[1024,128]{1,0:T(8,128)(2,1)S(1)} collective-permute-done((bf16[1024,128]{1,0:T(8,128)(2,1)S(1)}, bf16[1024,128]{1,0:T(8,128)(2,1)S(1)}, u32[]{:S(2)}, u32[]{:S(2)}) %collective-permute-start.8) | collective-permute-done | bytes 262176 | tf_op jit(solution)/shard_map/ppermute | solution.py:73
  126.4 0.1 fusion.2.base_ref
  126.6 0.9 prepare.1
  127.5 0.8 all-to-all-done.3
  128.3 0.9 choose.1
  129.2 8.1 %all-to-all-start.4 = ((bf16[32,4,128]{2,1,0:T(4,128)(2,1)}), bf16[32,4,128]{2,1,0:T(4,128)(2,1)S(1)}, u32[]{:S(2)}, u32[]{:S(2)}) async-start(bf16[32,4,128]{2,1,0:T(4,128)(2,1)} %bitcast.14), calls=%async_computation.4 | async-start | bytes 65536 | tf_op jit(solution)/shard_map/all_to_all | solution.py:339
  137.4 0.1 copy.14
  137.4 0.1 reshape.48.targets_ref
  137.5 2.4 %finish.1 = bf16[1024,128]{1,0:T(8,128)(2,1)} custom-call(s32[1,1024]{1,0:T(1,128)S(1)} %copy-done.8, bf16[2048,128]{1,0:T(8,128)(2,1)S(1)} %bitcast.30, f32[1024,128]{1,0:T(8,128)S(1)} %fusion.2.base_ref), custom_call_target="tpu_custom_call" | custom-call | flops 536870912 | bytes 1314816 | tf_op jit(solution)/shard_map/finish/pallas_call | solution.py:24
  140.0 6.1 %all-to-all-done.4 = bf16[32,4,128]{2,1,0:T(4,128)(2,1)S(1)} async-done(((bf16[32,4,128]{2,1,0:T(4,128)(2,1)}), bf16[32,4,128]{2,1,0:T(4,128)(2,1)S(1)}, u32[]{:S(2)}, u32[]{:S(2)}) %all-to-all-start.4) | async-done | bytes 32800 | tf_op jit(solution)/shard_map/all_to_all | solution.py:339
  146.1 0.8 cache.1
  (14 shorter events, 0.1 us)
Async XLA Ops:
  5.6 14.2 %copy-start = (bf16[512,2048]{1,0:T(8,128)(2,1)S(1)}, bf16[512,2048]{1,0:T(8,128)(2,1)}, u32[]{:S(2)}) copy-start(bf16[512,2048]{1,0:T(8,128)(2,1)} %weight_ref.8) | copy-start | bytes 6291460
  5.7 14.2 %copy-start.1 = (bf16[1024,512]{1,0:T(8,128)(2,1)S(1)}, bf16[1024,512]{1,0:T(8,128)(2,1)}, u32[]{:S(2)}) copy-start(bf16[1024,512]{1,0:T(8,128)(2,1)} %tokens_ref.3) | copy-start | bytes 3145732
  5.7 63.0 %all-to-all-start = ((bf16[32,64,512]{2,1,0:T(8,128)(2,1)}), bf16[32,64,512]{2,1,0:T(8,128)(2,1)}, u32[]{:S(2)}, u32[]{:S(2)}) async-start(bf16[32,64,512]{2,1,0:T(8,128)(2,1)} %bitcast.35), calls=%async_computation | async-start | bytes 4194304 | tf_op jit(solution)/shard_map/all_to_all | solution.py:339
  22.4 25.3 %collective-permute-start = (bf16[5,1024,128]{2,1,0:T(8,128)(2,1)S(1)}, bf16[5,1024,128]{2,1,0:T(8,128)(2,1)S(1)}, u32[]{:S(2)}, u32[]{:S(2)}) collective-permute-start(bf16[5,1024,128]{2,1,0:T(8,128)(2,1)S(1)} %base.5), channel_id=1, source_target_pairs={{0,1},{1,0},{2,3},{3,2},{4,5},{5,4},{6,7},{7,6},{8,9},{9,8},{10,11... | collective-permute-start | bytes 3932168 | tf_op jit(solution)/shard_map/ppermute | solution.py:85
  25.3 4.2 %collective-permute-start.1 = (bf16[3,1024,128]{2,1,0:T(8,128)(2,1)S(1)}, bf16[3,1024,128]{2,1,0:T(8,128)(2,1)S(1)}, u32[]{:S(2)}, u32[]{:S(2)}) collective-permute-start(bf16[3,1024,128]{2,1,0:T(8,128)(2,1)S(1)} %base.4), channel_id=1, source_target_pairs={{0,1},{1,0},{2,3},{3,2},{4,5},{5,4},{6,7},{7,6},{8,9},{9,8},{10,11... | collective-permute-start | bytes 2359304 | tf_op jit(solution)/shard_map/ppermute | solution.py:82
  30.5 9.0 %collective-permute-start.2 = (bf16[512,128]{1,0:T(8,128)(2,1)S(1)}, bf16[512,128]{1,0:T(8,128)(2,1)S(1)}, u32[]{:S(2)}, u32[]{:S(2)}) collective-permute-start(bf16[512,128]{1,0:T(8,128)(2,1)S(1)} %bitcast.34), channel_id=1, source_target_pairs={{0,2},{1,3},{2,4},{3,5},{4,6},{5,7},{6,8},{7,9},{8,10},{9,11},{10,... | collective-permute-start | bytes 393224 | tf_op jit(solution)/shard_map/ppermute | solution.py:73
  33.7 6.6 %collective-permute-start.3 = (bf16[512,128]{1,0:T(8,128)(2,1)S(1)}, bf16[512,128]{1,0:T(8,128)(2,1)S(1)}, u32[]{:S(2)}, u32[]{:S(2)}) collective-permute-start(bf16[512,128]{1,0:T(8,128)(2,1)S(1)} %bitcast.33), channel_id=1, source_target_pairs={{0,14},{1,15},{2,0},{3,1},{4,2},{5,3},{6,4},{7,5},{8,6},{9,7},{10,... | collective-permute-start | bytes 393224 | tf_op jit(solution)/shard_map/ppermute | solution.py:73
  40.4 11.3 %collective-permute-start.4 = (bf16[1024,128]{1,0:T(8,128)(2,1)S(1)}, bf16[1024,128]{1,0:T(8,128)(2,1)S(1)}, u32[]{:S(2)}, u32[]{:S(2)}) collective-permute-start(bf16[1024,128]{1,0:T(8,128)(2,1)S(1)} %get-tuple-element.36), channel_id=1, source_target_pairs={{0,2},{1,3},{2,4},{3,5},{4,6},{5,7},{6,8},{7,9},{8,10},{9,11},{10,... | collective-permute-start | bytes 786440 | tf_op jit(solution)/shard_map/ppermute | solution.py:73
  43.6 10.2 %collective-permute-start.6 = (bf16[1024,128]{1,0:T(8,128)(2,1)S(1)}, bf16[1024,128]{1,0:T(8,128)(2,1)S(1)}, u32[]{:S(2)}, u32[]{:S(2)}) collective-permute-start(bf16[1024,128]{1,0:T(8,128)(2,1)S(1)} %get-tuple-element.38), channel_id=1, source_target_pairs={{0,14},{1,15},{2,0},{3,1},{4,2},{5,3},{6,4},{7,5},{8,6},{9,7},{10,... | collective-permute-start | bytes 786440 | tf_op jit(solution)/shard_map/ppermute | solution.py:73
  49.2 0.7 copy-start.3
  49.9 0.7 copy-start.5
  51.7 9.7 %collective-permute-start.5 = (bf16[1024,128]{1,0:T(8,128)(2,1)S(1)}, bf16[1024,128]{1,0:T(8,128)(2,1)S(1)}, u32[]{:S(2)}, u32[]{:S(2)}) collective-permute-start(bf16[1024,128]{1,0:T(8,128)(2,1)S(1)} %fusion.4), channel_id=1, source_target_pairs={{0,2},{1,3},{2,4},{3,5},{4,6},{5,7},{6,8},{7,9},{8,10},{9,11},{10,... | collective-permute-start | bytes 786440 | tf_op jit(solution)/shard_map/ppermute | solution.py:73
  53.9 8.6 %collective-permute-start.7 = (bf16[1024,128]{1,0:T(8,128)(2,1)S(1)}, bf16[1024,128]{1,0:T(8,128)(2,1)S(1)}, u32[]{:S(2)}, u32[]{:S(2)}) collective-permute-start(bf16[1024,128]{1,0:T(8,128)(2,1)S(1)} %fusion.3), channel_id=1, source_target_pairs={{0,14},{1,15},{2,0},{3,1},{4,2},{5,3},{6,4},{7,5},{8,6},{9,7},{10,... | collective-permute-start | bytes 786440 | tf_op jit(solution)/shard_map/ppermute | solution.py:73
  62.5 1.2 copy-start.2
  72.7 34.2 %copy-start.7 = (bf16[16,64,128]{2,1,0:T(8,128)(2,1)S(1)}, bf16[16,64,128]{2,1,0:T(8,128)(2,1)}, u32[]{:S(2)}) copy-start(bf16[16,64,128]{2,1,0:T(8,128)(2,1)} %weight_ref.9) | copy-start | bytes 786436
  76.8 37.4 %copy-start.6 = (bf16[1,1024,128]{2,1,0:T(8,128)(2,1)S(1)}, bf16[1,1024,128]{2,1,0:T(8,128)(2,1)}, u32[]{:S(2)}) copy-start(bf16[1,1024,128]{2,1,0:T(8,128)(2,1)} %copy-done.5) | copy-start | bytes 786436
  76.8 39.5 %copy-start.4 = (bf16[1,1024,128]{2,1,0:T(8,128)(2,1)S(1)}, bf16[1,1024,128]{2,1,0:T(8,128)(2,1)}, u32[]{:S(2)}) copy-start(bf16[1,1024,128]{2,1,0:T(8,128)(2,1)} %copy-done.3) | copy-start | bytes 786436
  101.9 17.9 %copy-start.9 = (s32[1,32,4]{1,2,0:T(4,128)S(1)}, s32[1,32,4]{1,2,0:T(4,128)}, u32[]{:S(2)}) copy-start(s32[1,32,4]{1,2,0:T(4,128)} %param.12) | copy-start | bytes 1540
  108.2 18.4 %copy-start.8 = (s32[1,1024]{1,0:T(1,128)S(1)}, s32[1,1024]{1,0:T(1,128)}, u32[]{:S(2)}) copy-start(s32[1,1024]{1,0:T(1,128)} %get-tuple-element.27.slots_ref) | copy-start | bytes 12292
  108.2 20.1 %all-to-all-start.3 = ((bf16[32,64,128]{2,1,0:T(8,128)(2,1)}), bf16[32,64,128]{2,1,0:T(8,128)(2,1)S(1)}, u32[]{:S(2)}, u32[]{:S(2)}) async-start(bf16[32,64,128]{2,1,0:T(8,128)(2,1)} %bitcast.9), calls=%async_computation.3 | async-start | bytes 1048576 | tf_op jit(solution)/shard_map/all_to_all | solution.py:339
  114.3 23.1 %copy-start.10 = (s32[32,1,4]{0,2,1:T(4,128)S(1)}, s32[32,1,4]{0,2,1:T(4,128)}, u32[]{:S(2)}) copy-start(s32[32,1,4]{0,2,1:T(4,128)} %param.13) | copy-start | bytes 1540
  114.3 9.1 %collective-permute-start.9 = (bf16[1024,128]{1,0:T(8,128)(2,1)S(1)}, bf16[1024,128]{1,0:T(8,128)(2,1)S(1)}, u32[]{:S(2)}, u32[]{:S(2)}) collective-permute-start(bf16[1024,128]{1,0:T(8,128)(2,1)S(1)} %fusion), channel_id=1, source_target_pairs={{0,14},{1,15},{2,0},{3,1},{4,2},{5,3},{6,4},{7,5},{8,6},{9,7},{10,... | collective-permute-start | bytes 786440 | tf_op jit(solution)/shard_map/ppermute | solution.py:73
  116.4 10.0 %collective-permute-start.8 = (bf16[1024,128]{1,0:T(8,128)(2,1)S(1)}, bf16[1024,128]{1,0:T(8,128)(2,1)S(1)}, u32[]{:S(2)}, u32[]{:S(2)}) collective-permute-start(bf16[1024,128]{1,0:T(8,128)(2,1)S(1)} %fusion.1), channel_id=1, source_target_pairs={{0,2},{1,3},{2,4},{3,5},{4,6},{5,7},{6,8},{7,9},{8,10},{9,11},{10,... | collective-permute-start | bytes 786440 | tf_op jit(solution)/shard_map/ppermute | solution.py:73
  129.2 16.9 %all-to-all-start.4 = ((bf16[32,4,128]{2,1,0:T(4,128)(2,1)}), bf16[32,4,128]{2,1,0:T(4,128)(2,1)S(1)}, u32[]{:S(2)}, u32[]{:S(2)}) async-start(bf16[32,4,128]{2,1,0:T(4,128)(2,1)} %bitcast.14), calls=%async_computation.4 | async-start | bytes 65536 | tf_op jit(solution)/shard_map/all_to_all | solution.py:339

commit v9 on v6

--- a/solution.py
+++ b/solution.py
@@ -102,7 +102,7 @@
     up, down = shift(third, 1, groups), shift(fifth, -1, groups)
     up, down = shift(add(second[0], up), 1, groups), shift(add(sixth[0], down), -1, groups)
     down_weight, up, down = lax.optimization_barrier((down_weight, up, down))
-    down_weight = turn(down_weight)
+    down_weight = keep(down_weight)
     after, down_weight = lax.optimization_barrier((after, down_weight))
     up, down = shift(add(first[0], up), 1, groups), shift(add(seventh[0], down), -1, groups)
     return after, down_weight, [mine[0], up, down]
@@ -196,43 +196,25 @@
     )(labels, tokens)
 
 
-def turn_kernel(weight_ref, out_ref):
-    for quad in range(out_ref.shape[0]):
-        for k in range(QUAD):
-            turned = jnp.transpose(weight_ref[quad * QUAD + k])
-            rank = turned.shape[1]
-            out_ref[quad, :, k * rank : (k + 1) * rank] = turned
-
-
-def turn(weight):
-    adapters, rank, features = weight.shape
-    return call(
-        turn_kernel,
-        jax.ShapeDtypeStruct((adapters // QUAD, features, QUAD * rank), BF16),
-        (weight,),
-        0,
-        name="turn",
-    )
-
-
-def down_kernel(rows_hbm, weight_ref, out_ref, rows_ref, sems):
-    quads, sources, tile, features = rows_ref.shape
-    rank = weight_ref.shape[2] // QUAD
-    rows_in = [
-        pltpu.make_async_copy(
-            rows_hbm.at[:, pl.ds(quad * tile, tile), :], rows_ref.at[quad], sems.at[quad]
-        )
-        for quad in range(quads)
-    ]
-    for copy in rows_in:
-        copy.start()
+def keep_kernel(weight_ref, out_ref):
+    out_ref[...] = weight_ref[...]
+
+
+def keep(weight):
+    shape = jax.ShapeDtypeStruct(weight.shape, weight.dtype)
+    return call(keep_kernel, shape, (weight,), 0, name="keep")
+
+
+def down_kernel(rows_ref, weight_ref, out_ref):
+    sources, slots, features = rows_ref.shape
+    rank = weight_ref.shape[1]
+    tile = QUAD * CAP
     owner = lax.broadcasted_iota(jnp.int32, (1, tile, 1), 1) // CAP
-    for quad in range(quads):
-        rows_in[quad].wait()
-        product = jnp.dot(
-            rows_ref[quad].reshape(sources * tile, features),
-            weight_ref[quad],
-            preferred_element_type=F32,
+    for quad in range(slots // tile):
+        rows = rows_ref[:, quad * tile : (quad + 1) * tile, :].reshape(sources * tile, features)
+        weight = weight_ref[quad * QUAD : (quad + 1) * QUAD].reshape(QUAD * rank, features)
+        product = lax.dot_general(
+            rows, weight, (((1,), (1,)), ((), ())), preferred_element_type=F32
         ).reshape(sources, tile, QUAD * rank)
         lowered = jnp.zeros((sources, tile, rank), F32)
         for k in range(QUAD):
@@ -245,25 +227,14 @@
 
 def lower(received, weight):
     sources, slots, features = received.shape
-    rank = weight.shape[2] // QUAD
-    tile = QUAD * CAP
-    return pl.pallas_call(
+    rank = weight.shape[1]
+    return call(
         down_kernel,
-        in_specs=[HBM, VMEM],
-        out_specs=VMEM,
-        out_shape=jax.ShapeDtypeStruct((sources // 2, slots, 2 * rank), BF16),
-        scratch_shapes=[
-            pltpu.VMEM((slots // tile, sources, tile, features), BF16),
-            pltpu.SemaphoreType.DMA((slots // tile,)),
-        ],
-        compiler_params=pltpu.CompilerParams(vmem_limit_bytes=LIMIT),
-        cost_estimate=pl.CostEstimate(
-            flops=2 * sources * slots * features * rank * QUAD,
-            bytes_accessed=2 * (sources * slots * features + slots // CAP * rank * features),
-            transcendentals=0,
-        ),
+        jax.ShapeDtypeStruct((sources // 2, slots, 2 * rank), BF16),
+        (received, weight),
+        2 * sources * slots * features * rank * QUAD,
         name="down",
-    )(received, weight)
+    )
 
 
 def up_kernel(lowered_ref, weight_ref, out_ref):

time: 149 us -> 148 us (level)
  Pallas kernels: 19.7 us -> 17.3 us
    pallas_call x1 -> x0, Pallas kernels: 3.86 us -> none  [lower(): pl.pallas_call(down_kernel, in_specs=[HBM, VMEM], out_specs=VMEM, out_sha...]
    pallas_call x9 -> x10, Pallas kernels: 10.8 us -> 12.3 us  [call(): pl.pallas_call(kernel, out_shape=out_shape, in_specs=[VMEM] * len(operand...]
where the time goes in v9:
time: 148 us; the launch traced here: 147 us
  starting transfers between devices  59 us (40%)
  blocking collectives  34 us (23%)
  waiting for transfers between devices  32.1 us (22%)
  Pallas kernels  17.3 us (12%)
  local copies, waits for them, and re-layouts  3.06 us (2%)
    all_to_all x3, starting transfers between devices, exchange(): lax.all_to_all(array, axis, split_axis=0, concat_axis=0, tiled=True, axis...  28.2 us
    ppermute x8, starting transfers between devices, shift(): lax.ppermute(array, 'tensor', [(i, (i + step) % groups) for i in range(gr...  26 us
    all_to_all x2, blocking collectives, exchange(): lax.all_to_all(array, axis, split_axis=0, concat_axis=0, tiled=True, axis...  25 us
    all_to_all x3, waiting for transfers between devices, exchange(): lax.all_to_all(array, axis, split_axis=0, concat_axis=0, tiled=True, axis...  15.2 us
    ppermute x8, waiting for transfers between devices, shift(): lax.ppermute(array, 'tensor', [(i, (i + step) % groups) for i in range(gr...  14.7 us
    pallas_call x10, Pallas kernels, call(): pl.pallas_call(kernel, out_shape=out_shape, in_specs=[VMEM] * len(operand...  12.3 us
    pallas_call x1, Pallas kernels, pack(): pl.pallas_call(pack_kernel, out_shape=[jax.ShapeDtypeStruct((1, rows), jn...  5.01 us
    all_gather x1, blocking collectives, sum_over_tensor(): lax.all_gather(mine, 'tensor', axis=0, axis_index_groups=pairs, tiled=True)  4.93 us
  transfers between devices with their start and end apart: 13, of which 12 were waited for; matrix products, arithmetic and copies ran while one was open for 1% of the time, Pallas kernels for 4%

profile of v9, /device:TPU:1, one launch (start us, length us, event | category | flops | bytes accessed | tf_op | source)
XLA Modules:
  0.0 147.0 jit_solution(10121732007902671446)
XLA Ops:
  0.6 5.0 %pack.1 = (s32[1,1024]{1,0:T(1,128)}, bf16[2048,512]{1,0:T(8,128)(2,1)}) custom-call(s32[1,1024]{1,0:T(1,128)} %bitcast.36, bf16[1024,512]{1,0:T(8,128)(2,1)} %tokens_ref.3), custom_call_target="tpu_custom_call" | custom-call | flops 2147483648 | bytes 3145728 | tf_op jit(solution)/shard_map/pack/pallas_call | solution.py:175
  5.6 0.0 copy-start
  5.7 0.0 copy-start.1
  5.7 14.1 %all-to-all-start = ((bf16[32,64,512]{2,1,0:T(8,128)(2,1)}), bf16[32,64,512]{2,1,0:T(8,128)(2,1)}, u32[]{:S(2)}, u32[]{:S(2)}) async-start(bf16[32,64,512]{2,1,0:T(8,128)(2,1)} %bitcast.34), calls=%async_computation | async-start | bytes 4194304 | tf_op jit(solution)/shard_map/all_to_all | solution.py:301
  19.8 0.0 copy-done
  19.8 0.0 copy-done.1
  19.8 1.0 base.4
  20.8 1.5 %base.5 = bf16[5,1024,128]{2,1,0:T(8,128)(2,1)S(1)} custom-call(bf16[1024,512]{1,0:T(8,128)(2,1)S(1)} %copy-done.1, bf16[512,2048]{1,0:T(8,128)(2,1)S(1)} %copy-done), custom_call_target="tpu_custom_call" | custom-call | flops 671088640 | bytes 4456448 | tf_op jit(solution)/shard_map/base/pallas_call | solution.py:24
  22.4 2.9 %collective-permute-start = (bf16[5,1024,128]{2,1,0:T(8,128)(2,1)S(1)}, bf16[5,1024,128]{2,1,0:T(8,128)(2,1)S(1)}, u32[]{:S(2)}, u32[]{:S(2)}) collective-permute-start(bf16[5,1024,128]{2,1,0:T(8,128)(2,1)S(1)} %base.5), channel_id=1, source_target_pairs={{0,1},{1,0},{2,3},{3,2},{4,5},{5,4},{6,7},{7,6},{8,9},{9,8},{10,11... | collective-permute-start | bytes 3932168 | tf_op jit(solution)/shard_map/ppermute | solution.py:85
  25.3 1.9 %collective-permute-start.1 = (bf16[3,1024,128]{2,1,0:T(8,128)(2,1)S(1)}, bf16[3,1024,128]{2,1,0:T(8,128)(2,1)S(1)}, u32[]{:S(2)}, u32[]{:S(2)}) collective-permute-start(bf16[3,1024,128]{2,1,0:T(8,128)(2,1)S(1)} %base.4), channel_id=1, source_target_pairs={{0,1},{1,0},{2,3},{3,2},{4,5},{5,4},{6,7},{7,6},{8,9},{9,8},{10,11... | collective-permute-start | bytes 2359304 | tf_op jit(solution)/shard_map/ppermute | solution.py:82
  27.2 2.3 %collective-permute-done.1.rest_0_ = bf16[3,1024,128]{2,1,0:T(8,128)(2,1)S(1)} collective-permute-done((bf16[3,1024,128]{2,1,0:T(8,128)(2,1)S(1)}, bf16[3,1024,128]{2,1,0:T(8,128)(2,1)S(1)}, u32[]{:S(2)}, u32[]{:S(2)}) %collective-permute-start.1) | collective-permute-done | bytes 786464 | tf_op jit(solution)/shard_map/ppermute | solution.py:82
  29.5 1.0 base.7
  30.5 3.2 %collective-permute-start.2 = (bf16[512,128]{1,0:T(8,128)(2,1)S(1)}, bf16[512,128]{1,0:T(8,128)(2,1)S(1)}, u32[]{:S(2)}, u32[]{:S(2)}) collective-permute-start(bf16[512,128]{1,0:T(8,128)(2,1)S(1)} %bitcast.33), channel_id=1, source_target_pairs={{0,2},{1,3},{2,4},{3,5},{4,6},{5,7},{6,8},{7,9},{8,10},{9,11},{10,... | collective-permute-start | bytes 393224 | tf_op jit(solution)/shard_map/ppermute | solution.py:73
  33.7 3.8 %collective-permute-start.3 = (bf16[512,128]{1,0:T(8,128)(2,1)S(1)}, bf16[512,128]{1,0:T(8,128)(2,1)S(1)}, u32[]{:S(2)}, u32[]{:S(2)}) collective-permute-start(bf16[512,128]{1,0:T(8,128)(2,1)S(1)} %bitcast.32), channel_id=1, source_target_pairs={{0,14},{1,15},{2,0},{3,1},{4,2},{5,3},{6,4},{7,5},{8,6},{9,7},{10,... | collective-permute-start | bytes 393224 | tf_op jit(solution)/shard_map/ppermute | solution.py:73
  37.5 1.9 %collective-permute-done.2.up_ref = bf16[512,128]{1,0:T(8,128)(2,1)S(1)} collective-permute-done((bf16[512,128]{1,0:T(8,128)(2,1)S(1)}, bf16[512,128]{1,0:T(8,128)(2,1)S(1)}, u32[]{:S(2)}, u32[]{:S(2)}) %collective-permute-start.2) | collective-permute-done | bytes 131104 | tf_op jit(solution)/shard_map/ppermute | solution.py:73
  39.4 0.9 collective-permute-done.3.down_ref
  40.3 0.1 ring.1
  40.4 3.2 %collective-permute-start.4 = (bf16[1024,128]{1,0:T(8,128)(2,1)S(1)}, bf16[1024,128]{1,0:T(8,128)(2,1)S(1)}, u32[]{:S(2)}, u32[]{:S(2)}) collective-permute-start(bf16[1024,128]{1,0:T(8,128)(2,1)S(1)} %get-tuple-element.35), channel_id=1, source_target_pairs={{0,2},{1,3},{2,4},{3,5},{4,6},{5,7},{6,8},{7,9},{8,10},{9,11},{10,... | collective-permute-start | bytes 786440 | tf_op jit(solution)/shard_map/ppermute | solution.py:73
  43.6 4.1 %collective-permute-start.6 = (bf16[1024,128]{1,0:T(8,128)(2,1)S(1)}, bf16[1024,128]{1,0:T(8,128)(2,1)S(1)}, u32[]{:S(2)}, u32[]{:S(2)}) collective-permute-start(bf16[1024,128]{1,0:T(8,128)(2,1)S(1)} %get-tuple-element.37), channel_id=1, source_target_pairs={{0,14},{1,15},{2,0},{3,1},{4,2},{5,3},{6,4},{7,5},{8,6},{9,7},{10,... | collective-permute-start | bytes 786440 | tf_op jit(solution)/shard_map/ppermute | solution.py:73
  47.7 0.0 collective-permute-done.rest_0_
  47.7 1.6 %base.6 = (bf16[1,1024,128]{2,1,0:T(8,128)(2,1)S(1)}, bf16[1,1024,128]{2,1,0:T(8,128)(2,1)S(1)}, bf16[1,1024,128]{2,1,0:T(8,128)(2,1)S(1)}, bf16[1,1024,128]{2,1,0:T(8,128)(2,1)S(1)}, bf16[1,1024,128]{2,1,0:T(8,128)(2,1)S(1)}) custom-call(bf16[1024,512]{1,0:T(8,128)(2,1)S(1)} %copy-done.1, bf16[512,2048]{1,0:T(8,128)(2,1)S(1)} %copy-done, ...), custom_call_target="tpu_custom_call" | custom-call | flops 671088640 | bytes 5767168 | tf_op jit(solution)/shard_map/base/pallas_call | solution.py:24
  49.3 0.0 copy-start.3
  49.3 0.7 copy-done.3
  50.0 0.7 copy-done.5
  50.7 1.0 collective-permute-done.4
  51.7 0.1 fusion.4
  51.7 1.9 %collective-permute-start.5 = (bf16[1024,128]{1,0:T(8,128)(2,1)S(1)}, bf16[1024,128]{1,0:T(8,128)(2,1)S(1)}, u32[]{:S(2)}, u32[]{:S(2)}) collective-permute-start(bf16[1024,128]{1,0:T(8,128)(2,1)S(1)} %fusion.4), channel_id=1, source_target_pairs={{0,2},{1,3},{2,4},{3,5},{4,6},{5,7},{6,8},{7,9},{8,10},{9,11},{10,... | collective-permute-start | bytes 786440 | tf_op jit(solution)/shard_map/ppermute | solution.py:73
  53.7 0.1 collective-permute-done.6
  53.8 0.1 fusion.3
  53.9 4.5 %collective-permute-start.7 = (bf16[1024,128]{1,0:T(8,128)(2,1)S(1)}, bf16[1024,128]{1,0:T(8,128)(2,1)S(1)}, u32[]{:S(2)}, u32[]{:S(2)}) collective-permute-start(bf16[1024,128]{1,0:T(8,128)(2,1)S(1)} %fusion.3), channel_id=1, source_target_pairs={{0,14},{1,15},{2,0},{3,1},{4,2},{5,3},{6,4},{7,5},{8,6},{9,7},{10,... | collective-permute-start | bytes 786440 | tf_op jit(solution)/shard_map/ppermute | solution.py:73
  58.4 3.1 %collective-permute-done.5 = bf16[1024,128]{1,0:T(8,128)(2,1)S(1)} collective-permute-done((bf16[1024,128]{1,0:T(8,128)(2,1)S(1)}, bf16[1024,128]{1,0:T(8,128)(2,1)S(1)}, u32[]{:S(2)}, u32[]{:S(2)}) %collective-permute-start.5) | collective-permute-done | bytes 262176 | tf_op jit(solution)/shard_map/ppermute | solution.py:73
  61.4 1.1 collective-permute-done.7
  62.5 1.2 copy-done.2
  63.7 0.1 keep.1.weight_ref
  63.8 4.9 %all-to-all-done.rows_ref = bf16[32,64,512]{2,1,0:T(8,128)(2,1)} async-done(((bf16[32,64,512]{2,1,0:T(8,128)(2,1)}), bf16[32,64,512]{2,1,0:T(8,128)(2,1)}, u32[]{:S(2)}, u32[]{:S(2)}) %all-to-all-start) | async-done | bytes 2097184 | tf_op jit(solution)/shard_map/all_to_all | solution.py:301
  68.7 2.6 %down.1 = bf16[16,64,128]{2,1,0:T(8,128)(2,1)S(1)} custom-call(bf16[32,64,512]{2,1,0:T(8,128)(2,1)} %all-to-all-done.rows_ref, bf16[16,64,512]{2,1,0:T(8,128)(2,1)S(1)} %keep.1.weight_ref), custom_call_target="tpu_custom_call" | custom-call | flops 536870912 | bytes 3407872 | tf_op jit(solution)/shard_map/down/pallas_call | solution.py:24
  71.3 0.0 copy-start.7
  71.3 4.0 %all-gather = bf16[32,64,128]{2,1,0:T(8,128)(2,1)S(1)} all-gather(bf16[16,64,128]{2,1,0:T(8,128)(2,1)S(1)} %down.1), channel_id=2, replica_groups={{0,1},{2,3},{4,5},{6,7},{8,9},{10,11},{12,13},{14,15},{16,17},{18,19},{..., dimensions={0}, use_global_device_ids=true | all-gather | bytes 786432 | tf_op jit(solution)/shard_map/all_gather | solution.py:307
  75.4 0.0 copy-start.6
  75.4 14.6 %all_to_all.25 = bf16[8,64,128]{2,1,0:T(8,128)(2,1)S(1)} all-to-all(bf16[8,64,128]{2,1,0:T(8,128)(2,1)S(1)} %fusion.6), channel_id=1, replica_groups={{0,2,4,6,8,10,12,14},{1,3,5,7,9,11,13,15},{16,18,20,22,24,26,28,30},{17..., dimensions={0} | all-to-all | bytes 262144 | tf_op jit(solution)/shard_map/all_to_all | solution.py:301
  90.1 10.4 %all_to_all.26 = bf16[8,64,128]{2,1,0:T(8,128)(2,1)S(1)} all-to-all(bf16[8,64,128]{2,1,0:T(8,128)(2,1)S(1)} %broadcast_in_dim.2), channel_id=1, replica_groups={{0,2,4,6,8,10,12,14},{1,3,5,7,9,11,13,15},{16,18,20,22,24,26,28,30},{17..., dimensions={0} | all-to-all | bytes 262144 | tf_op jit(solution)/shard_map/all_to_all | solution.py:301
  100.6 4.9 %all_gather.11.lowered_ref = bf16[16,64,128]{2,1,0:T(8,128)(2,1)S(1)} all-gather(bf16[8,64,128]{2,1,0:T(8,128)(2,1)S(1)} %all_to_all.26), channel_id=1, replica_groups={{0,1},{2,3},{4,5},{6,7},{8,9},{10,11},{12,13},{14,15},{16,17},{18,19},{..., dimensions={0}, use_global_device_ids=true | all-gather | bytes 393216 | tf_op jit(solution)/shard_map/all_gather | solution.py:316
  105.5 1.3 up.1
  106.8 6.0 %all-to-all-start.3 = ((bf16[32,64,128]{2,1,0:T(8,128)(2,1)}), bf16[32,64,128]{2,1,0:T(8,128)(2,1)S(1)}, u32[]{:S(2)}, u32[]{:S(2)}) async-start(bf16[32,64,128]{2,1,0:T(8,128)(2,1)} %bitcast.9), calls=%async_computation.3 | async-start | bytes 1048576 | tf_op jit(solution)/shard_map/all_to_all | solution.py:301
  112.8 0.1 fusion
  112.9 0.0 copy-start.10
  112.9 2.1 %collective-permute-start.9 = (bf16[1024,128]{1,0:T(8,128)(2,1)S(1)}, bf16[1024,128]{1,0:T(8,128)(2,1)S(1)}, u32[]{:S(2)}, u32[]{:S(2)}) collective-permute-start(bf16[1024,128]{1,0:T(8,128)(2,1)S(1)} %fusion), channel_id=1, source_target_pairs={{0,14},{1,15},{2,0},{3,1},{4,2},{5,3},{6,4},{7,5},{8,6},{9,7},{10,... | collective-permute-start | bytes 786440 | tf_op jit(solution)/shard_map/ppermute | solution.py:73
  114.9 0.0 copy-done.4
  115.0 0.1 fusion.1
  115.0 3.2 %collective-permute-start.8 = (bf16[1024,128]{1,0:T(8,128)(2,1)S(1)}, bf16[1024,128]{1,0:T(8,128)(2,1)S(1)}, u32[]{:S(2)}, u32[]{:S(2)}) collective-permute-start(bf16[1024,128]{1,0:T(8,128)(2,1)S(1)} %fusion.1), channel_id=1, source_target_pairs={{0,2},{1,3},{2,4},{3,5},{4,6},{5,7},{6,8},{7,9},{8,10},{9,11},{10,... | collective-permute-start | bytes 786440 | tf_op jit(solution)/shard_map/ppermute | solution.py:73
  118.3 0.0 copy-done.9
  118.3 0.1 copy.13
  118.4 0.1 reshape.47.accepted_ref
  118.5 3.5 %collective-permute-done.9 = bf16[1024,128]{1,0:T(8,128)(2,1)S(1)} collective-permute-done((bf16[1024,128]{1,0:T(8,128)(2,1)S(1)}, bf16[1024,128]{1,0:T(8,128)(2,1)S(1)}, u32[]{:S(2)}, u32[]{:S(2)}) %collective-permute-start.9) | collective-permute-done | bytes 262176 | tf_op jit(solution)/shard_map/ppermute | solution.py:73
  122.0 3.1 %collective-permute-done.8 = bf16[1024,128]{1,0:T(8,128)(2,1)S(1)} collective-permute-done((bf16[1024,128]{1,0:T(8,128)(2,1)S(1)}, bf16[1024,128]{1,0:T(8,128)(2,1)S(1)}, u32[]{:S(2)}, u32[]{:S(2)}) %collective-permute-start.8) | collective-permute-done | bytes 262176 | tf_op jit(solution)/shard_map/ppermute | solution.py:73
  125.0 0.1 fusion.2.base_ref
  125.2 1.7 %all-to-all-done.3 = bf16[32,64,128]{2,1,0:T(8,128)(2,1)S(1)} async-done(((bf16[32,64,128]{2,1,0:T(8,128)(2,1)}), bf16[32,64,128]{2,1,0:T(8,128)(2,1)S(1)}, u32[]{:S(2)}, u32[]{:S(2)}) %all-to-all-start.3) | async-done | bytes 524320 | tf_op jit(solution)/shard_map/all_to_all | solution.py:301
  126.9 2.4 %finish.1 = (bf16[1024,128]{1,0:T(8,128)(2,1)}, bf16[128,128]{1,0:T(8,128)(2,1)}) custom-call(s32[1,1024]{1,0:T(1,128)S(1)} %copy-done.8, bf16[2048,128]{1,0:T(8,128)(2,1)S(1)} %bitcast.30, f32[1024,128]{1,0:T(8,128)S(1)} %fusion.2.base_ref, s32[1,128]{1,0:T(1,128)S(1)} %reshape.47.accepted_ref), custom_call_target="tpu_custom_call" | custom-call | flops 536870912 | bytes 1348096 | tf_op jit(solution)/shard_map/finish/pallas_call | solution.py:24
  129.3 8.1 %all-to-all-start.4 = ((bf16[32,4,128]{2,1,0:T(4,128)(2,1)}), bf16[32,4,128]{2,1,0:T(4,128)(2,1)S(1)}, u32[]{:S(2)}, u32[]{:S(2)}) async-start(bf16[32,4,128]{2,1,0:T(4,128)(2,1)} %bitcast.14), calls=%async_computation.4 | async-start | bytes 65536 | tf_op jit(solution)/shard_map/all_to_all | solution.py:301
  137.5 0.0 copy-done.10
  137.5 0.1 copy.14
  137.6 0.1 reshape.48.targets_ref
  137.7 8.6 %all-to-all-done.4 = bf16[32,4,128]{2,1,0:T(4,128)(2,1)S(1)} async-done(((bf16[32,4,128]{2,1,0:T(4,128)(2,1)}), bf16[32,4,128]{2,1,0:T(4,128)(2,1)S(1)}, u32[]{:S(2)}, u32[]{:S(2)}) %all-to-all-start.4) | async-done | bytes 32800 | tf_op jit(solution)/shard_map/all_to_all | solution.py:301
  146.3 0.8 cache.1
  (12 shorter events, 0.1 us)
Async XLA Ops:
  5.6 14.2 %copy-start = (bf16[512,2048]{1,0:T(8,128)(2,1)S(1)}, bf16[512,2048]{1,0:T(8,128)(2,1)}, u32[]{:S(2)}) copy-start(bf16[512,2048]{1,0:T(8,128)(2,1)} %weight_ref.8) | copy-start | bytes 6291460
  5.7 14.2 %copy-start.1 = (bf16[1024,512]{1,0:T(8,128)(2,1)S(1)}, bf16[1024,512]{1,0:T(8,128)(2,1)}, u32[]{:S(2)}) copy-start(bf16[1024,512]{1,0:T(8,128)(2,1)} %tokens_ref.3) | copy-start | bytes 3145732
  5.7 63.0 %all-to-all-start = ((bf16[32,64,512]{2,1,0:T(8,128)(2,1)}), bf16[32,64,512]{2,1,0:T(8,128)(2,1)}, u32[]{:S(2)}, u32[]{:S(2)}) async-start(bf16[32,64,512]{2,1,0:T(8,128)(2,1)} %bitcast.34), calls=%async_computation | async-start | bytes 4194304 | tf_op jit(solution)/shard_map/all_to_all | solution.py:301
  22.4 25.3 %collective-permute-start = (bf16[5,1024,128]{2,1,0:T(8,128)(2,1)S(1)}, bf16[5,1024,128]{2,1,0:T(8,128)(2,1)S(1)}, u32[]{:S(2)}, u32[]{:S(2)}) collective-permute-start(bf16[5,1024,128]{2,1,0:T(8,128)(2,1)S(1)} %base.5), channel_id=1, source_target_pairs={{0,1},{1,0},{2,3},{3,2},{4,5},{5,4},{6,7},{7,6},{8,9},{9,8},{10,11... | collective-permute-start | bytes 3932168 | tf_op jit(solution)/shard_map/ppermute | solution.py:85
  25.3 4.2 %collective-permute-start.1 = (bf16[3,1024,128]{2,1,0:T(8,128)(2,1)S(1)}, bf16[3,1024,128]{2,1,0:T(8,128)(2,1)S(1)}, u32[]{:S(2)}, u32[]{:S(2)}) collective-permute-start(bf16[3,1024,128]{2,1,0:T(8,128)(2,1)S(1)} %base.4), channel_id=1, source_target_pairs={{0,1},{1,0},{2,3},{3,2},{4,5},{5,4},{6,7},{7,6},{8,9},{9,8},{10,11... | collective-permute-start | bytes 2359304 | tf_op jit(solution)/shard_map/ppermute | solution.py:82
  30.5 9.0 %collective-permute-start.2 = (bf16[512,128]{1,0:T(8,128)(2,1)S(1)}, bf16[512,128]{1,0:T(8,128)(2,1)S(1)}, u32[]{:S(2)}, u32[]{:S(2)}) collective-permute-start(bf16[512,128]{1,0:T(8,128)(2,1)S(1)} %bitcast.33), channel_id=1, source_target_pairs={{0,2},{1,3},{2,4},{3,5},{4,6},{5,7},{6,8},{7,9},{8,10},{9,11},{10,... | collective-permute-start | bytes 393224 | tf_op jit(solution)/shard_map/ppermute | solution.py:73
  33.7 6.6 %collective-permute-start.3 = (bf16[512,128]{1,0:T(8,128)(2,1)S(1)}, bf16[512,128]{1,0:T(8,128)(2,1)S(1)}, u32[]{:S(2)}, u32[]{:S(2)}) collective-permute-start(bf16[512,128]{1,0:T(8,128)(2,1)S(1)} %bitcast.32), channel_id=1, source_target_pairs={{0,14},{1,15},{2,0},{3,1},{4,2},{5,3},{6,4},{7,5},{8,6},{9,7},{10,... | collective-permute-start | bytes 393224 | tf_op jit(solution)/shard_map/ppermute | solution.py:73
  40.4 11.3 %collective-permute-start.4 = (bf16[1024,128]{1,0:T(8,128)(2,1)S(1)}, bf16[1024,128]{1,0:T(8,128)(2,1)S(1)}, u32[]{:S(2)}, u32[]{:S(2)}) collective-permute-start(bf16[1024,128]{1,0:T(8,128)(2,1)S(1)} %get-tuple-element.35), channel_id=1, source_target_pairs={{0,2},{1,3},{2,4},{3,5},{4,6},{5,7},{6,8},{7,9},{8,10},{9,11},{10,... | collective-permute-start | bytes 786440 | tf_op jit(solution)/shard_map/ppermute | solution.py:73
  43.6 10.2 %collective-permute-start.6 = (bf16[1024,128]{1,0:T(8,128)(2,1)S(1)}, bf16[1024,128]{1,0:T(8,128)(2,1)S(1)}, u32[]{:S(2)}, u32[]{:S(2)}) collective-permute-start(bf16[1024,128]{1,0:T(8,128)(2,1)S(1)} %get-tuple-element.37), channel_id=1, source_target_pairs={{0,14},{1,15},{2,0},{3,1},{4,2},{5,3},{6,4},{7,5},{8,6},{9,7},{10,... | collective-permute-start | bytes 786440 | tf_op jit(solution)/shard_map/ppermute | solution.py:73
  49.3 0.7 copy-start.3
  50.0 0.7 copy-start.5
  51.7 9.7 %collective-permute-start.5 = (bf16[1024,128]{1,0:T(8,128)(2,1)S(1)}, bf16[1024,128]{1,0:T(8,128)(2,1)S(1)}, u32[]{:S(2)}, u32[]{:S(2)}) collective-permute-start(bf16[1024,128]{1,0:T(8,128)(2,1)S(1)} %fusion.4), channel_id=1, source_target_pairs={{0,2},{1,3},{2,4},{3,5},{4,6},{5,7},{6,8},{7,9},{8,10},{9,11},{10,... | collective-permute-start | bytes 786440 | tf_op jit(solution)/shard_map/ppermute | solution.py:73
  53.9 8.6 %collective-permute-start.7 = (bf16[1024,128]{1,0:T(8,128)(2,1)S(1)}, bf16[1024,128]{1,0:T(8,128)(2,1)S(1)}, u32[]{:S(2)}, u32[]{:S(2)}) collective-permute-start(bf16[1024,128]{1,0:T(8,128)(2,1)S(1)} %fusion.3), channel_id=1, source_target_pairs={{0,14},{1,15},{2,0},{3,1},{4,2},{5,3},{6,4},{7,5},{8,6},{9,7},{10,... | collective-permute-start | bytes 786440 | tf_op jit(solution)/shard_map/ppermute | solution.py:73
  62.5 1.2 copy-start.2
  71.3 34.2 %copy-start.7 = (bf16[16,64,128]{2,1,0:T(8,128)(2,1)S(1)}, bf16[16,64,128]{2,1,0:T(8,128)(2,1)}, u32[]{:S(2)}) copy-start(bf16[16,64,128]{2,1,0:T(8,128)(2,1)} %weight_ref.9) | copy-start | bytes 786436
  75.4 37.4 %copy-start.6 = (bf16[1,1024,128]{2,1,0:T(8,128)(2,1)S(1)}, bf16[1,1024,128]{2,1,0:T(8,128)(2,1)}, u32[]{:S(2)}) copy-start(bf16[1,1024,128]{2,1,0:T(8,128)(2,1)} %copy-done.5) | copy-start | bytes 786436
  75.4 39.5 %copy-start.4 = (bf16[1,1024,128]{2,1,0:T(8,128)(2,1)S(1)}, bf16[1,1024,128]{2,1,0:T(8,128)(2,1)}, u32[]{:S(2)}) copy-start(bf16[1,1024,128]{2,1,0:T(8,128)(2,1)} %copy-done.3) | copy-start | bytes 786436
  100.6 17.7 %copy-start.9 = (s32[1,32,4]{1,2,0:T(4,128)S(1)}, s32[1,32,4]{1,2,0:T(4,128)}, u32[]{:S(2)}) copy-start(s32[1,32,4]{1,2,0:T(4,128)} %param.12) | copy-start | bytes 1540
  106.8 20.1 %copy-start.8 = (s32[1,1024]{1,0:T(1,128)S(1)}, s32[1,1024]{1,0:T(1,128)}, u32[]{:S(2)}) copy-start(s32[1,1024]{1,0:T(1,128)} %get-tuple-element.26.slots_ref) | copy-start | bytes 12292
  106.8 20.1 %all-to-all-start.3 = ((bf16[32,64,128]{2,1,0:T(8,128)(2,1)}), bf16[32,64,128]{2,1,0:T(8,128)(2,1)S(1)}, u32[]{:S(2)}, u32[]{:S(2)}) async-start(bf16[32,64,128]{2,1,0:T(8,128)(2,1)} %bitcast.9), calls=%async_computation.3 | async-start | bytes 1048576 | tf_op jit(solution)/shard_map/all_to_all | solution.py:301
  112.9 24.6 %copy-start.10 = (s32[32,1,4]{0,2,1:T(4,128)S(1)}, s32[32,1,4]{0,2,1:T(4,128)}, u32[]{:S(2)}) copy-start(s32[32,1,4]{0,2,1:T(4,128)} %param.13) | copy-start | bytes 1540
  112.9 9.1 %collective-permute-start.9 = (bf16[1024,128]{1,0:T(8,128)(2,1)S(1)}, bf16[1024,128]{1,0:T(8,128)(2,1)S(1)}, u32[]{:S(2)}, u32[]{:S(2)}) collective-permute-start(bf16[1024,128]{1,0:T(8,128)(2,1)S(1)} %fusion), channel_id=1, source_target_pairs={{0,14},{1,15},{2,0},{3,1},{4,2},{5,3},{6,4},{7,5},{8,6},{9,7},{10,... | collective-permute-start | bytes 786440 | tf_op jit(solution)/shard_map/ppermute | solution.py:73
  115.0 10.0 %collective-permute-start.8 = (bf16[1024,128]{1,0:T(8,128)(2,1)S(1)}, bf16[1024,128]{1,0:T(8,128)(2,1)S(1)}, u32[]{:S(2)}, u32[]{:S(2)}) collective-permute-start(bf16[1024,128]{1,0:T(8,128)(2,1)S(1)} %fusion.1), channel_id=1, source_target_pairs={{0,2},{1,3},{2,4},{3,5},{4,6},{5,7},{6,8},{7,9},{8,10},{9,11},{10,... | collective-permute-start | bytes 786440 | tf_op jit(solution)/shard_map/ppermute | solution.py:73
  129.3 16.9 %all-to-all-start.4 = ((bf16[32,4,128]{2,1,0:T(4,128)(2,1)}), bf16[32,4,128]{2,1,0:T(4,128)(2,1)S(1)}, u32[]{:S(2)}, u32[]{:S(2)}) async-start(bf16[32,4,128]{2,1,0:T(4,128)(2,1)} %bitcast.14), calls=%async_computation.4 | async-start | bytes 65536 | tf_op jit(solution)/shard_map/all_to_all | solution.py:301

commit v10 on v8

--- a/solution.py
+++ b/solution.py
@@ -205,25 +205,16 @@
     return call(keep_kernel, shape, (weight,), 0, name="keep")
 
 
-def down_kernel(rows_hbm, weight_ref, out_ref, rows_ref, sems):
-    quads, sources, tile, features = rows_ref.shape
+def down_kernel(rows_ref, weight_ref, out_ref):
+    sources, slots, features = rows_ref.shape
     rank = weight_ref.shape[1]
-    rows_in = [
-        pltpu.make_async_copy(
-            rows_hbm.at[:, pl.ds(quad * tile, tile), :], rows_ref.at[quad], sems.at[quad]
-        )
-        for quad in range(quads)
-    ]
-    for copy in rows_in:
-        copy.start()
+    tile = QUAD * CAP
     owner = lax.broadcasted_iota(jnp.int32, (1, tile, 1), 1) // CAP
-    for quad in range(quads):
-        rows_in[quad].wait()
+    for quad in range(slots // tile):
+        rows = rows_ref[:, quad * tile : (quad + 1) * tile, :].reshape(sources * tile, features)
+        weight = weight_ref[quad * QUAD : (quad + 1) * QUAD].reshape(QUAD * rank, features)
         product = lax.dot_general(
-            rows_ref[quad].reshape(sources * tile, features),
-            weight_ref[quad * QUAD : (quad + 1) * QUAD].reshape(QUAD * rank, features),
-            (((1,), (1,)), ((), ())),
-            preferred_element_type=F32,
+            rows, weight, (((1,), (1,)), ((), ())), preferred_element_type=F32
         ).reshape(sources, tile, QUAD * rank)
         lowered = jnp.zeros((sources, tile, rank), F32)
         for k in range(QUAD):
@@ -237,24 +228,13 @@
 def lower(received, weight):
     sources, slots, features = received.shape
     rank = weight.shape[1]
-    tile = QUAD * CAP
-    return pl.pallas_call(
+    return call(
         down_kernel,
-        in_specs=[HBM, VMEM],
-        out_specs=VMEM,
-        out_shape=jax.ShapeDtypeStruct((sources // 2, slots, 2 * rank), BF16),
-        scratch_shapes=[
-            pltpu.VMEM((slots // tile, sources, tile, features), BF16),
-            pltpu.SemaphoreType.DMA((slots // tile,)),
-        ],
-        compiler_params=pltpu.CompilerParams(vmem_limit_bytes=LIMIT),
-        cost_estimate=pl.CostEstimate(
-            flops=2 * sources * slots * features * rank * QUAD,
-            bytes_accessed=2 * (sources * slots * features + slots // CAP * rank * features),
-            transcendentals=0,
-        ),
+        jax.ShapeDtypeStruct((sources // 2, slots, 2 * rank), BF16),
+        (received, weight),
+        2 * sources * slots * features * rank * QUAD,
         name="down",
-    )(received, weight)
+    )
 
 
 def up_kernel(lowered_ref, weight_ref, out_ref):

time: 149 us -> 147 us (0.987)
    pallas_call x1 -> x0, Pallas kernels: 3.99 us -> none  [lower(): pl.pallas_call(down_kernel, in_specs=[HBM, VMEM], out_specs=VMEM, out_sha...]
    pallas_call x11 -> x12, Pallas kernels: 11.5 us -> 14.2 us  [call(): pl.pallas_call(kernel, out_shape=out_shape, in_specs=[VMEM] * len(operand...]
where the time goes in v10:
time: 147 us; the launch traced here: 145 us
  starting transfers between devices  59.2 us (40%)
  blocking collectives  34 us (23%)
  waiting for transfers between devices  28.6 us (19%)
  Pallas kernels  19.2 us (13%)
  local copies, waits for them, and re-layouts  3.06 us (2%)
    all_to_all x3, starting transfers between devices, exchange(): lax.all_to_all(array, axis, split_axis=0, concat_axis=0, tiled=True, axis...  28.2 us
    ppermute x8, starting transfers between devices, shift(): lax.ppermute(array, 'tensor', [(i, (i + step) % groups) for i in range(gr...  26.1 us
    all_to_all x2, blocking collectives, exchange(): lax.all_to_all(array, axis, split_axis=0, concat_axis=0, tiled=True, axis...  25.1 us
    ppermute x8, waiting for transfers between devices, shift(): lax.ppermute(array, 'tensor', [(i, (i + step) % groups) for i in range(gr...  14.5 us
    pallas_call x12, Pallas kernels, call(): pl.pallas_call(kernel, out_shape=out_shape, in_specs=[VMEM] * len(operand...  14.2 us
    all_to_all x3, waiting for transfers between devices, exchange(): lax.all_to_all(array, axis, split_axis=0, concat_axis=0, tiled=True, axis...  11.8 us
    pallas_call x1, Pallas kernels, pack(): pl.pallas_call(pack_kernel, out_shape=[jax.ShapeDtypeStruct((1, rows), jn...  5.01 us
    all_gather x1, blocking collectives, sum_over_tensor(): lax.all_gather(mine, 'tensor', axis=0, axis_index_groups=pairs, tiled=True)  4.93 us
  transfers between devices with their start and end apart: 13, of which 12 were waited for; matrix products, arithmetic and copies ran while one was open for 1% of the time, Pallas kernels for 6%

profile of v10, /device:TPU:1, one launch (start us, length us, event | category | flops | bytes accessed | tf_op | source)
XLA Modules:
  0.0 145.5 jit_solution(1353774924186255068)
XLA Ops:
  0.6 5.0 %pack.1 = (s32[1,1024]{1,0:T(1,128)}, bf16[2048,512]{1,0:T(8,128)(2,1)}) custom-call(s32[1,1024]{1,0:T(1,128)} %bitcast.37, bf16[1024,512]{1,0:T(8,128)(2,1)} %tokens_ref.3), custom_call_target="tpu_custom_call" | custom-call | flops 2147483648 | bytes 3145728 | tf_op jit(solution)/shard_map/pack/pallas_call | solution.py:175
  5.6 0.0 copy-start
  5.7 0.0 copy-start.1
  5.7 14.1 %all-to-all-start = ((bf16[32,64,512]{2,1,0:T(8,128)(2,1)}), bf16[32,64,512]{2,1,0:T(8,128)(2,1)}, u32[]{:S(2)}, u32[]{:S(2)}) async-start(bf16[32,64,512]{2,1,0:T(8,128)(2,1)} %bitcast.35), calls=%async_computation | async-start | bytes 4194304 | tf_op jit(solution)/shard_map/all_to_all | solution.py:319
  19.8 1.0 base.4
  20.8 1.5 %base.5 = bf16[5,1024,128]{2,1,0:T(8,128)(2,1)S(1)} custom-call(bf16[1024,512]{1,0:T(8,128)(2,1)S(1)} %copy-done.1, bf16[512,2048]{1,0:T(8,128)(2,1)S(1)} %copy-done), custom_call_target="tpu_custom_call" | custom-call | flops 671088640 | bytes 4456448 | tf_op jit(solution)/shard_map/base/pallas_call | solution.py:24
  22.4 2.9 %collective-permute-start = (bf16[5,1024,128]{2,1,0:T(8,128)(2,1)S(1)}, bf16[5,1024,128]{2,1,0:T(8,128)(2,1)S(1)}, u32[]{:S(2)}, u32[]{:S(2)}) collective-permute-start(bf16[5,1024,128]{2,1,0:T(8,128)(2,1)S(1)} %base.5), channel_id=1, source_target_pairs={{0,1},{1,0},{2,3},{3,2},{4,5},{5,4},{6,7},{7,6},{8,9},{9,8},{10,11... | collective-permute-start | bytes 3932168 | tf_op jit(solution)/shard_map/ppermute | solution.py:85
  25.3 1.9 %collective-permute-start.1 = (bf16[3,1024,128]{2,1,0:T(8,128)(2,1)S(1)}, bf16[3,1024,128]{2,1,0:T(8,128)(2,1)S(1)}, u32[]{:S(2)}, u32[]{:S(2)}) collective-permute-start(bf16[3,1024,128]{2,1,0:T(8,128)(2,1)S(1)} %base.4), channel_id=1, source_target_pairs={{0,1},{1,0},{2,3},{3,2},{4,5},{5,4},{6,7},{7,6},{8,9},{9,8},{10,11... | collective-permute-start | bytes 2359304 | tf_op jit(solution)/shard_map/ppermute | solution.py:82
  27.2 2.3 %collective-permute-done.1.rest_0_ = bf16[3,1024,128]{2,1,0:T(8,128)(2,1)S(1)} collective-permute-done((bf16[3,1024,128]{2,1,0:T(8,128)(2,1)S(1)}, bf16[3,1024,128]{2,1,0:T(8,128)(2,1)S(1)}, u32[]{:S(2)}, u32[]{:S(2)}) %collective-permute-start.1) | collective-permute-done | bytes 786464 | tf_op jit(solution)/shard_map/ppermute | solution.py:82
  29.5 1.0 base.7
  30.5 3.2 %collective-permute-start.2 = (bf16[512,128]{1,0:T(8,128)(2,1)S(1)}, bf16[512,128]{1,0:T(8,128)(2,1)S(1)}, u32[]{:S(2)}, u32[]{:S(2)}) collective-permute-start(bf16[512,128]{1,0:T(8,128)(2,1)S(1)} %bitcast.34), channel_id=1, source_target_pairs={{0,2},{1,3},{2,4},{3,5},{4,6},{5,7},{6,8},{7,9},{8,10},{9,11},{10,... | collective-permute-start | bytes 393224 | tf_op jit(solution)/shard_map/ppermute | solution.py:73
  33.7 3.8 %collective-permute-start.3 = (bf16[512,128]{1,0:T(8,128)(2,1)S(1)}, bf16[512,128]{1,0:T(8,128)(2,1)S(1)}, u32[]{:S(2)}, u32[]{:S(2)}) collective-permute-start(bf16[512,128]{1,0:T(8,128)(2,1)S(1)} %bitcast.33), channel_id=1, source_target_pairs={{0,14},{1,15},{2,0},{3,1},{4,2},{5,3},{6,4},{7,5},{8,6},{9,7},{10,... | collective-permute-start | bytes 393224 | tf_op jit(solution)/shard_map/ppermute | solution.py:73
  37.5 1.9 %collective-permute-done.2.up_ref = bf16[512,128]{1,0:T(8,128)(2,1)S(1)} collective-permute-done((bf16[512,128]{1,0:T(8,128)(2,1)S(1)}, bf16[512,128]{1,0:T(8,128)(2,1)S(1)}, u32[]{:S(2)}, u32[]{:S(2)}) %collective-permute-start.2) | collective-permute-done | bytes 131104 | tf_op jit(solution)/shard_map/ppermute | solution.py:73
  39.4 0.9 collective-permute-done.3.down_ref
  40.3 0.1 ring.1
  40.4 3.2 %collective-permute-start.4 = (bf16[1024,128]{1,0:T(8,128)(2,1)S(1)}, bf16[1024,128]{1,0:T(8,128)(2,1)S(1)}, u32[]{:S(2)}, u32[]{:S(2)}) collective-permute-start(bf16[1024,128]{1,0:T(8,128)(2,1)S(1)} %get-tuple-element.36), channel_id=1, source_target_pairs={{0,2},{1,3},{2,4},{3,5},{4,6},{5,7},{6,8},{7,9},{8,10},{9,11},{10,... | collective-permute-start | bytes 786440 | tf_op jit(solution)/shard_map/ppermute | solution.py:73
  43.6 4.1 %collective-permute-start.6 = (bf16[1024,128]{1,0:T(8,128)(2,1)S(1)}, bf16[1024,128]{1,0:T(8,128)(2,1)S(1)}, u32[]{:S(2)}, u32[]{:S(2)}) collective-permute-start(bf16[1024,128]{1,0:T(8,128)(2,1)S(1)} %get-tuple-element.38), channel_id=1, source_target_pairs={{0,14},{1,15},{2,0},{3,1},{4,2},{5,3},{6,4},{7,5},{8,6},{9,7},{10,... | collective-permute-start | bytes 786440 | tf_op jit(solution)/shard_map/ppermute | solution.py:73
  47.7 0.0 collective-permute-done.rest_0_
  47.7 1.6 %base.6 = (bf16[1,1024,128]{2,1,0:T(8,128)(2,1)S(1)}, bf16[1,1024,128]{2,1,0:T(8,128)(2,1)S(1)}, bf16[1,1024,128]{2,1,0:T(8,128)(2,1)S(1)}, bf16[1,1024,128]{2,1,0:T(8,128)(2,1)S(1)}, bf16[1,1024,128]{2,1,0:T(8,128)(2,1)S(1)}) custom-call(bf16[1024,512]{1,0:T(8,128)(2,1)S(1)} %copy-done.1, bf16[512,2048]{1,0:T(8,128)(2,1)S(1)} %copy-done, ...), custom_call_target="tpu_custom_call" | custom-call | flops 671088640 | bytes 5767168 | tf_op jit(solution)/shard_map/base/pallas_call | solution.py:24
  49.3 0.7 copy-done.3
  50.0 0.7 copy-done.5
  50.7 1.0 collective-permute-done.4
  51.7 0.1 fusion.4
  51.7 1.9 %collective-permute-start.5 = (bf16[1024,128]{1,0:T(8,128)(2,1)S(1)}, bf16[1024,128]{1,0:T(8,128)(2,1)S(1)}, u32[]{:S(2)}, u32[]{:S(2)}) collective-permute-start(bf16[1024,128]{1,0:T(8,128)(2,1)S(1)} %fusion.4), channel_id=1, source_target_pairs={{0,2},{1,3},{2,4},{3,5},{4,6},{5,7},{6,8},{7,9},{8,10},{9,11},{10,... | collective-permute-start | bytes 786440 | tf_op jit(solution)/shard_map/ppermute | solution.py:73
  53.7 0.1 collective-permute-done.6
  53.8 0.1 fusion.3
  53.9 4.5 %collective-permute-start.7 = (bf16[1024,128]{1,0:T(8,128)(2,1)S(1)}, bf16[1024,128]{1,0:T(8,128)(2,1)S(1)}, u32[]{:S(2)}, u32[]{:S(2)}) collective-permute-start(bf16[1024,128]{1,0:T(8,128)(2,1)S(1)} %fusion.3), channel_id=1, source_target_pairs={{0,14},{1,15},{2,0},{3,1},{4,2},{5,3},{6,4},{7,5},{8,6},{9,7},{10,... | collective-permute-start | bytes 786440 | tf_op jit(solution)/shard_map/ppermute | solution.py:73
  58.4 3.1 %collective-permute-done.5 = bf16[1024,128]{1,0:T(8,128)(2,1)S(1)} collective-permute-done((bf16[1024,128]{1,0:T(8,128)(2,1)S(1)}, bf16[1024,128]{1,0:T(8,128)(2,1)S(1)}, u32[]{:S(2)}, u32[]{:S(2)}) %collective-permute-start.5) | collective-permute-done | bytes 262176 | tf_op jit(solution)/shard_map/ppermute | solution.py:73
  61.4 1.1 collective-permute-done.7
  62.5 1.2 copy-done.2
  63.7 0.1 keep.1.weight_ref
  63.8 4.9 %all-to-all-done.rows_ref = bf16[32,64,512]{2,1,0:T(8,128)(2,1)} async-done(((bf16[32,64,512]{2,1,0:T(8,128)(2,1)}), bf16[32,64,512]{2,1,0:T(8,128)(2,1)}, u32[]{:S(2)}, u32[]{:S(2)}) %all-to-all-start) | async-done | bytes 2097184 | tf_op jit(solution)/shard_map/all_to_all | solution.py:319
  68.7 2.6 %down.1 = bf16[16,64,128]{2,1,0:T(8,128)(2,1)S(1)} custom-call(bf16[32,64,512]{2,1,0:T(8,128)(2,1)} %all-to-all-done.rows_ref, bf16[16,64,512]{2,1,0:T(8,128)(2,1)S(1)} %keep.1.weight_ref), custom_call_target="tpu_custom_call" | custom-call | flops 536870912 | bytes 3407872 | tf_op jit(solution)/shard_map/down/pallas_call | solution.py:24
  71.3 0.0 copy-start.7
  71.3 4.0 %all-gather = bf16[32,64,128]{2,1,0:T(8,128)(2,1)S(1)} all-gather(bf16[16,64,128]{2,1,0:T(8,128)(2,1)S(1)} %down.1), channel_id=2, replica_groups={{0,1},{2,3},{4,5},{6,7},{8,9},{10,11},{12,13},{14,15},{16,17},{18,19},{..., dimensions={0}, use_global_device_ids=true | all-gather | bytes 786432 | tf_op jit(solution)/shard_map/all_gather | solution.py:325
  75.4 0.0 copy-start.6
  75.4 0.0 copy-start.4
  75.4 14.7 %all_to_all.25 = bf16[8,64,128]{2,1,0:T(8,128)(2,1)S(1)} all-to-all(bf16[8,64,128]{2,1,0:T(8,128)(2,1)S(1)} %fusion.6), channel_id=1, replica_groups={{0,2,4,6,8,10,12,14},{1,3,5,7,9,11,13,15},{16,18,20,22,24,26,28,30},{17..., dimensions={0} | all-to-all | bytes 262144 | tf_op jit(solution)/shard_map/all_to_all | solution.py:319
  90.1 10.4 %all_to_all.26 = bf16[8,64,128]{2,1,0:T(8,128)(2,1)S(1)} all-to-all(bf16[8,64,128]{2,1,0:T(8,128)(2,1)S(1)} %broadcast_in_dim.2), channel_id=1, replica_groups={{0,2,4,6,8,10,12,14},{1,3,5,7,9,11,13,15},{16,18,20,22,24,26,28,30},{17..., dimensions={0} | all-to-all | bytes 262144 | tf_op jit(solution)/shard_map/all_to_all | solution.py:319
  100.6 4.9 %all_gather.11.lowered_ref = bf16[16,64,128]{2,1,0:T(8,128)(2,1)S(1)} all-gather(bf16[8,64,128]{2,1,0:T(8,128)(2,1)S(1)} %all_to_all.26), channel_id=1, replica_groups={{0,1},{2,3},{4,5},{6,7},{8,9},{10,11},{12,13},{14,15},{16,17},{18,19},{..., dimensions={0}, use_global_device_ids=true | all-gather | bytes 393216 | tf_op jit(solution)/shard_map/all_gather | solution.py:334
  105.5 0.0 copy-done.7
  105.5 1.3 up.1
  106.8 6.0 %all-to-all-start.3 = ((bf16[32,64,128]{2,1,0:T(8,128)(2,1)}), bf16[32,64,128]{2,1,0:T(8,128)(2,1)S(1)}, u32[]{:S(2)}, u32[]{:S(2)}) async-start(bf16[32,64,128]{2,1,0:T(8,128)(2,1)} %bitcast.9), calls=%async_computation.3 | async-start | bytes 1048576 | tf_op jit(solution)/shard_map/all_to_all | solution.py:319
  112.8 0.0 copy-done.6
  112.8 0.1 fusion
  112.9 0.0 copy-start.10
  112.9 2.1 %collective-permute-start.9 = (bf16[1024,128]{1,0:T(8,128)(2,1)S(1)}, bf16[1024,128]{1,0:T(8,128)(2,1)S(1)}, u32[]{:S(2)}, u32[]{:S(2)}) collective-permute-start(bf16[1024,128]{1,0:T(8,128)(2,1)S(1)} %fusion), channel_id=1, source_target_pairs={{0,14},{1,15},{2,0},{3,1},{4,2},{5,3},{6,4},{7,5},{8,6},{9,7},{10,... | collective-permute-start | bytes 786440 | tf_op jit(solution)/shard_map/ppermute | solution.py:73
  115.0 0.1 fusion.1
  115.0 3.4 %collective-permute-start.8 = (bf16[1024,128]{1,0:T(8,128)(2,1)S(1)}, bf16[1024,128]{1,0:T(8,128)(2,1)S(1)}, u32[]{:S(2)}, u32[]{:S(2)}) collective-permute-start(bf16[1024,128]{1,0:T(8,128)(2,1)S(1)} %fusion.1), channel_id=1, source_target_pairs={{0,2},{1,3},{2,4},{3,5},{4,6},{5,7},{6,8},{7,9},{8,10},{9,11},{10,... | collective-permute-start | bytes 786440 | tf_op jit(solution)/shard_map/ppermute | solution.py:73
  118.4 0.1 copy.13
  118.5 0.1 reshape.47.accepted_ref
  118.6 3.3 %collective-permute-done.9 = bf16[1024,128]{1,0:T(8,128)(2,1)S(1)} collective-permute-done((bf16[1024,128]{1,0:T(8,128)(2,1)S(1)}, bf16[1024,128]{1,0:T(8,128)(2,1)S(1)}, u32[]{:S(2)}, u32[]{:S(2)}) %collective-permute-start.9) | collective-permute-done | bytes 262176 | tf_op jit(solution)/shard_map/ppermute | solution.py:73
  122.0 3.1 %collective-permute-done.8 = bf16[1024,128]{1,0:T(8,128)(2,1)S(1)} collective-permute-done((bf16[1024,128]{1,0:T(8,128)(2,1)S(1)}, bf16[1024,128]{1,0:T(8,128)(2,1)S(1)}, u32[]{:S(2)}, u32[]{:S(2)}) %collective-permute-start.8) | collective-permute-done | bytes 262176 | tf_op jit(solution)/shard_map/ppermute | solution.py:73
  125.0 0.1 fusion.2.base_ref
  125.2 0.0 copy-done.8
  125.2 0.9 prepare.1
  126.1 0.8 all-to-all-done.3
  126.9 0.9 choose.1
  127.8 8.1 %all-to-all-start.4 = ((bf16[32,4,128]{2,1,0:T(4,128)(2,1)}), bf16[32,4,128]{2,1,0:T(4,128)(2,1)S(1)}, u32[]{:S(2)}, u32[]{:S(2)}) async-start(bf16[32,4,128]{2,1,0:T(4,128)(2,1)} %bitcast.14), calls=%async_computation.4 | async-start | bytes 65536 | tf_op jit(solution)/shard_map/all_to_all | solution.py:319
  136.0 0.1 copy.14
  136.0 0.1 reshape.48.targets_ref
  136.2 2.4 %finish.1 = bf16[1024,128]{1,0:T(8,128)(2,1)} custom-call(s32[1,1024]{1,0:T(1,128)S(1)} %copy-done.8, bf16[2048,128]{1,0:T(8,128)(2,1)S(1)} %bitcast.30, f32[1024,128]{1,0:T(8,128)S(1)} %fusion.2.base_ref), custom_call_target="tpu_custom_call" | custom-call | flops 536870912 | bytes 1314816 | tf_op jit(solution)/shard_map/finish/pallas_call | solution.py:24
  138.6 6.1 %all-to-all-done.4 = bf16[32,4,128]{2,1,0:T(4,128)(2,1)S(1)} async-done(((bf16[32,4,128]{2,1,0:T(4,128)(2,1)}), bf16[32,4,128]{2,1,0:T(4,128)(2,1)S(1)}, u32[]{:S(2)}, u32[]{:S(2)}) %all-to-all-start.4) | async-done | bytes 32800 | tf_op jit(solution)/shard_map/all_to_all | solution.py:319
  144.7 0.8 cache.1
  (14 shorter events, 0.1 us)
Async XLA Ops:
  5.6 14.2 %copy-start = (bf16[512,2048]{1,0:T(8,128)(2,1)S(1)}, bf16[512,2048]{1,0:T(8,128)(2,1)}, u32[]{:S(2)}) copy-start(bf16[512,2048]{1,0:T(8,128)(2,1)} %weight_ref.8) | copy-start | bytes 6291460
  5.7 14.2 %copy-start.1 = (bf16[1024,512]{1,0:T(8,128)(2,1)S(1)}, bf16[1024,512]{1,0:T(8,128)(2,1)}, u32[]{:S(2)}) copy-start(bf16[1024,512]{1,0:T(8,128)(2,1)} %tokens_ref.3) | copy-start | bytes 3145732
  5.7 63.0 %all-to-all-start = ((bf16[32,64,512]{2,1,0:T(8,128)(2,1)}), bf16[32,64,512]{2,1,0:T(8,128)(2,1)}, u32[]{:S(2)}, u32[]{:S(2)}) async-start(bf16[32,64,512]{2,1,0:T(8,128)(2,1)} %bitcast.35), calls=%async_computation | async-start | bytes 4194304 | tf_op jit(solution)/shard_map/all_to_all | solution.py:319
  22.4 25.3 %collective-permute-start = (bf16[5,1024,128]{2,1,0:T(8,128)(2,1)S(1)}, bf16[5,1024,128]{2,1,0:T(8,128)(2,1)S(1)}, u32[]{:S(2)}, u32[]{:S(2)}) collective-permute-start(bf16[5,1024,128]{2,1,0:T(8,128)(2,1)S(1)} %base.5), channel_id=1, source_target_pairs={{0,1},{1,0},{2,3},{3,2},{4,5},{5,4},{6,7},{7,6},{8,9},{9,8},{10,11... | collective-permute-start | bytes 3932168 | tf_op jit(solution)/shard_map/ppermute | solution.py:85
  25.3 4.2 %collective-permute-start.1 = (bf16[3,1024,128]{2,1,0:T(8,128)(2,1)S(1)}, bf16[3,1024,128]{2,1,0:T(8,128)(2,1)S(1)}, u32[]{:S(2)}, u32[]{:S(2)}) collective-permute-start(bf16[3,1024,128]{2,1,0:T(8,128)(2,1)S(1)} %base.4), channel_id=1, source_target_pairs={{0,1},{1,0},{2,3},{3,2},{4,5},{5,4},{6,7},{7,6},{8,9},{9,8},{10,11... | collective-permute-start | bytes 2359304 | tf_op jit(solution)/shard_map/ppermute | solution.py:82
  30.5 9.0 %collective-permute-start.2 = (bf16[512,128]{1,0:T(8,128)(2,1)S(1)}, bf16[512,128]{1,0:T(8,128)(2,1)S(1)}, u32[]{:S(2)}, u32[]{:S(2)}) collective-permute-start(bf16[512,128]{1,0:T(8,128)(2,1)S(1)} %bitcast.34), channel_id=1, source_target_pairs={{0,2},{1,3},{2,4},{3,5},{4,6},{5,7},{6,8},{7,9},{8,10},{9,11},{10,... | collective-permute-start | bytes 393224 | tf_op jit(solution)/shard_map/ppermute | solution.py:73
  33.7 6.6 %collective-permute-start.3 = (bf16[512,128]{1,0:T(8,128)(2,1)S(1)}, bf16[512,128]{1,0:T(8,128)(2,1)S(1)}, u32[]{:S(2)}, u32[]{:S(2)}) collective-permute-start(bf16[512,128]{1,0:T(8,128)(2,1)S(1)} %bitcast.33), channel_id=1, source_target_pairs={{0,14},{1,15},{2,0},{3,1},{4,2},{5,3},{6,4},{7,5},{8,6},{9,7},{10,... | collective-permute-start | bytes 393224 | tf_op jit(solution)/shard_map/ppermute | solution.py:73
  40.4 11.3 %collective-permute-start.4 = (bf16[1024,128]{1,0:T(8,128)(2,1)S(1)}, bf16[1024,128]{1,0:T(8,128)(2,1)S(1)}, u32[]{:S(2)}, u32[]{:S(2)}) collective-permute-start(bf16[1024,128]{1,0:T(8,128)(2,1)S(1)} %get-tuple-element.36), channel_id=1, source_target_pairs={{0,2},{1,3},{2,4},{3,5},{4,6},{5,7},{6,8},{7,9},{8,10},{9,11},{10,... | collective-permute-start | bytes 786440 | tf_op jit(solution)/shard_map/ppermute | solution.py:73
  43.6 10.2 %collective-permute-start.6 = (bf16[1024,128]{1,0:T(8,128)(2,1)S(1)}, bf16[1024,128]{1,0:T(8,128)(2,1)S(1)}, u32[]{:S(2)}, u32[]{:S(2)}) collective-permute-start(bf16[1024,128]{1,0:T(8,128)(2,1)S(1)} %get-tuple-element.38), channel_id=1, source_target_pairs={{0,14},{1,15},{2,0},{3,1},{4,2},{5,3},{6,4},{7,5},{8,6},{9,7},{10,... | collective-permute-start | bytes 786440 | tf_op jit(solution)/shard_map/ppermute | solution.py:73
  49.2 0.7 copy-start.3
  49.9 0.7 copy-start.5
  51.7 9.7 %collective-permute-start.5 = (bf16[1024,128]{1,0:T(8,128)(2,1)S(1)}, bf16[1024,128]{1,0:T(8,128)(2,1)S(1)}, u32[]{:S(2)}, u32[]{:S(2)}) collective-permute-start(bf16[1024,128]{1,0:T(8,128)(2,1)S(1)} %fusion.4), channel_id=1, source_target_pairs={{0,2},{1,3},{2,4},{3,5},{4,6},{5,7},{6,8},{7,9},{8,10},{9,11},{10,... | collective-permute-start | bytes 786440 | tf_op jit(solution)/shard_map/ppermute | solution.py:73
  53.9 8.6 %collective-permute-start.7 = (bf16[1024,128]{1,0:T(8,128)(2,1)S(1)}, bf16[1024,128]{1,0:T(8,128)(2,1)S(1)}, u32[]{:S(2)}, u32[]{:S(2)}) collective-permute-start(bf16[1024,128]{1,0:T(8,128)(2,1)S(1)} %fusion.3), channel_id=1, source_target_pairs={{0,14},{1,15},{2,0},{3,1},{4,2},{5,3},{6,4},{7,5},{8,6},{9,7},{10,... | collective-permute-start | bytes 786440 | tf_op jit(solution)/shard_map/ppermute | solution.py:73
  62.5 1.2 copy-start.2
  71.3 34.2 %copy-start.7 = (bf16[16,64,128]{2,1,0:T(8,128)(2,1)S(1)}, bf16[16,64,128]{2,1,0:T(8,128)(2,1)}, u32[]{:S(2)}) copy-start(bf16[16,64,128]{2,1,0:T(8,128)(2,1)} %weight_ref.9) | copy-start | bytes 786436
  75.4 37.4 %copy-start.6 = (bf16[1,1024,128]{2,1,0:T(8,128)(2,1)S(1)}, bf16[1,1024,128]{2,1,0:T(8,128)(2,1)}, u32[]{:S(2)}) copy-start(bf16[1,1024,128]{2,1,0:T(8,128)(2,1)} %copy-done.5) | copy-start | bytes 786436
  75.4 39.5 %copy-start.4 = (bf16[1,1024,128]{2,1,0:T(8,128)(2,1)S(1)}, bf16[1,1024,128]{2,1,0:T(8,128)(2,1)}, u32[]{:S(2)}) copy-start(bf16[1,1024,128]{2,1,0:T(8,128)(2,1)} %copy-done.3) | copy-start | bytes 786436
  100.6 17.9 %copy-start.9 = (s32[1,32,4]{1,2,0:T(4,128)S(1)}, s32[1,32,4]{1,2,0:T(4,128)}, u32[]{:S(2)}) copy-start(s32[1,32,4]{1,2,0:T(4,128)} %param.12) | copy-start | bytes 1540
  106.8 18.4 %copy-start.8 = (s32[1,1024]{1,0:T(1,128)S(1)}, s32[1,1024]{1,0:T(1,128)}, u32[]{:S(2)}) copy-start(s32[1,1024]{1,0:T(1,128)} %get-tuple-element.27.slots_ref) | copy-start | bytes 12292
  106.8 20.1 %all-to-all-start.3 = ((bf16[32,64,128]{2,1,0:T(8,128)(2,1)}), bf16[32,64,128]{2,1,0:T(8,128)(2,1)S(1)}, u32[]{:S(2)}, u32[]{:S(2)}) async-start(bf16[32,64,128]{2,1,0:T(8,128)(2,1)} %bitcast.9), calls=%async_computation.3 | async-start | bytes 1048576 | tf_op jit(solution)/shard_map/all_to_all | solution.py:319
  112.9 23.1 %copy-start.10 = (s32[32,1,4]{0,2,1:T(4,128)S(1)}, s32[32,1,4]{0,2,1:T(4,128)}, u32[]{:S(2)}) copy-start(s32[32,1,4]{0,2,1:T(4,128)} %param.13) | copy-start | bytes 1540
  112.9 9.1 %collective-permute-start.9 = (bf16[1024,128]{1,0:T(8,128)(2,1)S(1)}, bf16[1024,128]{1,0:T(8,128)(2,1)S(1)}, u32[]{:S(2)}, u32[]{:S(2)}) collective-permute-start(bf16[1024,128]{1,0:T(8,128)(2,1)S(1)} %fusion), channel_id=1, source_target_pairs={{0,14},{1,15},{2,0},{3,1},{4,2},{5,3},{6,4},{7,5},{8,6},{9,7},{10,... | collective-permute-start | bytes 786440 | tf_op jit(solution)/shard_map/ppermute | solution.py:73
  115.0 10.0 %collective-permute-start.8 = (bf16[1024,128]{1,0:T(8,128)(2,1)S(1)}, bf16[1024,128]{1,0:T(8,128)(2,1)S(1)}, u32[]{:S(2)}, u32[]{:S(2)}) collective-permute-start(bf16[1024,128]{1,0:T(8,128)(2,1)S(1)} %fusion.1), channel_id=1, source_target_pairs={{0,2},{1,3},{2,4},{3,5},{4,6},{5,7},{6,8},{7,9},{8,10},{9,11},{10,... | collective-permute-start | bytes 786440 | tf_op jit(solution)/shard_map/ppermute | solution.py:73
  127.8 16.9 %all-to-all-start.4 = ((bf16[32,4,128]{2,1,0:T(4,128)(2,1)}), bf16[32,4,128]{2,1,0:T(4,128)(2,1)S(1)}, u32[]{:S(2)}, u32[]{:S(2)}) async-start(bf16[32,4,128]{2,1,0:T(4,128)(2,1)} %bitcast.14), calls=%async_computation.4 | async-start | bytes 65536 | tf_op jit(solution)/shard_map/all_to_all | solution.py:319
